TPU v7x, 256 devices: a whole 4x4x8 slice. The times are simulated.
256 devices in a mesh: rup: 16 (over x, z_hi), site: 16 (over z_lo, y, core).
Axes of the slice: x: 4, y: 4, z: 8 (z_hi: 4, z_lo: 2; z = z_hi * 2 + z_lo), core: 2. Of those that a mesh axis runs over, the one named last changes fastest.
Arguments:
- site_x: float32 [65536], P('site'), may hold values from 0 to 100
- site_y: float32 [65536], P('site'), may hold values from 0 to 100
- site_amp: float32 [65536], P('site'), may hold values from -1.2 to 1.2
- rup_x: float32 [2048], P('rup'), may hold values from 0 to 100
- rup_y: float32 [2048], P('rup'), may hold values from 0 to 100
- rup_mag: float32 [2048], P('rup'), may hold values from 5 to 8
- rup_rate: float32 [2048], P('rup'), may hold values from 0.0002 to 0.012
- rup_source: int32 [2048], P('rup'), may hold values from 0 to 63
- src_sigma: float32 [64], replicated, may hold values from 0.04 to 0.85
- src_shift: float32 [64], replicated, may hold values from -1.6 to 1.6
- relay_sites: int32 [16, 16, 16, 128], P('rup', 'site'), may hold values from 0 to 4095
- relay_count: int32 [16, 16, 16], P('rup', 'site'), may hold values from 1 to 128, 1536 in all within a row
- asset_source: int32 [524288], P(('rup', 'site')), may hold values from 0 to 15
- asset_pick: int32 [524288], P(('rup', 'site')), may hold values from 0 to 16383
- asset_class: int32 [524288], P(('rup', 'site')), may hold values from 0 to 127
- vulnerability: float32 [128, 32, 32], replicated, may hold values from 0 to 1
Outputs:
- hazard: float32 [32, 65536], P(None, 'site')
- losses: float32 [32, 524288], P(None, ('rup', 'site'))
Inputs may be any that keep to these rules, and one draw needn't show every extreme that they name: `relay_count`: for each index of rup and each owner, the counts of that owner over its source blocks add up to 3 * 128 * (devices of site) / 4 (the sum is per owner, not over a whole index of rup), and among them some count is exactly 128.
All inputs are finite; a program needn't handle non-finite values.
Results may differ from a plain program's by a relative error of at most 0.00019.
Values sent between devices are 32-bit elements; how exact they have to be, the bound alone decides.
No kernel may reach another device: no remote copies, remote signals or barrier semaphores. Data moves between devices by JAX's collectives and lax.ppermute only.
A program may use at most 128 MiB of HBM per device.

v0:
```python
import math

import jax
import jax.numpy as jnp
from jax import lax
from jax.sharding import PartitionSpec as P


def log_levels(count):
    position = jnp.arange(count, dtype=jnp.float32)
    return math.log(0.005) + position * (math.log(600.0) / (count - 1))


def table_lookup(indices, table):
    match = indices[:, None] == jnp.arange(table.shape[0], dtype=jnp.int32)[None, :]
    return jnp.sum(jnp.where(match, table[None, :], jnp.zeros_like(table)[None, :]), axis=1)


def exceed_rates(north_pos, east_pos, amplify, rup_x, rup_y, median_base, spread, rup_rate, levels):
    delta_x = north_pos[None, :] - rup_x[:, None]
    delta_y = east_pos[None, :] - rup_y[:, None]
    median = (
        median_base[:, None]
        + amplify[None, :]
        - 0.6 * jnp.log((delta_x * delta_x + delta_y * delta_y + 100.0) / 100.0)
    )
    scaled = (levels[:, None, None] - median[None, :, :]) / (spread[None, :, None] * math.sqrt(2.0))
    chance = 0.5 * lax.erfc(scaled)
    return jnp.sum(chance * rup_rate[None, :, None], axis=1)


def per_device(
    site_x,
    site_y,
    site_amp,
    rup_x,
    rup_y,
    rup_mag,
    rup_rate,
    rup_source,
    src_sigma,
    src_shift,
    relay_sites,
    relay_count,
    asset_source,
    asset_pick,
    asset_class,
    vulnerability,
):
    classes = vulnerability.shape[0]
    levels_count = vulnerability.shape[1]
    loss_bins = vulnerability.shape[2]
    site_count = site_x.shape[0]
    capacity = relay_sites.shape[3]
    wanted = relay_sites[0, 0]
    counts = relay_count[0, 0]
    levels = log_levels(levels_count)
    median_base = -1.0 + (rup_mag - 6.5) + table_lookup(rup_source, src_shift)
    spread = table_lookup(rup_source, src_sigma)
    site_block = 256
    blocks = site_count // site_block

    def one_block(pieces):
        return exceed_rates(
            pieces[0], pieces[1], pieces[2], rup_x, rup_y, median_base, spread, rup_rate, levels
        )

    partial_rates = lax.map(
        one_block,
        (
            site_x.reshape(blocks, site_block),
            site_y.reshape(blocks, site_block),
            site_amp.reshape(blocks, site_block),
        ),
    )
    partial_rates = jnp.moveaxis(partial_rates, 1, 0).reshape(levels_count, site_count)
    hazard = 1.0 - jnp.exp(-lax.psum(partial_rates, "rup"))
    source_count = table_lookup(asset_source, counts)
    slot_index = asset_source * capacity + asset_pick % source_count
    every_curve = lax.all_gather(hazard, "site", axis=1, tiled=True)
    global_site = asset_source * site_count + jnp.take(wanted.reshape(-1), slot_index)
    curves = jnp.take(every_curve, global_site, axis=1)
    asset_count = curves.shape[1]
    occurrence = curves - jnp.concatenate(
        [curves[1:], jnp.zeros((1, asset_count), jnp.float32)], axis=0
    )
    asset_block = 512
    nblocks = asset_count // asset_block
    class_table = vulnerability.reshape(classes, levels_count * loss_bins)

    def block_losses(pieces):
        occur_part, class_part = pieces
        onehot = (jnp.arange(classes, dtype=jnp.int32)[:, None] == class_part[None, :]).astype(
            jnp.float32
        )
        chosen = lax.dot_general(
            class_table, onehot, (((0,), (0,)), ((), ())), precision=lax.Precision.HIGHEST
        )
        chosen = chosen.reshape(levels_count, loss_bins, class_part.shape[0])
        return jnp.sum(occur_part[:, None, :] * chosen, axis=0)

    loss_parts = lax.map(
        block_losses,
        (
            jnp.moveaxis(occurrence.reshape(levels_count, nblocks, asset_block), 1, 0),
            asset_class.reshape(nblocks, asset_block),
        ),
    )
    losses = jnp.moveaxis(loss_parts, 0, 1).reshape(loss_bins, asset_count)
    return (hazard, losses)


def solution(mesh):
    return jax.shard_map(
        per_device,
        mesh=mesh,
        in_specs=(
            P("site"),
            P("site"),
            P("site"),
            P("rup"),
            P("rup"),
            P("rup"),
            P("rup"),
            P("rup"),
            P(),
            P(),
            P("rup", "site", None, None),
            P("rup", "site", None),
            P(("rup", "site")),
            P(("rup", "site")),
            P(("rup", "site")),
            P(),
        ),
        out_specs=(P(None, "site"), P(None, ("rup", "site"))),
        check_vma=False,
    )
```

profile of v0, /device:TPU:1, one launch (start us, length us, event | category | flops | bytes accessed | tf_op | source)
XLA Modules:
  0.0 593.9 jit_solution(5321849734481075054)
XLA Ops:
  10.8 178.2 %while.22 = (s32[]{:T(128)}, f32[16,32,256]{2,1,0:T(8,128)S(1)}, f32[128]{0:T(128)S(1)}, f32[16,256]{1,0:T(8,128)S(1)}, f32[16,256]{1,0:T(8,128)S(1)}, /*index=5...) while((s32[]{:T(128)}, f32[16,32,256]{2,1,0:T(8,128)S(1)}, ...), condition=%wide.region_4.5_spmd.clone, body=%wide.region_2.4_spmd.clone.sunk | while | flops 67428672 | bytes 374657 | solution.py:68
  11.5 0.8 multiply_subtract_fusion.2
  12.3 9.6 %fusion.17 = f32[32,256]{1,0:T(8,128)S(1)} fusion(f32[128]{0:T(128)S(1)} %get-tuple-element.260, f32[128]{0:T(128)S(1)} %get-tuple-element.261, f32[128,256]{1,0:T(8,128)S(1)} %multiply_subtract_fusion.2, f32[32]{0:T(128)S(1)} %multiply_add_fusion.2), kind=kLoop, calls=%fused_computation.13.clone.1 | loop fusion | flops 67100672 | bytes 164992 | tf_op jit(solution)/shard_map/while/body/eval_jaxpr/reduce_sum | solution.py:29
  22.7 0.8 multiply_subtract_fusion.2
  23.5 9.6 %fusion.17 = f32[32,256]{1,0:T(8,128)S(1)} fusion(f32[128]{0:T(128)S(1)} %get-tuple-element.260, f32[128]{0:T(128)S(1)} %get-tuple-element.261, f32[128,256]{1,0:T(8,128)S(1)} %multiply_subtract_fusion.2, f32[32]{0:T(128)S(1)} %multiply_add_fusion.2), kind=kLoop, calls=%fused_computation.13.clone.1 | loop fusion | flops 67100672 | bytes 164992 | tf_op jit(solution)/shard_map/while/body/eval_jaxpr/reduce_sum | solution.py:29
  33.8 0.8 multiply_subtract_fusion.2
  34.6 9.6 %fusion.17 = f32[32,256]{1,0:T(8,128)S(1)} fusion(f32[128]{0:T(128)S(1)} %get-tuple-element.260, f32[128]{0:T(128)S(1)} %get-tuple-element.261, f32[128,256]{1,0:T(8,128)S(1)} %multiply_subtract_fusion.2, f32[32]{0:T(128)S(1)} %multiply_add_fusion.2), kind=kLoop, calls=%fused_computation.13.clone.1 | loop fusion | flops 67100672 | bytes 164992 | tf_op jit(solution)/shard_map/while/body/eval_jaxpr/reduce_sum | solution.py:29
  44.9 0.8 multiply_subtract_fusion.2
  45.8 9.6 %fusion.17 = f32[32,256]{1,0:T(8,128)S(1)} fusion(f32[128]{0:T(128)S(1)} %get-tuple-element.260, f32[128]{0:T(128)S(1)} %get-tuple-element.261, f32[128,256]{1,0:T(8,128)S(1)} %multiply_subtract_fusion.2, f32[32]{0:T(128)S(1)} %multiply_add_fusion.2), kind=kLoop, calls=%fused_computation.13.clone.1 | loop fusion | flops 67100672 | bytes 164992 | tf_op jit(solution)/shard_map/while/body/eval_jaxpr/reduce_sum | solution.py:29
  56.1 0.8 multiply_subtract_fusion.2
  56.9 9.6 %fusion.17 = f32[32,256]{1,0:T(8,128)S(1)} fusion(f32[128]{0:T(128)S(1)} %get-tuple-element.260, f32[128]{0:T(128)S(1)} %get-tuple-element.261, f32[128,256]{1,0:T(8,128)S(1)} %multiply_subtract_fusion.2, f32[32]{0:T(128)S(1)} %multiply_add_fusion.2), kind=kLoop, calls=%fused_computation.13.clone.1 | loop fusion | flops 67100672 | bytes 164992 | tf_op jit(solution)/shard_map/while/body/eval_jaxpr/reduce_sum | solution.py:29
  67.2 0.8 multiply_subtract_fusion.2
  68.0 9.6 %fusion.17 = f32[32,256]{1,0:T(8,128)S(1)} fusion(f32[128]{0:T(128)S(1)} %get-tuple-element.260, f32[128]{0:T(128)S(1)} %get-tuple-element.261, f32[128,256]{1,0:T(8,128)S(1)} %multiply_subtract_fusion.2, f32[32]{0:T(128)S(1)} %multiply_add_fusion.2), kind=kLoop, calls=%fused_computation.13.clone.1 | loop fusion | flops 67100672 | bytes 164992 | tf_op jit(solution)/shard_map/while/body/eval_jaxpr/reduce_sum | solution.py:29
  78.4 0.8 multiply_subtract_fusion.2
  79.2 9.6 %fusion.17 = f32[32,256]{1,0:T(8,128)S(1)} fusion(f32[128]{0:T(128)S(1)} %get-tuple-element.260, f32[128]{0:T(128)S(1)} %get-tuple-element.261, f32[128,256]{1,0:T(8,128)S(1)} %multiply_subtract_fusion.2, f32[32]{0:T(128)S(1)} %multiply_add_fusion.2), kind=kLoop, calls=%fused_computation.13.clone.1 | loop fusion | flops 67100672 | bytes 164992 | tf_op jit(solution)/shard_map/while/body/eval_jaxpr/reduce_sum | solution.py:29
  89.5 0.8 multiply_subtract_fusion.2
  90.3 9.6 %fusion.17 = f32[32,256]{1,0:T(8,128)S(1)} fusion(f32[128]{0:T(128)S(1)} %get-tuple-element.260, f32[128]{0:T(128)S(1)} %get-tuple-element.261, f32[128,256]{1,0:T(8,128)S(1)} %multiply_subtract_fusion.2, f32[32]{0:T(128)S(1)} %multiply_add_fusion.2), kind=kLoop, calls=%fused_computation.13.clone.1 | loop fusion | flops 67100672 | bytes 164992 | tf_op jit(solution)/shard_map/while/body/eval_jaxpr/reduce_sum | solution.py:29
  100.7 0.8 multiply_subtract_fusion.2
  101.5 9.6 %fusion.17 = f32[32,256]{1,0:T(8,128)S(1)} fusion(f32[128]{0:T(128)S(1)} %get-tuple-element.260, f32[128]{0:T(128)S(1)} %get-tuple-element.261, f32[128,256]{1,0:T(8,128)S(1)} %multiply_subtract_fusion.2, f32[32]{0:T(128)S(1)} %multiply_add_fusion.2), kind=kLoop, calls=%fused_computation.13.clone.1 | loop fusion | flops 67100672 | bytes 164992 | tf_op jit(solution)/shard_map/while/body/eval_jaxpr/reduce_sum | solution.py:29
  111.8 0.8 multiply_subtract_fusion.2
  112.6 9.6 %fusion.17 = f32[32,256]{1,0:T(8,128)S(1)} fusion(f32[128]{0:T(128)S(1)} %get-tuple-element.260, f32[128]{0:T(128)S(1)} %get-tuple-element.261, f32[128,256]{1,0:T(8,128)S(1)} %multiply_subtract_fusion.2, f32[32]{0:T(128)S(1)} %multiply_add_fusion.2), kind=kLoop, calls=%fused_computation.13.clone.1 | loop fusion | flops 67100672 | bytes 164992 | tf_op jit(solution)/shard_map/while/body/eval_jaxpr/reduce_sum | solution.py:29
  123.8 9.6 %fusion.17 = f32[32,256]{1,0:T(8,128)S(1)} fusion(f32[128]{0:T(128)S(1)} %get-tuple-element.260, f32[128]{0:T(128)S(1)} %get-tuple-element.261, f32[128,256]{1,0:T(8,128)S(1)} %multiply_subtract_fusion.2, f32[32]{0:T(128)S(1)} %multiply_add_fusion.2), kind=kLoop, calls=%fused_computation.13.clone.1 | loop fusion | flops 67100672 | bytes 164992 | tf_op jit(solution)/shard_map/while/body/eval_jaxpr/reduce_sum | solution.py:29
  134.1 0.8 multiply_subtract_fusion.2
  134.9 9.6 %fusion.17 = f32[32,256]{1,0:T(8,128)S(1)} fusion(f32[128]{0:T(128)S(1)} %get-tuple-element.260, f32[128]{0:T(128)S(1)} %get-tuple-element.261, f32[128,256]{1,0:T(8,128)S(1)} %multiply_subtract_fusion.2, f32[32]{0:T(128)S(1)} %multiply_add_fusion.2), kind=kLoop, calls=%fused_computation.13.clone.1 | loop fusion | flops 67100672 | bytes 164992 | tf_op jit(solution)/shard_map/while/body/eval_jaxpr/reduce_sum | solution.py:29
  145.2 0.8 multiply_subtract_fusion.2
  146.0 9.6 %fusion.17 = f32[32,256]{1,0:T(8,128)S(1)} fusion(f32[128]{0:T(128)S(1)} %get-tuple-element.260, f32[128]{0:T(128)S(1)} %get-tuple-element.261, f32[128,256]{1,0:T(8,128)S(1)} %multiply_subtract_fusion.2, f32[32]{0:T(128)S(1)} %multiply_add_fusion.2), kind=kLoop, calls=%fused_computation.13.clone.1 | loop fusion | flops 67100672 | bytes 164992 | tf_op jit(solution)/shard_map/while/body/eval_jaxpr/reduce_sum | solution.py:29
  156.4 0.8 multiply_subtract_fusion.2
  157.2 9.6 %fusion.17 = f32[32,256]{1,0:T(8,128)S(1)} fusion(f32[128]{0:T(128)S(1)} %get-tuple-element.260, f32[128]{0:T(128)S(1)} %get-tuple-element.261, f32[128,256]{1,0:T(8,128)S(1)} %multiply_subtract_fusion.2, f32[32]{0:T(128)S(1)} %multiply_add_fusion.2), kind=kLoop, calls=%fused_computation.13.clone.1 | loop fusion | flops 67100672 | bytes 164992 | tf_op jit(solution)/shard_map/while/body/eval_jaxpr/reduce_sum | solution.py:29
  167.5 0.8 multiply_subtract_fusion.2
  168.3 9.6 %fusion.17 = f32[32,256]{1,0:T(8,128)S(1)} fusion(f32[128]{0:T(128)S(1)} %get-tuple-element.260, f32[128]{0:T(128)S(1)} %get-tuple-element.261, f32[128,256]{1,0:T(8,128)S(1)} %multiply_subtract_fusion.2, f32[32]{0:T(128)S(1)} %multiply_add_fusion.2), kind=kLoop, calls=%fused_computation.13.clone.1 | loop fusion | flops 67100672 | bytes 164992 | tf_op jit(solution)/shard_map/while/body/eval_jaxpr/reduce_sum | solution.py:29
  178.6 0.8 multiply_subtract_fusion.2
  179.5 9.6 %fusion.17 = f32[32,256]{1,0:T(8,128)S(1)} fusion(f32[128]{0:T(128)S(1)} %get-tuple-element.260, f32[128]{0:T(128)S(1)} %get-tuple-element.261, f32[128,256]{1,0:T(8,128)S(1)} %multiply_subtract_fusion.2, f32[32]{0:T(128)S(1)} %multiply_add_fusion.2), kind=kLoop, calls=%fused_computation.13.clone.1 | loop fusion | flops 67100672 | bytes 164992 | tf_op jit(solution)/shard_map/while/body/eval_jaxpr/reduce_sum | solution.py:29
  189.1 1.9 copy.29
  191.1 174.2 %all-reduce.3.cloned.1.call-done = f32[32,4096]{0,1:T(8,128)} async-done(((f32[32,4096]{0,1:T(8,128)}), f32[32,4096]{0,1:T(8,128)}) %all-reduce.3.cloned.1.call-update) | async-done | bytes 524304 | tf_op jit(solution)/shard_map/psum | solution.py:77
  365.3 3.2 exponential_subtract_fusion
  369.0 11.8 %gather_fusion = s32[2048]{0:T(1024)S(1)} fusion(s32[2048]{0:T(1024)S(1)} %bitcast.48, s32[2048]{0:T(1024)S(1)} %broadcast_clamp_fusion.1), kind=kCustom, calls=%fused_computation | custom fusion | bytes 24576 | tf_op jit(solution)/shard_map/jit(_take)/gather | solution.py:81
  381.0 1.4 copy.33
  382.4 167.7 %all-gather.2.cloned.1.call-done = f32[32,65536]{0,1:T(8,128)} async-done(((f32[32,4096]{0,1:T(8,128)}), f32[32,65536]{0,1:T(8,128)}) %all-gather.2.cloned.1.call-update) | async-done | bytes 8388624 | tf_op jit(solution)/shard_map/all_gather | solution.py:80
  550.1 16.0 %gather_fusion.1 = f32[2048,32]{1,0:T(8,128)S(1)} fusion(f32[32,65536]{0,1:T(8,128)} %all-gather.2.cloned.1.call-done, s32[2048]{0:T(1024)S(1)} %broadcast_clamp_fusion), kind=kCustom, calls=%fused_computation.1 | custom fusion | bytes 532480 | tf_op jit(solution)/shard_map/jit(_take)/gather | solution.py:82
  567.4 18.9 %while.21 = (s32[]{:T(128)}, f32[4,32,512]{2,1,0:T(8,128)S(1)}, f32[4,32,512]{2,1,0:T(8,128)S(1)}, s32[4,512]{1,0:T(4,128)S(1)}, f32[128,1024]{1,0:T(8,128)S(1)}, /*index=5*/s32[]{:T(128)}) while((s32[]{:T(128)}, f32[4,32,512]{2,1,0:T(8,128)S(1)}, f32[4,32,512]{2,1,0:T(8,128)S(1)}, s32[4,512]{1,0:T(4,128)S(1)}, f32[128,1024]{1,0:T(8,128)S(1)}, ...), condition=%wide.region_9.10_spmd, body=%wide.region_7.9_spmd.sunk | while | flops 806404096 | bytes 9312345 | solution.py:102
  567.5 2.4 convolution_bitcast_fusion.2
  569.8 1.9 copy.36
  572.2 2.4 convolution_bitcast_fusion.2
  574.6 1.9 copy.36
  576.9 2.4 convolution_bitcast_fusion.2
  579.3 1.9 copy.36
  581.6 2.4 convolution_bitcast_fusion.2
  584.0 1.9 copy.36
  (133 shorter events, 19.8 us)
Async XLA Ops:
  7.2 361.9 %copy-start = (s32[1,1,16,128]{3,2,1,0:T(8,128)S(1)}, s32[1,1,16,128]{3,2,1,0:T(8,128)}, u32[]{:S(2)}) copy-start(s32[1,1,16,128]{3,2,1,0:T(8,128)} %param.30) | copy-start | bytes 24580
  7.2 358.1 %all-reduce.3.cloned.1.call-start = ((), (), s32[]{:S(2)}) async-start(), calls=%async_computation | async-start | bytes 4194304 | tf_op jit(solution)/shard_map/psum | solution.py:77
  191.0 177.5 %copy-start.5 = (s32[2048]{0:T(1024)S(1)}, s32[2048]{0:T(1024)}, u32[]{:S(2)}) copy-start(s32[2048]{0:T(1024)} %param.34) | copy-start | bytes 24580
  191.0 177.5 %copy-start.2 = (f32[128,32,32]{0,2,1:T(8,128)S(1)}, f32[128,32,32]{0,2,1:T(8,128)}, u32[]{:S(2)}) copy-start(f32[128,32,32]{0,2,1:T(8,128)} %param.35) | copy-start | bytes 1572868
  191.0 177.7 %copy-start.3 = (s32[2048]{0:T(1024)S(1)}, s32[2048]{0:T(1024)}, u32[]{:S(2)}) copy-start(s32[2048]{0:T(1024)} %param.32) | copy-start | bytes 24580
  191.0 177.7 %copy-start.6 = (s32[1,1,16]{2,1,0:T(1,128)S(1)}, s32[1,1,16]{2,1,0:T(1,128)}, u32[]{:S(2)}) copy-start(s32[1,1,16]{2,1,0:T(1,128)} %param.31) | copy-start | bytes 196
  191.1 177.8 %copy-start.4 = (s32[2048]{0:T(1024)S(1)}, s32[2048]{0:T(1024)}, u32[]{:S(2)}) copy-start(s32[2048]{0:T(1024)} %param.33) | copy-start | bytes 24580
  191.1 359.0 %all-gather.2.cloned.1.call-start = ((), (), s32[]{:S(2)}) async-start(), calls=%async_computation.1 | async-start | bytes 35651584 | tf_op jit(solution)/shard_map/all_gather | solution.py:80
  369.0 12.0 %copy-start.1 = (f32[32,4096]{0,1:T(8,128)S(1)}, f32[32,4096]{0,1:T(8,128)}, u32[]{:S(2)}) copy-start(f32[32,4096]{0,1:T(8,128)} %exponential_subtract_fusion) | copy-start | bytes 1572868
Sparse Core Ops, SparseCore 0:
  191.2 174.0 all-reduce.2
  368.6 181.3 all-gather.1
where the time goes:
time: 595 us; the launch traced here: 594 us
  waiting for transfers between devices  342 us (57%)
  other arithmetic  184 us (31%)
  local copies, waits for them, and re-layouts  43 us (7%)
  between operations  14.2 us (2%)
  matrix products  9.49 us (2%)
    psum x1, waiting for transfers between devices, per_device(): hazard = 1.0 - jnp.exp(-lax.psum(partial_rates, 'rup'))  174 us
    all_gather x1, waiting for transfers between devices, per_device(): every_curve = lax.all_gather(hazard, 'site', axis=1, tiled=True)  168 us
    reduce_sum x16, other arithmetic, exceed_rates(): return jnp.sum(chance * rup_rate[None, :, None], axis=1)  154 us
    gather x1, local copies, waits for them, and re-layouts, per_device(): curves = jnp.take(every_curve, global_site, axis=1)  16 us
    sub x16, other arithmetic, exceed_rates(): median_base[:, None] + amplify[None, :]  12.7 us
  transfers between devices with their start and end apart: 2, of which 2 were waited for; matrix products, arithmetic and copies ran while one was open for 2% of the time, Pallas kernels for 0%

commit v1 on v0

v1 whole, which is shorter than its diff:
```python
import functools
import math

import jax
import jax.numpy as jnp
from jax import lax
from jax.experimental import pallas as pl
from jax.experimental.pallas import tpu as pltpu
from jax.sharding import PartitionSpec as P

LANES = 128
SUBLANES = 8
VMEM = pl.BlockSpec(memory_space=pltpu.VMEM)
SMEM = pl.BlockSpec(memory_space=pltpu.SMEM)
LEVEL_FIRST = math.log(0.005)
LEVEL_RANGE = math.log(600.0)


def lane_gather(row, index):
    return jnp.take_along_axis(row, index, axis=1, mode="promise_in_bounds")


def pack_kernel(x_ref, y_ref, mag_ref, rate_ref, source_ref, sigma_ref, shift_ref, out_ref):
    sources = sigma_ref.shape[1]
    index = jnp.broadcast_to(source_ref[...], (SUBLANES, LANES))
    pad = jnp.zeros((1, LANES - sources), jnp.float32)
    sigma = jnp.broadcast_to(jnp.concatenate([sigma_ref[...], pad], axis=1), (SUBLANES, LANES))
    shift = jnp.broadcast_to(jnp.concatenate([shift_ref[...], pad], axis=1), (SUBLANES, LANES))
    spread = lane_gather(sigma, index)[0:1]
    base = -1.0 + (mag_ref[...] - 6.5) + lane_gather(shift, index)[0:1]
    inverse = 1.0 / (spread * math.sqrt(2.0))
    zero = jnp.zeros((1, LANES), jnp.float32)
    packed = jnp.concatenate(
        [x_ref[...], y_ref[...], base, inverse, 0.5 * rate_ref[...], zero, zero, zero], axis=0
    )
    for peer in range(out_ref.shape[0]):
        out_ref[peer] = packed


def hazard_kernel(levels, row_ref, sx_ref, sy_ref, amp_ref, rup_ref, out_ref, col_ref, start_ref):
    blocks = rup_ref.shape[0]
    ruptures = blocks * LANES
    tiles = out_ref.shape[1] // LANES
    row = row_ref[0] * tiles
    step = LEVEL_RANGE / (levels - 1)
    for b in range(blocks):
        packed = rup_ref[b]
        square = jnp.concatenate(
            [packed, jnp.zeros((LANES - SUBLANES, LANES), jnp.float32)], axis=0
        )
        columns = jnp.transpose(square)
        for p in range(5):
            col_ref[p, b * LANES : (b + 1) * LANES, :] = jnp.broadcast_to(
                columns[:, p : p + 1], (LANES, LANES)
            )
    unroll = 8
    rows = unroll * SUBLANES
    for t in range(tiles):
        site_x = sx_ref[pl.ds(row + t, 1), :]
        site_y = sy_ref[pl.ds(row + t, 1), :]
        amp = amp_ref[pl.ds(row + t, 1), :]

        def prepare(g, carry):
            at = pl.ds(pl.multiple_of(g * rows, rows), rows)
            dx = site_x - col_ref[0, at, :]
            dy = site_y - col_ref[1, at, :]
            median = col_ref[2, at, :] + amp - 0.6 * jnp.log((dx * dx + dy * dy + 100.0) / 100.0)
            start_ref[t, at, :] = (LEVEL_FIRST - median) * col_ref[3, at, :]
            return carry

        lax.fori_loop(0, ruptures // rows, prepare, 0)

    half = levels // 2
    for t in range(tiles):
        for first in range(0, levels, half):

            def body(g, acc):
                acc = list(acc)
                for u in range(unroll):
                    at = pl.ds(pl.multiple_of(g * rows + u * SUBLANES, SUBLANES), SUBLANES)
                    gap = col_ref[3, at, :] * step
                    rate = col_ref[4, at, :]
                    z = start_ref[t, at, :]
                    if first:
                        z = z + gap * float(first)
                    for l in range(half):
                        acc[l] = acc[l] + rate * (1.0 - lax.erf(z))
                        z = z + gap
                return tuple(acc)

            zero = jnp.zeros((SUBLANES, LANES), jnp.float32)
            acc = lax.fori_loop(0, ruptures // rows, body, (zero,) * half)
            for l in range(half):
                rates = jnp.sum(acc[l], axis=0, keepdims=True)
                out_ref[pl.ds(first + l, 1), t * LANES : (t + 1) * LANES] = 1.0 - jnp.exp(-rates)


def relay_kernel(blocks_ref, index_ref, hazard_ref, send_ref):
    blocks, levels, width = blocks_ref.shape
    owners = index_ref.shape[0]
    groups = levels // SUBLANES
    tiles = width // LANES
    for b in range(blocks):
        hazard_ref[:, b * width : (b + 1) * width] = blocks_ref[b]

    def one_owner(d, carry):
        index = jnp.broadcast_to(index_ref[pl.ds(d, 1), :], (SUBLANES, LANES))
        lane = index & (LANES - 1)
        tile = index >> 7
        picked = [jnp.zeros((SUBLANES, LANES), jnp.float32)] * groups
        for c in range(blocks * tiles):
            b, t = c // tiles, c % tiles
            here = tile == c
            for q in range(groups):
                part = blocks_ref[b, q * SUBLANES : (q + 1) * SUBLANES, t * LANES : (t + 1) * LANES]
                picked[q] = jnp.where(here, lane_gather(part, lane), picked[q])
        for q in range(groups):
            send_ref[d, q * SUBLANES : (q + 1) * SUBLANES, :] = picked[q]
        return carry

    lax.fori_loop(0, owners, one_owner, 0)


def loss_kernel(
    curves_ref, source_ref, pick_ref, class_ref, count_ref, table_ref, out_ref, split_ref
):
    sources, levels, _ = curves_ref.shape
    bins = out_ref.shape[0]
    classes = table_ref.shape[1]
    groups = levels // SUBLANES
    assets = out_ref.shape[1]
    source = source_ref[...]
    count = jnp.zeros(source.shape, jnp.int32)
    for s in range(sources):
        count = jnp.where(source == s, count_ref[0, s], count)
    pick = pick_ref[...]
    count_f = count.astype(jnp.float32)
    quotient = jnp.floor(pick.astype(jnp.float32) / count_f).astype(jnp.int32)
    slot = pick - quotient * count
    slot = jnp.where(slot < 0, slot + count, slot)
    slot = jnp.where(slot >= count, slot - count, slot)
    table = table_ref[...]
    high = table.astype(jnp.bfloat16)
    low = (table - high.astype(jnp.float32)).astype(jnp.bfloat16)
    split_ref[:, 0:classes] = high
    split_ref[:, classes : 2 * classes] = low
    width = 2 * LANES
    for t in range(assets // width):
        curve = []
        for h in range(width // LANES):
            i = t * (width // LANES) + h
            lane = jnp.broadcast_to(slot[i : i + 1, :], (SUBLANES, LANES))
            which = jnp.broadcast_to(source[i : i + 1, :], (SUBLANES, LANES))
            picked = [jnp.zeros((SUBLANES, LANES), jnp.float32)] * groups
            for s in range(sources):
                here = which == s
                for q in range(groups):
                    part = curves_ref[s, q * SUBLANES : (q + 1) * SUBLANES, :]
                    picked[q] = jnp.where(here, lane_gather(part, lane), picked[q])
            curve.append(jnp.concatenate(picked, axis=0))
        curves = jnp.concatenate(curve, axis=1)
        following = jnp.concatenate([curves[1:], jnp.zeros((1, width), jnp.float32)], axis=0)
        occurrence = curves - following
        kinds = jnp.concatenate(
            [class_ref[t * (width // LANES) + h : t * (width // LANES) + h + 1, :] for h in range(width // LANES)],
            axis=1,
        )
        match = lax.broadcasted_iota(jnp.int32, (classes, width), 0) == kinds
        onehot = jnp.where(match, 1.0, 0.0).astype(jnp.bfloat16)
        both = jnp.concatenate([onehot, onehot], axis=0)
        chosen = jnp.dot(split_ref[...], both, preferred_element_type=jnp.float32)
        total = jnp.zeros((bins, width), jnp.float32)
        for l in range(levels):
            total = total + occurrence[l : l + 1, :] * chosen[l * bins : (l + 1) * bins, :]
        out_ref[:, t * width : (t + 1) * width] = total


def per_device(
    site_x,
    site_y,
    site_amp,
    rup_x,
    rup_y,
    rup_mag,
    rup_rate,
    rup_source,
    src_sigma,
    src_shift,
    relay_sites,
    relay_count,
    asset_source,
    asset_pick,
    asset_class,
    vulnerability,
    rows,
):
    classes, levels, bins = vulnerability.shape
    sites = site_x.shape[0]
    sources, capacity = relay_sites.shape[2:]
    assets = asset_source.shape[0]
    own_sites = sites // rows
    limit = pltpu.CompilerParams(vmem_limit_bytes=48 * 2**20)

    wanted = lax.all_to_all(relay_sites[0, 0], "site", 0, 0, tiled=True)
    line = lambda a: a.reshape(1, -1)
    packed = pl.pallas_call(
        pack_kernel,
        out_shape=jax.ShapeDtypeStruct((rows, SUBLANES, LANES), jnp.float32),
        in_specs=[VMEM] * 7,
        out_specs=VMEM,
    )(
        line(rup_x),
        line(rup_y),
        line(rup_mag),
        line(rup_rate),
        line(rup_source),
        line(src_sigma),
        line(src_shift),
    )
    ruptures = lax.all_to_all(packed, "rup", 0, 0, tiled=True)
    row = lax.axis_index("rup").astype(jnp.int32).reshape(1)
    square = lambda a: a.reshape(-1, LANES)
    own = pl.pallas_call(
        functools.partial(hazard_kernel, levels),
        out_shape=jax.ShapeDtypeStruct((levels, own_sites), jnp.float32),
        in_specs=[SMEM] + [VMEM] * 4,
        out_specs=VMEM,
        scratch_shapes=[
            pltpu.VMEM((5, rows * LANES, LANES), jnp.float32),
            pltpu.VMEM((own_sites // LANES, rows * LANES, LANES), jnp.float32),
        ],
        compiler_params=limit,
    )(row, square(site_x), square(site_y), square(site_amp), ruptures)
    spread = jnp.broadcast_to(own[None], (rows, levels, own_sites))
    blocks = lax.all_to_all(spread, "rup", 0, 0, tiled=True)
    hazard, send = pl.pallas_call(
        relay_kernel,
        out_shape=(
            jax.ShapeDtypeStruct((levels, sites), jnp.float32),
            jax.ShapeDtypeStruct((sources, levels, capacity), jnp.float32),
        ),
        in_specs=[VMEM] * 2,
        out_specs=(VMEM, VMEM),
        compiler_params=limit,
    )(blocks, wanted)
    curves = lax.all_to_all(send, "site", 0, 0, tiled=True)
    table = jnp.transpose(vulnerability, (1, 2, 0)).reshape(levels * bins, classes)
    losses = pl.pallas_call(
        loss_kernel,
        out_shape=jax.ShapeDtypeStruct((bins, assets), jnp.float32),
        in_specs=[VMEM] * 4 + [SMEM, VMEM],
        out_specs=VMEM,
        scratch_shapes=[pltpu.VMEM((levels * bins, 2 * classes), jnp.bfloat16)],
        compiler_params=limit,
    )(
        curves,
        square(asset_source),
        square(asset_pick),
        square(asset_class),
        relay_count.reshape(1, sources),
        table,
    )
    return hazard, losses


def solution(mesh):
    return jax.shard_map(
        functools.partial(per_device, rows=mesh.shape["rup"]),
        mesh=mesh,
        in_specs=(
            P("site"),
            P("site"),
            P("site"),
            P("rup"),
            P("rup"),
            P("rup"),
            P("rup"),
            P("rup"),
            P(),
            P(),
            P("rup", "site", None, None),
            P("rup", "site", None),
            P(("rup", "site")),
            P(("rup", "site")),
            P(("rup", "site")),
            P(),
        ),
        out_specs=(P(None, "site"), P(None, ("rup", "site"))),
        check_vma=False,
    )
```

time: 595 us -> 88.4 us (0.15)
  waiting for transfers between devices: 342 us -> 0.01 us
  other arithmetic: 184 us -> 0 us
  blocking collectives: 0 us -> 55.4 us
  local copies, waits for them, and re-layouts: 43 us -> 0.75 us
  Pallas kernels: 0 us -> 23.9 us
  between operations: 14.2 us -> 0.69 us
  matrix products: 9.49 us -> 0 us
  starting transfers between devices: 0.08 us -> 7.22 us
    psum x1 -> x0, waiting for transfers between devices: 174 us -> none  [per_device(): hazard = 1.0 - jnp.exp(-lax.psum(partial_rates, 'rup'))]
    all_gather x1 -> x0, waiting for transfers between devices: 168 us -> none  [per_device(): every_curve = lax.all_gather(hazard, 'site', axis=1, tiled=True)]
    reduce_sum x22 -> x0, other arithmetic: 156 us -> none  [the longest x16 154 us: exceed_rates(): return jnp.sum(chance * rup_rate[None, :, None], axis=1)]
    all_to_all x0 -> x3, blocking collectives: none -> 55.4 us  [the longest x1 20.7 us: per_device(): ruptures = lax.all_to_all(packed, 'rup', 0, 0, tiled=True)]
    gather x2 -> x0, local copies, waits for them, and re-layouts: 27.8 us -> none  [the longest x1 16 us: per_device(): curves = jnp.take(every_curve, global_site, axis=1)]
    pallas_call x0 -> x4, Pallas kernels: none -> 23.9 us  [the longest x1 15.7 us: per_device(): pl.pallas_call(functools.partial(hazard_kernel, levels), out_shape=jax.Sh...]
    sub x18 -> x0, other arithmetic: 16.3 us -> none  [the longest x16 12.7 us: exceed_rates(): median_base[:, None] + amplify[None, :]]
    mul x16 -> x0, other arithmetic: 10.6 us -> none  [exceed_rates(): return jnp.sum(chance * rup_rate[None, :, None], axis=1)]
  transfers between devices with their start and end apart: 2 -> 1, of which waited for: 2 -> 0; matrix products, arithmetic and copies ran while one was open for 2% -> 0% of each run, Pallas kernels for 0% -> 18%
where the time goes in v1:
time: 88.4 us; the launch traced here: 88 us
  blocking collectives  55.4 us (63%)
  Pallas kernels  23.9 us (27%)
  starting transfers between devices  7.22 us (8%)
    all_to_all x1, blocking collectives, per_device(): ruptures = lax.all_to_all(packed, 'rup', 0, 0, tiled=True)  20.7 us
    all_to_all x1, blocking collectives, per_device(): blocks = lax.all_to_all(spread, 'rup', 0, 0, tiled=True)  18.7 us
    all_to_all x1, blocking collectives, per_device(): curves = lax.all_to_all(send, 'site', 0, 0, tiled=True)  15.9 us
    pallas_call x1, Pallas kernels, per_device(): pl.pallas_call(functools.partial(hazard_kernel, levels), out_shape=jax.Sh...  15.7 us
    all_to_all x1, starting transfers between devices, per_device(): wanted = lax.all_to_all(relay_sites[0, 0], 'site', 0, 0, tiled=True)  7.22 us
    pallas_call x1, Pallas kernels, per_device(): pl.pallas_call(relay_kernel, out_shape=(jax.ShapeDtypeStruct((levels, sit...  3.95 us
    pallas_call x1, Pallas kernels, per_device(): pl.pallas_call(loss_kernel, out_shape=jax.ShapeDtypeStruct((bins, assets)...  2.87 us
  transfers between devices with their start and end apart: 1, of which 0 were waited for; matrix products, arithmetic and copies ran while one was open for 0% of the time, Pallas kernels for 18%

profile of v1, /device:TPU:1, one launch (start us, length us, event | category | flops | bytes accessed | tf_op | source)
XLA Modules:
  0.0 88.0 jit_solution(7910402484122958150)
XLA Ops:
  0.6 1.5 %shard_map.167 = f32[16,8,128]{2,1,0:T(8,128)} custom-call(f32[1,128]{1,0:T(1,128)} %bitcast.29, f32[1,128]{1,0:T(1,128)} %bitcast.30, f32[1,128]{1,0:T(1,128)} %bitcast.31, f32[1,128]{1,0:T(1,128)} %bitcast.32, s32[1,128]{1,0:T(1,128)} %bitcast.33, f32[1,64]{1,0:T(1,128)} %bitcast.34, f32[1,64]{1,0:T(1,128)} %bitcast.35), custom_call_target="tpu_custom_call" | custom-call | tf_op jit(solution)/shard_map/pallas_call | solution.py:206
  2.1 0.0 copy-start.3
  2.1 20.7 %all_to_all.26.rup_ref = f32[16,8,128]{2,1,0:T(8,128)S(1)} all-to-all(f32[16,8,128]{2,1,0:T(8,128)} %shard_map.167), channel_id=1, replica_groups=mesh['rup'=16,'site'=16] {'rup'}, dimensions={0} | all-to-all | bytes 131072 | tf_op jit(solution)/shard_map/all_to_all | solution.py:220
  22.8 0.0 copy-start.2
  22.8 0.0 copy-start.1
  22.8 7.2 %all-to-all-start.2 = ((s32[16,1,128]{2,1,0:T(1,128)}), s32[16,1,128]{2,1,0:T(1,128)S(1)}, u32[]{:S(2)}, u32[]{:S(2)}) async-start(s32[16,1,128]{2,1,0:T(1,128)} %bitcast.11), calls=%async_computation.2 | async-start | bytes 16384 | tf_op jit(solution)/shard_map/all_to_all | solution.py:204
  30.1 0.0 copy-done.3
  30.1 0.0 copy-done.2
  30.1 0.0 copy-done.1
  30.1 15.7 %shard_map.168 = f32[32,256]{1,0:T(8,128)S(1)} custom-call(s32[1]{0:T(128)} %bitcast.row_ref, f32[32,128]{1,0:T(8,128)S(1)} %bitcast.22, f32[32,128]{1,0:T(8,128)S(1)} %bitcast.23, f32[32,128]{1,0:T(8,128)S(1)} %bitcast.24, f32[16,8,128]{2,1,0:T(8,128)S(1)} %all_to_all.26.rup_ref), custom_call_target="tpu_custom_call" | custom-call | tf_op jit(solution)/shard_map/pallas_call | solution.py:223
  45.7 0.0 all-to-all-done.2
  45.8 18.7 %all_to_all.27.blocks_ref = f32[16,32,256]{2,1,0:T(8,128)S(1)} all-to-all(f32[16,32,256]{2,1,0:T(8,128)S(1)} %broadcast_in_dim.2), channel_id=1, replica_groups=mesh['rup'=16,'site'=16] {'rup'}, dimensions={0} | all-to-all | bytes 1048576 | tf_op jit(solution)/shard_map/all_to_all | solution.py:235
  64.5 0.0 copy-start
  64.5 3.9 %shard_map.169 = (f32[32,4096]{1,0:T(8,128)}, f32[16,32,128]{2,1,0:T(8,128)S(1)}) custom-call(f32[16,32,256]{2,1,0:T(8,128)S(1)} %all_to_all.27.blocks_ref, s32[16,128]{1,0:T(8,128)S(1)} %bitcast.21), custom_call_target="tpu_custom_call" | custom-call | tf_op jit(solution)/shard_map/pallas_call | solution.py:236
  68.5 0.0 copy-start.5
  68.5 0.0 copy-start.6
  68.5 15.9 %all_to_all.28.curves_ref = f32[16,32,128]{2,1,0:T(8,128)S(1)} all-to-all(f32[16,32,128]{2,1,0:T(8,128)S(1)} %get-tuple-element.5), channel_id=1, replica_groups=mesh['rup'=16,'site'=16] {'site'}, dimensions={0} | all-to-all | bytes 524288 | tf_op jit(solution)/shard_map/all_to_all | solution.py:246
  84.4 0.0 copy-start.4
  84.4 0.0 copy-start.7
  84.4 0.0 copy-done
  84.4 0.0 copy-done.5
  84.4 0.0 copy-done.6
  84.4 0.7 copy-done.4
  85.1 0.0 copy-done.7
  85.1 2.9 %shard_map.170 = f32[32,2048]{1,0:T(8,128)} custom-call(f32[16,32,128]{2,1,0:T(8,128)S(1)} %all_to_all.28.curves_ref, s32[16,128]{1,0:T(8,128)S(1)} %bitcast.25, s32[16,128]{1,0:T(8,128)S(1)} %bitcast.26, s32[16,128]{1,0:T(8,128)S(1)} %bitcast.27, s32[1,16]{1,0:T(1,128)S(1)} %bitcast.28, f32[1024,128]{1,0:T(8,128)S(1)} %bitcast.20), custom_call_target="tpu_custom_call" | custom-call | tf_op jit(solution)/shard_map/pallas_call | solution.py:248
  (1 shorter events, 0.0 us)
Async XLA Ops:
  2.1 28.0 %copy-start.3 = (f32[4096]{0:T(1024)S(1)}, f32[4096]{0:T(1024)}, u32[]{:S(2)}) copy-start(f32[4096]{0:T(1024)} %param.18) | copy-start | bytes 49156
  22.8 7.2 %copy-start.2 = (f32[4096]{0:T(1024)S(1)}, f32[4096]{0:T(1024)}, u32[]{:S(2)}) copy-start(f32[4096]{0:T(1024)} %param.17) | copy-start | bytes 49156
  22.8 7.2 %copy-start.1 = (f32[4096]{0:T(1024)S(1)}, f32[4096]{0:T(1024)}, u32[]{:S(2)}) copy-start(f32[4096]{0:T(1024)} %param.16) | copy-start | bytes 49156
  22.8 22.9 %all-to-all-start.2 = ((s32[16,1,128]{2,1,0:T(1,128)}), s32[16,1,128]{2,1,0:T(1,128)S(1)}, u32[]{:S(2)}, u32[]{:S(2)}) async-start(s32[16,1,128]{2,1,0:T(1,128)} %bitcast.11), calls=%async_computation.2 | async-start | bytes 16384 | tf_op jit(solution)/shard_map/all_to_all | solution.py:204
  64.5 19.9 %copy-start = (f32[128,32,32]{0,2,1:T(8,128)S(1)}, f32[128,32,32]{0,2,1:T(8,128)}, u32[]{:S(2)}) copy-start(f32[128,32,32]{0,2,1:T(8,128)} %param.31) | copy-start | bytes 1572868
  68.5 15.9 %copy-start.5 = (s32[2048]{0:T(1024)S(1)}, s32[2048]{0:T(1024)}, u32[]{:S(2)}) copy-start(s32[2048]{0:T(1024)} %param.29) | copy-start | bytes 24580
  68.5 15.9 %copy-start.6 = (s32[2048]{0:T(1024)S(1)}, s32[2048]{0:T(1024)}, u32[]{:S(2)}) copy-start(s32[2048]{0:T(1024)} %param.30) | copy-start | bytes 24580
  84.4 0.7 copy-start.4
  84.4 0.7 copy-start.7

commit v2 on v1

v2 whole, which is shorter than its diff:
```python
import functools
import math

import jax
import jax.numpy as jnp
from jax import lax
from jax.experimental import pallas as pl
from jax.experimental.pallas import tpu as pltpu
from jax.sharding import PartitionSpec as P

LANES = 128
SUBLANES = 8
LIST = 5
PRODUCTS = 2
VMEM = pl.BlockSpec(memory_space=pltpu.VMEM)
SMEM = pl.BlockSpec(memory_space=pltpu.SMEM)
LEVEL_FIRST = math.log(0.005)
LEVEL_RANGE = math.log(600.0)


def lane_gather(row, index):
    return jnp.take_along_axis(row, index, axis=1, mode="promise_in_bounds")


def partner(row, site, other):
    inner = lambda r: (((r & 3) + 1) >> 1) & 1
    south = lambda r: 2 * inner(r) - (r >> 2)
    z_lo = (site >> 3) ^ inner(row) ^ inner(other)
    y = (((site >> 1) & 3) - south(row) + south(other)) & 3
    core = (site & 1) ^ ((row & 3) >> 1) ^ ((other & 3) >> 1)
    return z_lo * 8 + y * 2 + core


def place():
    return lax.axis_index("rup"), lax.axis_index("site")


def split_in_three(value):
    high = value.astype(jnp.bfloat16)
    rest = value - high.astype(jnp.float32)
    middle = rest.astype(jnp.bfloat16)
    return high, middle, (rest - middle.astype(jnp.float32)).astype(jnp.bfloat16)


def pack_kernel(
    x_ref,
    y_ref,
    mag_ref,
    rate_ref,
    source_ref,
    relay_ref,
    sigma_ref,
    shift_ref,
    sx_ref,
    sy_ref,
    amp_ref,
    out_ref,
    own_ref,
):
    row, site = place()
    tiles = sx_ref.shape[0] // out_ref.shape[0]
    for i, ref in enumerate((sx_ref, sy_ref, amp_ref)):
        own_ref[i * tiles : (i + 1) * tiles, :] = ref[pl.ds(row * tiles, tiles), :]
    sources = sigma_ref.shape[1]
    own_ref[3 * tiles : 3 * tiles + 2, :] = jnp.zeros((2, LANES), jnp.float32)
    own_ref[3 * tiles : 3 * tiles + 1, 0:sources] = sigma_ref[...]
    own_ref[3 * tiles + 1 : 3 * tiles + 2, 0:sources] = shift_ref[...]
    source = source_ref[...].astype(jnp.float32)
    zero = jnp.zeros((1, LANES), jnp.float32)
    packed = jnp.concatenate(
        [x_ref[...], y_ref[...], mag_ref[...], rate_ref[...], source, zero, zero, zero], axis=0
    )
    for j in range(out_ref.shape[0]):
        out_ref[j] = packed
        wanted = relay_ref[pl.ds(partner(row, site, j), 1), :]
        out_ref[j, LIST : LIST + 1, :] = wanted.astype(jnp.float32)


def hazard_kernel(levels, own_ref, rup_ref, out_ref, pre_ref, acc_ref):
    blocks = rup_ref.shape[0]
    tiles = out_ref.shape[1] // levels
    units = LANES // SUBLANES
    step = LEVEL_RANGE / (levels - 1)
    wide = lambda i: jnp.broadcast_to(own_ref[i : i + 1, :], (SUBLANES, LANES))
    sigma, shift = wide(3 * tiles), wide(3 * tiles + 1)
    sites = [[wide(i * tiles + t) for i in range(3)] for t in range(tiles)]
    acc_ref[...] = jnp.zeros_like(acc_ref)
    part = lax.broadcasted_iota(jnp.int32, (4 * SUBLANES, 5 * LANES), 0)
    which = lax.broadcasted_iota(jnp.int32, (4 * SUBLANES, 5 * LANES), 1) >> 7
    chosen = (part < 3 * SUBLANES) & ((part & (SUBLANES - 1)) == which)
    spread_out = jnp.where(chosen, 1.0, 0.0).astype(jnp.bfloat16)

    def prepare(b):
        raw = rup_ref[b]
        index = jnp.broadcast_to(raw[4:5], (SUBLANES, LANES)).astype(jnp.int32)
        inverse = 1.0 / (lane_gather(sigma, index)[0:1] * math.sqrt(2.0))
        base = -1.0 + (raw[2:3] - 6.5) + lane_gather(shift, index)[0:1]
        zero = jnp.zeros((3, LANES), jnp.float32)
        rows = jnp.concatenate([raw[0:2], base, inverse, 0.5 * raw[3:4], zero], axis=0)
        thirds = [third.astype(jnp.float32) for third in split_in_three(rows)]
        stack = jnp.concatenate(thirds + [jnp.zeros_like(rows)], axis=0).astype(jnp.bfloat16)
        columns = lax.dot_general(
            stack, spread_out, (((0,), (0,)), ((), ())), preferred_element_type=jnp.float32
        )
        for u in range(units):
            x, y, base, inverse, rate = [
                columns[u * SUBLANES : (u + 1) * SUBLANES, p * LANES : (p + 1) * LANES]
                for p in range(5)
            ]
            k = b * units + u
            pre_ref[0, k] = rate
            pre_ref[1, k] = inverse * step
            for t in range(tiles):
                site_x, site_y, amp = sites[t]
                dx = site_x - x
                dy = site_y - y
                median = base + amp - 0.6 * jnp.log((dx * dx + dy * dy + 100.0) * 0.01)
                pre_ref[2 + t, k] = (LEVEL_FIRST - median) * inverse

    together = 8

    def prepare_some(g, carry):
        for i in range(together):
            prepare(g * together + i)
        return carry

    lax.fori_loop(0, blocks // together, prepare_some, 0)
    unroll = 2 * units

    for t in range(tiles):

        def add(g, carry):
            total = [None] * levels
            for u in range(unroll):
                k = g * unroll + u
                rate = pre_ref[0, k]
                gap = pre_ref[1, k]
                z = pre_ref[2 + t, k]
                whole = rate if u == 0 else whole + rate
                for l in range(levels):
                    term = rate * lax.erf(z)
                    total[l] = term if u == 0 else total[l] + term
                    if l < levels - 1:
                        z = z + gap
            for l in range(levels):
                at = t * levels + l
                acc_ref[at] = acc_ref[at] + (whole - total[l])
            return carry

        lax.fori_loop(0, blocks * units // unroll, add, 0)
    for t in range(tiles):
        for q in range(0, levels, SUBLANES):
            rates = jnp.concatenate(
                [
                    jnp.sum(acc_ref[t * levels + l], axis=0, keepdims=True)
                    for l in range(q, q + SUBLANES)
                ],
                axis=0,
            )
            hazard = 1.0 - jnp.exp(-rates)
            for b in range(blocks):
                out_ref[b, t * levels + q : t * levels + q + SUBLANES, :] = hazard
    for b in range(blocks):
        out_ref[b, tiles * levels : tiles * levels + SUBLANES, :] = jnp.broadcast_to(
            rup_ref[b, LIST : LIST + 1, :], (SUBLANES, LANES)
        )


def pick_by_product(lhs_ref, levels, index):
    span = lhs_ref.shape[1] // 3
    blocks = lhs_ref.shape[0] // levels
    width = index.shape[1]
    low = index & (span - 1)
    high = jnp.broadcast_to(index >> (span.bit_length() - 1), (SUBLANES, width))
    match = lax.broadcasted_iota(jnp.int32, (span, width), 0) == low
    onehot = jnp.where(match, 1.0, 0.0).astype(jnp.bfloat16)
    found = jnp.dot(
        lhs_ref[...],
        jnp.concatenate([onehot] * 3, axis=0),
        preferred_element_type=jnp.float32,
    )
    picked = [jnp.zeros((SUBLANES, width), jnp.float32)] * (levels // SUBLANES)
    for b in range(blocks):
        here = high == b
        for q in range(len(picked)):
            at = b * levels + q * SUBLANES
            picked[q] = jnp.where(here, found[at : at + SUBLANES], picked[q])
    return picked


def relay_kernel(levels, blocks_ref, send_ref, lhs_ref):
    blocks, rows, _ = blocks_ref.shape
    groups = levels // SUBLANES
    tiles = rows // levels
    lists = tiles * levels
    row, site = place()
    span = tiles * LANES
    for b in range(blocks):
        for t in range(tiles):
            thirds = split_in_three(blocks_ref[b, t * levels : (t + 1) * levels, :])
            for i in range(3):
                at = i * span + t * LANES
                lhs_ref[b * levels : (b + 1) * levels, at : at + LANES] = thirds[i]

    def by_product(k):
        index = jnp.concatenate([blocks_ref[k + i, lists : lists + 1, :] for i in range(2)], axis=1)
        picked = pick_by_product(lhs_ref, levels, index.astype(jnp.int32))
        for i in range(2):
            owner = partner(k + i, site, row)
            for q in range(groups):
                send_ref[owner, q * SUBLANES : (q + 1) * SUBLANES, :] = picked[q][
                    :, i * LANES : (i + 1) * LANES
                ]

    def by_gather(k):
        index = blocks_ref[k, lists : lists + SUBLANES, :].astype(jnp.int32)
        lane = index & (LANES - 1)
        tile = index >> 7
        picked = [jnp.zeros((SUBLANES, LANES), jnp.float32)] * groups
        for c in range(blocks * tiles):
            b, t = c // tiles, c % tiles
            here = tile == c
            for q in range(groups):
                at = t * levels + q * SUBLANES
                picked[q] = jnp.where(
                    here, lane_gather(blocks_ref[b, at : at + SUBLANES, :], lane), picked[q]
                )
        owner = partner(k, site, row)
        for q in range(groups):
            send_ref[owner, q * SUBLANES : (q + 1) * SUBLANES, :] = picked[q]

    products = blocks * 5 // 16
    for i in range(products):
        by_product(2 * i)
        by_gather(2 * products + i)
    for k in range(3 * products, blocks):
        by_gather(k)


def table_kernel(source_ref, pick_ref, count_ref, table_ref, slot_ref, split_ref):
    source = source_ref[...]
    count = jnp.zeros(source.shape, jnp.int32)
    for s in range(count_ref.shape[1]):
        count = jnp.where(source == s, count_ref[0, s], count)
    pick = pick_ref[...]
    quotient = jnp.floor(pick.astype(jnp.float32) / count.astype(jnp.float32)).astype(jnp.int32)
    slot = pick - quotient * count
    slot = jnp.where(slot < 0, slot + count, slot)
    slot_ref[...] = jnp.where(slot >= count, slot - count, slot)
    classes = table_ref.shape[1]
    table = table_ref[...]
    high = table.astype(jnp.bfloat16)
    split_ref[:, 0:classes] = high
    split_ref[:, classes : 2 * classes] = (table - high.astype(jnp.float32)).astype(jnp.bfloat16)


def loss_kernel(curves_ref, source_ref, slot_ref, class_ref, split_ref, out_ref, lhs_ref):
    sources, levels, _ = curves_ref.shape
    bins, assets = out_ref.shape
    classes = split_ref.shape[1] // 2
    groups = levels // SUBLANES
    width = 2 * LANES
    for s in range(sources):
        thirds = split_in_three(curves_ref[s])
        for i in range(3):
            at = i * width + (s % 2) * LANES
            lhs_ref[s // 2 * levels : (s // 2 + 1) * levels, at : at + LANES] = thirds[i]
    for t in range(assets // width):
        pair = range(2 * t, 2 * t + 2)
        if t % PRODUCTS == 0:
            index = jnp.concatenate(
                [source_ref[i : i + 1, :] * LANES + slot_ref[i : i + 1, :] for i in pair], axis=1
            )
            picked = pick_by_product(lhs_ref, levels, index)
        else:
            halves = []
            for i in pair:
                lane = jnp.broadcast_to(slot_ref[i : i + 1, :], (SUBLANES, LANES))
                which = jnp.broadcast_to(source_ref[i : i + 1, :], (SUBLANES, LANES))
                half = [jnp.zeros((SUBLANES, LANES), jnp.float32)] * groups
                for s in range(sources):
                    here = which == s
                    for q in range(groups):
                        part = curves_ref[s, q * SUBLANES : (q + 1) * SUBLANES, :]
                        half[q] = jnp.where(here, lane_gather(part, lane), half[q])
                halves.append(half)
            picked = [jnp.concatenate([h[q] for h in halves], axis=1) for q in range(groups)]
        curves = jnp.concatenate(picked, axis=0)
        following = jnp.concatenate([curves[1:], jnp.zeros((1, width), jnp.float32)], axis=0)
        occurrence = curves - following
        kinds = jnp.concatenate([class_ref[i : i + 1, :] for i in pair], axis=1)
        match = lax.broadcasted_iota(jnp.int32, (classes, width), 0) == kinds
        onehot = jnp.where(match, 1.0, 0.0).astype(jnp.bfloat16)
        both = jnp.concatenate([onehot, onehot], axis=0)
        chosen = jnp.dot(split_ref[...], both, preferred_element_type=jnp.float32)
        total = jnp.zeros((bins, width), jnp.float32)
        for l in range(levels):
            total = total + occurrence[l : l + 1, :] * chosen[l * bins : (l + 1) * bins, :]
        out_ref[:, t * width : (t + 1) * width] = total


def per_device(
    site_x,
    site_y,
    site_amp,
    rup_x,
    rup_y,
    rup_mag,
    rup_rate,
    rup_source,
    src_sigma,
    src_shift,
    relay_sites,
    relay_count,
    asset_source,
    asset_pick,
    asset_class,
    vulnerability,
    rows,
    columns,
):
    classes, levels, bins = vulnerability.shape
    sites = site_x.shape[0]
    sources, capacity = relay_sites.shape[2:]
    assets = asset_source.shape[0]
    own_sites = sites // rows
    limit = pltpu.CompilerParams(vmem_limit_bytes=48 * 2**20)

    line = lambda a: a.reshape(1, -1)
    square = lambda a: a.reshape(-1, LANES)
    tiles = own_sites // LANES
    packed, own = pl.pallas_call(
        pack_kernel,
        out_shape=(
            jax.ShapeDtypeStruct((rows, SUBLANES, LANES), jnp.float32),
            jax.ShapeDtypeStruct((3 * tiles + 2, LANES), jnp.float32),
        ),
        in_specs=[VMEM] * 11,
        out_specs=(VMEM, VMEM),
    )(
        line(rup_x),
        line(rup_y),
        line(rup_mag),
        line(rup_rate),
        line(rup_source),
        relay_sites[0, 0],
        line(src_sigma),
        line(src_shift),
        square(site_x),
        square(site_y),
        square(site_amp),
    )
    groups = [[j * columns + partner(0, d, j) for j in range(rows)] for d in range(columns)]
    ruptures = lax.all_to_all(packed, ("rup", "site"), 0, 0, axis_index_groups=groups, tiled=True)
    height = tiles * levels + SUBLANES
    copies = pl.pallas_call(
        functools.partial(hazard_kernel, levels),
        out_shape=jax.ShapeDtypeStruct((rows, height, LANES), jnp.float32),
        in_specs=[VMEM] * 2,
        out_specs=VMEM,
        scratch_shapes=[
            pltpu.VMEM((2 + tiles, rows * LANES // SUBLANES, SUBLANES, LANES), jnp.float32),
            pltpu.VMEM((tiles * levels, SUBLANES, LANES), jnp.float32),
        ],
        compiler_params=limit,
    )(own, ruptures)
    blocks = lax.all_to_all(copies, "rup", 0, 0, tiled=True)
    hazard = blocks[:, : tiles * levels].reshape(rows, tiles, levels, LANES)
    hazard = jnp.transpose(hazard, (2, 0, 1, 3)).reshape(levels, sites)
    send = pl.pallas_call(
        functools.partial(relay_kernel, levels),
        out_shape=jax.ShapeDtypeStruct((columns, levels, capacity), jnp.float32),
        in_specs=[VMEM],
        out_specs=VMEM,
        scratch_shapes=[pltpu.VMEM((rows * levels, 3 * own_sites), jnp.bfloat16)],
        compiler_params=limit,
    )(blocks)
    curves = lax.all_to_all(send, "site", 0, 0, tiled=True)
    table = jnp.transpose(vulnerability, (1, 2, 0)).reshape(levels * bins, classes)
    slot, split = pl.pallas_call(
        table_kernel,
        out_shape=(
            jax.ShapeDtypeStruct((assets // LANES, LANES), jnp.int32),
            jax.ShapeDtypeStruct((levels * bins, 2 * classes), jnp.bfloat16),
        ),
        in_specs=[VMEM, VMEM, SMEM, VMEM],
        out_specs=(VMEM, VMEM),
        compiler_params=limit,
    )(square(asset_source), square(asset_pick), relay_count.reshape(1, sources), table)
    losses = pl.pallas_call(
        loss_kernel,
        out_shape=jax.ShapeDtypeStruct((bins, assets), jnp.float32),
        in_specs=[VMEM] * 5,
        out_specs=VMEM,
        scratch_shapes=[pltpu.VMEM((sources * levels // 2, 6 * LANES), jnp.bfloat16)],
        compiler_params=limit,
    )(curves, square(asset_source), slot, square(asset_class), split)
    return hazard, losses


def solution(mesh):
    return jax.shard_map(
        functools.partial(per_device, rows=mesh.shape["rup"], columns=mesh.shape["site"]),
        mesh=mesh,
        in_specs=(
            P("site"),
            P("site"),
            P("site"),
            P("rup"),
            P("rup"),
            P("rup"),
            P("rup"),
            P("rup"),
            P(),
            P(),
            P("rup", "site", None, None),
            P("rup", "site", None),
            P(("rup", "site")),
            P(("rup", "site")),
            P(("rup", "site")),
            P(),
        ),
        out_specs=(P(None, "site"), P(None, ("rup", "site"))),
        check_vma=False,
    )
```

time: 88.4 us -> 77.8 us (0.88)
  blocking collectives: 55.4 us -> 44.1 us
  Pallas kernels: 23.9 us -> 17.8 us
  waiting for transfers between devices: 0.01 us -> 4.16 us
  local copies, waits for them, and re-layouts: 0.75 us -> 2.3 us
  starting transfers between devices: 7.22 us -> 8.27 us
    all_to_all x3 -> x2, blocking collectives: 55.4 us -> 44.1 us  [the longest x1 24.7 us: per_device(): lax.all_to_all(packed, ('rup', 'site'), 0, 0, axis_index_groups=groups, t...]
    pallas_call x1, Pallas kernels: 15.7 us -> 11.2 us  [per_device(): pl.pallas_call(functools.partial(hazard_kernel, levels), out_shape=jax.Sh...]
    all_to_all x1, waiting for transfers between devices: 0.01 us -> 4.16 us  [per_device(): curves = lax.all_to_all(send, 'site', 0, 0, tiled=True)]
    pallas_call x2 -> x3, Pallas kernels: 5.42 us -> 4.12 us  [the longest x1 1.93 us: per_device(): pl.pallas_call(functools.partial(relay_kernel, levels), out_shape=jax.Sha...]
    reshape x0 -> x1, local copies, waits for them, and re-layouts: none -> 1.21 us  [per_device(): hazard = jnp.transpose(hazard, (2, 0, 1, 3)).reshape(levels, sites)]
    all_to_all x1, starting transfers between devices: 7.22 us -> 8.27 us  [per_device(): curves = lax.all_to_all(send, 'site', 0, 0, tiled=True)]
  transfers between devices with their start and end apart: 1 -> 1, of which waited for: 0 -> 1; matrix products, arithmetic and copies ran while one was open for 0% -> 2% of each run, Pallas kernels for 18% -> 1%
where the time goes in v2:
time: 77.8 us; the launch traced here: 77.3 us
  blocking collectives  44.1 us (57%)
  Pallas kernels  17.8 us (23%)
  starting transfers between devices  8.27 us (11%)
  waiting for transfers between devices  4.16 us (5%)
  local copies, waits for them, and re-layouts  2.3 us (3%)
    all_to_all x1, blocking collectives, per_device(): lax.all_to_all(packed, ('rup', 'site'), 0, 0, axis_index_groups=groups, t...  24.7 us
    all_to_all x1, blocking collectives, per_device(): blocks = lax.all_to_all(copies, 'rup', 0, 0, tiled=True)  19.4 us
    pallas_call x1, Pallas kernels, per_device(): pl.pallas_call(functools.partial(hazard_kernel, levels), out_shape=jax.Sh...  11.2 us
    all_to_all x1, starting transfers between devices, per_device(): curves = lax.all_to_all(send, 'site', 0, 0, tiled=True)  8.27 us
    all_to_all x1, waiting for transfers between devices, per_device(): curves = lax.all_to_all(send, 'site', 0, 0, tiled=True)  4.16 us
    pallas_call x1, Pallas kernels, per_device(): pl.pallas_call(loss_kernel, out_shape=jax.ShapeDtypeStruct((bins, assets)...  2.51 us
    pallas_call x1, Pallas kernels, per_device(): pl.pallas_call(functools.partial(relay_kernel, levels), out_shape=jax.Sha...  1.93 us
  transfers between devices with their start and end apart: 1, of which 1 were waited for; matrix products, arithmetic and copies ran while one was open for 2% of the time, Pallas kernels for 1%

profile of v2, /device:TPU:1, one launch (start us, length us, event | category | flops | bytes accessed | tf_op | source)
XLA Modules:
  0.0 77.3 jit_solution(6712999191009858350)
XLA Ops:
  0.6 1.5 %shard_map.167 = (f32[16,8,128]{2,1,0:T(8,128)}, f32[8,128]{1,0:T(8,128)}) custom-call(f32[1,128]{1,0:T(1,128)} %bitcast.32, f32[1,128]{1,0:T(1,128)} %bitcast.33, f32[1,128]{1,0:T(1,128)} %bitcast.34, f32[1,128]{1,0:T(1,128)} %bitcast.35, s32[1,128]{1,0:T(1,128)} %bitcast.36, s32[16,128]{1,0:T(8,128)} %bitcast.31, f32[1,64]{1,0:T(1,128)} %bitcast.37, ...), custom_call_target="tpu_custom_call" | custom-call | tf_op jit(solution)/shard_map/pallas_call | solution.py:332
  2.2 0.0 copy-start.4
  2.2 24.7 %all_to_all.15.rup_ref = f32[16,8,128]{2,1,0:T(8,128)S(1)} all-to-all(f32[16,8,128]{2,1,0:T(8,128)} %get-tuple-element.7), channel_id=1, replica_groups={{0,28,45,49,70,90,107,119,132,152,169,181,194,222,239,243},{1,29,44,48,..., dimensions={0} | all-to-all | bytes 131072 | tf_op jit(solution)/shard_map/all_to_all | solution.py:354
  26.8 0.0 copy-done.4
  26.8 11.2 %shard_map.168 = f32[16,72,128]{2,1,0:T(8,128)S(1)} custom-call(f32[8,128]{1,0:T(8,128)S(1)} %copy-done.4, f32[16,8,128]{2,1,0:T(8,128)S(1)} %all_to_all.15.rup_ref), custom_call_target="tpu_custom_call" | custom-call | tf_op jit(solution)/shard_map/pallas_call | solution.py:356
  38.1 19.4 %all_to_all.16.blocks_ref = f32[16,72,128]{2,1,0:T(8,128)S(1)} all-to-all(f32[16,72,128]{2,1,0:T(8,128)S(1)} %shard_map.168), channel_id=1, replica_groups=mesh['rup'=16,'site'=16] {'rup'}, dimensions={0} | all-to-all | bytes 1179648 | tf_op jit(solution)/shard_map/all_to_all | solution.py:367
  57.4 0.0 copy-start
  57.4 1.9 %shard_map.169 = f32[16,32,128]{2,1,0:T(8,128)} custom-call(f32[16,72,128]{2,1,0:T(8,128)S(1)} %all_to_all.16.blocks_ref), custom_call_target="tpu_custom_call" | custom-call | tf_op jit(solution)/shard_map/pallas_call | solution.py:370
  59.4 0.0 copy-start.1
  59.4 0.0 copy-start.2
  59.4 8.3 %all-to-all-start.2 = ((f32[16,32,128]{2,1,0:T(8,128)}), f32[16,32,128]{2,1,0:T(8,128)S(1)}, u32[]{:S(2)}, u32[]{:S(2)}) async-start(f32[16,32,128]{2,1,0:T(8,128)} %shard_map.169), calls=%async_computation.2 | async-start | bytes 524288 | tf_op jit(solution)/shard_map/all_to_all | solution.py:378
  67.7 0.0 copy-start.5
  67.7 0.0 copy-done
  67.7 0.0 copy-done.1
  67.7 0.0 copy-done.2
  67.7 0.6 copy-done.5
  68.3 0.7 shard_map.170
  69.0 0.4 copy.18
  69.5 0.0 copy-start.3
  69.5 1.2 %reshape.67 = f32[32,4096]{1,0:T(8,128)} reshape(f32[32,16,2,128]{3,2,1,0:T(2,128)S(1)} %copy.18) | data formatting | bytes 1048576 | tf_op jit(solution)/shard_map/reshape | solution.py:369
  70.7 4.2 %all-to-all-done.2.curves_ref = f32[16,32,128]{2,1,0:T(8,128)S(1)} async-done(((f32[16,32,128]{2,1,0:T(8,128)}), f32[16,32,128]{2,1,0:T(8,128)S(1)}, u32[]{:S(2)}, u32[]{:S(2)}) %all-to-all-start.2) | async-done | bytes 262176 | tf_op jit(solution)/shard_map/all_to_all | solution.py:378
  74.8 0.0 copy-done.3
  74.8 2.5 %shard_map.171 = f32[32,2048]{1,0:T(8,128)} custom-call(f32[16,32,128]{2,1,0:T(8,128)S(1)} %all-to-all-done.2.curves_ref, s32[16,128]{1,0:T(8,128)S(1)} %bitcast.23, s32[16,128]{1,0:T(8,128)S(1)} %get-tuple-element.8.slot_ref, s32[16,128]{1,0:T(8,128)S(1)} %bitcast.25, bf16[1024,256]{1,0:T(8,128)(2,1)S(1)} %get-tuple-element.9.split_ref), custom_call_target="tpu_custom_call" | custom-call | tf_op jit(solution)/shard_map/pallas_call | solution.py:390
  (1 shorter events, 0.0 us)
Async XLA Ops:
  2.2 24.7 %copy-start.4 = (f32[8,128]{1,0:T(8,128)S(1)}, f32[8,128]{1,0:T(8,128)}, u32[]{:S(2)}) copy-start(f32[8,128]{1,0:T(8,128)} %get-tuple-element.6.own_ref) | copy-start | bytes 12292
  57.4 10.2 %copy-start = (f32[128,32,32]{0,2,1:T(8,128)S(1)}, f32[128,32,32]{0,2,1:T(8,128)}, u32[]{:S(2)}) copy-start(f32[128,32,32]{0,2,1:T(8,128)} %param.31) | copy-start | bytes 1572868
  59.4 8.3 %copy-start.1 = (s32[2048]{0:T(1024)S(1)}, s32[2048]{0:T(1024)}, u32[]{:S(2)}) copy-start(s32[2048]{0:T(1024)} %param.28) | copy-start | bytes 24580
  59.4 8.3 %copy-start.2 = (s32[2048]{0:T(1024)S(1)}, s32[2048]{0:T(1024)}, u32[]{:S(2)}) copy-start(s32[2048]{0:T(1024)} %param.29) | copy-start | bytes 24580
  59.4 15.4 %all-to-all-start.2 = ((f32[16,32,128]{2,1,0:T(8,128)}), f32[16,32,128]{2,1,0:T(8,128)S(1)}, u32[]{:S(2)}, u32[]{:S(2)}) async-start(f32[16,32,128]{2,1,0:T(8,128)} %shard_map.169), calls=%async_computation.2 | async-start | bytes 524288 | tf_op jit(solution)/shard_map/all_to_all | solution.py:378
  67.7 0.7 copy-start.5
  69.5 5.4 %copy-start.3 = (s32[2048]{0:T(1024)S(1)}, s32[2048]{0:T(1024)}, u32[]{:S(2)}) copy-start(s32[2048]{0:T(1024)} %param.30) | copy-start | bytes 24580

commit v3 on v2

--- a/solution.py
+++ b/solution.py
@@ -11,6 +11,7 @@
 LANES = 128
 SUBLANES = 8
 LIST = 5
+UNROLL = 24
 PRODUCTS = 2
 VMEM = pl.BlockSpec(memory_space=pltpu.VMEM)
 SMEM = pl.BlockSpec(memory_space=pltpu.SMEM)
@@ -42,112 +43,127 @@
     return high, middle, (rest - middle.astype(jnp.float32)).astype(jnp.bfloat16)
 
 
-def pack_kernel(
-    x_ref,
-    y_ref,
-    mag_ref,
-    rate_ref,
-    source_ref,
-    relay_ref,
-    sigma_ref,
-    shift_ref,
-    sx_ref,
-    sy_ref,
-    amp_ref,
-    out_ref,
-    own_ref,
+def pack_kernel(x_ref, y_ref, mag_ref, rate_ref, source_ref, relay_ref, out_ref):
+    row, site = place()
+    source = source_ref[...].astype(jnp.float32)
+    zero = jnp.zeros((1, LANES), jnp.float32)
+    packed = jnp.concatenate(
+        [x_ref[...], y_ref[...], mag_ref[...], rate_ref[...], source, zero, zero, zero], axis=0
+    )
+    for j in range(out_ref.shape[0]):
+        out_ref[j] = packed
+        wanted = relay_ref[pl.ds(partner(row, site, j), 1), :]
+        out_ref[j, LIST : LIST + 1, :] = wanted.astype(jnp.float32)
+
+
+def wide(row):
+    return jnp.broadcast_to(row, (SUBLANES, LANES))
+
+
+def spreading():
+    part = lax.broadcasted_iota(jnp.int32, (4 * SUBLANES, 5 * LANES), 0)
+    which = lax.broadcasted_iota(jnp.int32, (4 * SUBLANES, 5 * LANES), 1) >> 7
+    chosen = (part < 3 * SUBLANES) & ((part & (SUBLANES - 1)) == which)
+    return jnp.where(chosen, 1.0, 0.0).astype(jnp.bfloat16)
+
+
+def prepare(raw, at, levels, own_ref, spread_out, pre_ref):
+    tiles = pre_ref.shape[0] - 2
+    units = LANES // SUBLANES
+    step = LEVEL_RANGE / (levels - 1)
+    index = wide(raw[4:5]).astype(jnp.int32)
+    sigma = wide(own_ref[3 * tiles : 3 * tiles + 1, :])
+    shift = wide(own_ref[3 * tiles + 1 : 3 * tiles + 2, :])
+    inverse = 1.0 / (lane_gather(sigma, index)[0:1] * math.sqrt(2.0))
+    base = -1.0 + (raw[2:3] - 6.5) + lane_gather(shift, index)[0:1]
+    zero = jnp.zeros((3, LANES), jnp.float32)
+    rows = jnp.concatenate([raw[0:2], base, inverse, 0.5 * raw[3:4], zero], axis=0)
+    thirds = [third.astype(jnp.float32) for third in split_in_three(rows)]
+    stack = jnp.concatenate(thirds + [jnp.zeros_like(rows)], axis=0).astype(jnp.bfloat16)
+    columns = lax.dot_general(
+        stack, spread_out, (((0,), (0,)), ((), ())), preferred_element_type=jnp.float32
+    )
+    sites = [[wide(own_ref[i * tiles + t : i * tiles + t + 1, :]) for i in range(3)] for t in range(tiles)]
+    for u in range(units):
+        x, y, base, inverse, rate = [
+            columns[u * SUBLANES : (u + 1) * SUBLANES, p * LANES : (p + 1) * LANES]
+            for p in range(5)
+        ]
+        k = at * units + u
+        pre_ref[0, k] = rate
+        pre_ref[1, k] = inverse * step
+        for t in range(tiles):
+            site_x, site_y, amp = sites[t]
+            dx = site_x - x
+            dy = site_y - y
+            median = base + amp - 0.6 * jnp.log((dx * dx + dy * dy + 100.0) * 0.01)
+            pre_ref[2 + t, k] = (LEVEL_FIRST - median) * inverse
+
+
+def tails(first, count, t, levels, pre_ref):
+    total = [None] * levels
+    for u in range(count):
+        rate = pre_ref[0, first + u]
+        gap = pre_ref[1, first + u]
+        z = pre_ref[2 + t, first + u]
+        whole = rate if u == 0 else whole + rate
+        for l in range(levels):
+            term = rate * lax.erf(z)
+            total[l] = term if u == 0 else total[l] + term
+            if l < levels - 1:
+                z = z + gap
+    return [whole - part for part in total]
+
+
+def own_kernel(
+    levels, rup_ref, sx_ref, sy_ref, amp_ref, sigma_ref, shift_ref, own_ref, acc_ref, pre_ref
 ):
-    row, site = place()
-    tiles = sx_ref.shape[0] // out_ref.shape[0]
+    rows = rup_ref.shape[0]
+    row = place()[0]
+    tiles = sx_ref.shape[0] // rows
     for i, ref in enumerate((sx_ref, sy_ref, amp_ref)):
         own_ref[i * tiles : (i + 1) * tiles, :] = ref[pl.ds(row * tiles, tiles), :]
     sources = sigma_ref.shape[1]
     own_ref[3 * tiles : 3 * tiles + 2, :] = jnp.zeros((2, LANES), jnp.float32)
     own_ref[3 * tiles : 3 * tiles + 1, 0:sources] = sigma_ref[...]
     own_ref[3 * tiles + 1 : 3 * tiles + 2, 0:sources] = shift_ref[...]
-    source = source_ref[...].astype(jnp.float32)
-    zero = jnp.zeros((1, LANES), jnp.float32)
-    packed = jnp.concatenate(
-        [x_ref[...], y_ref[...], mag_ref[...], rate_ref[...], source, zero, zero, zero], axis=0
-    )
-    for j in range(out_ref.shape[0]):
-        out_ref[j] = packed
-        wanted = relay_ref[pl.ds(partner(row, site, j), 1), :]
-        out_ref[j, LIST : LIST + 1, :] = wanted.astype(jnp.float32)
-
-
-def hazard_kernel(levels, own_ref, rup_ref, out_ref, pre_ref, acc_ref):
+    prepare(rup_ref[0], 0, levels, own_ref, spreading(), pre_ref)
+    for t in range(tiles):
+        sums = tails(0, LANES // SUBLANES, t, levels, pre_ref)
+        for l in range(levels):
+            acc_ref[t * levels + l] = sums[l]
+
+
+def hazard_kernel(levels, own_ref, sums_ref, rup_ref, out_ref, pre_ref, acc_ref):
     blocks = rup_ref.shape[0]
     tiles = out_ref.shape[1] // levels
     units = LANES // SUBLANES
-    step = LEVEL_RANGE / (levels - 1)
-    wide = lambda i: jnp.broadcast_to(own_ref[i : i + 1, :], (SUBLANES, LANES))
-    sigma, shift = wide(3 * tiles), wide(3 * tiles + 1)
-    sites = [[wide(i * tiles + t) for i in range(3)] for t in range(tiles)]
-    acc_ref[...] = jnp.zeros_like(acc_ref)
-    part = lax.broadcasted_iota(jnp.int32, (4 * SUBLANES, 5 * LANES), 0)
-    which = lax.broadcasted_iota(jnp.int32, (4 * SUBLANES, 5 * LANES), 1) >> 7
-    chosen = (part < 3 * SUBLANES) & ((part & (SUBLANES - 1)) == which)
-    spread_out = jnp.where(chosen, 1.0, 0.0).astype(jnp.bfloat16)
-
-    def prepare(b):
-        raw = rup_ref[b]
-        index = jnp.broadcast_to(raw[4:5], (SUBLANES, LANES)).astype(jnp.int32)
-        inverse = 1.0 / (lane_gather(sigma, index)[0:1] * math.sqrt(2.0))
-        base = -1.0 + (raw[2:3] - 6.5) + lane_gather(shift, index)[0:1]
-        zero = jnp.zeros((3, LANES), jnp.float32)
-        rows = jnp.concatenate([raw[0:2], base, inverse, 0.5 * raw[3:4], zero], axis=0)
-        thirds = [third.astype(jnp.float32) for third in split_in_three(rows)]
-        stack = jnp.concatenate(thirds + [jnp.zeros_like(rows)], axis=0).astype(jnp.bfloat16)
-        columns = lax.dot_general(
-            stack, spread_out, (((0,), (0,)), ((), ())), preferred_element_type=jnp.float32
-        )
-        for u in range(units):
-            x, y, base, inverse, rate = [
-                columns[u * SUBLANES : (u + 1) * SUBLANES, p * LANES : (p + 1) * LANES]
-                for p in range(5)
-            ]
-            k = b * units + u
-            pre_ref[0, k] = rate
-            pre_ref[1, k] = inverse * step
-            for t in range(tiles):
-                site_x, site_y, amp = sites[t]
-                dx = site_x - x
-                dy = site_y - y
-                median = base + amp - 0.6 * jnp.log((dx * dx + dy * dy + 100.0) * 0.01)
-                pre_ref[2 + t, k] = (LEVEL_FIRST - median) * inverse
-
-    together = 8
+    row = place()[0]
+    spread_out = spreading()
+    acc_ref[...] = sums_ref[...]
+    others = blocks - 1
+    together = 5
 
     def prepare_some(g, carry):
         for i in range(together):
-            prepare(g * together + i)
+            at = g * together + i
+            block = (row + 1 + at) & (blocks - 1)
+            prepare(rup_ref[block], at, levels, own_ref, spread_out, pre_ref)
         return carry
 
-    lax.fori_loop(0, blocks // together, prepare_some, 0)
-    unroll = 2 * units
+    lax.fori_loop(0, others // together, prepare_some, 0)
+    unroll = UNROLL
 
     for t in range(tiles):
 
         def add(g, carry):
-            total = [None] * levels
-            for u in range(unroll):
-                k = g * unroll + u
-                rate = pre_ref[0, k]
-                gap = pre_ref[1, k]
-                z = pre_ref[2 + t, k]
-                whole = rate if u == 0 else whole + rate
-                for l in range(levels):
-                    term = rate * lax.erf(z)
-                    total[l] = term if u == 0 else total[l] + term
-                    if l < levels - 1:
-                        z = z + gap
+            sums = tails(g * unroll, unroll, t, levels, pre_ref)
             for l in range(levels):
                 at = t * levels + l
-                acc_ref[at] = acc_ref[at] + (whole - total[l])
+                acc_ref[at] = acc_ref[at] + sums[l]
             return carry
 
-        lax.fori_loop(0, blocks * units // unroll, add, 0)
+        lax.fori_loop(0, others * units // unroll, add, 0)
     for t in range(tiles):
         for q in range(0, levels, SUBLANES):
             rates = jnp.concatenate(
@@ -161,8 +177,8 @@
             for b in range(blocks):
                 out_ref[b, t * levels + q : t * levels + q + SUBLANES, :] = hazard
     for b in range(blocks):
-        out_ref[b, tiles * levels : tiles * levels + SUBLANES, :] = jnp.broadcast_to(
-            rup_ref[b, LIST : LIST + 1, :], (SUBLANES, LANES)
+        out_ref[b, tiles * levels : tiles * levels + SUBLANES, :] = wide(
+            rup_ref[b, LIST : LIST + 1, :]
         )
 
 
@@ -254,7 +270,9 @@
     split_ref[:, classes : 2 * classes] = (table - high.astype(jnp.float32)).astype(jnp.bfloat16)
 
 
-def loss_kernel(curves_ref, source_ref, slot_ref, class_ref, split_ref, out_ref, lhs_ref):
+def loss_kernel(
+    curves_ref, source_ref, slot_ref, class_ref, split_ref, out_ref, lhs_ref, change_ref
+):
     sources, levels, _ = curves_ref.shape
     bins, assets = out_ref.shape
     classes = split_ref.shape[1] // 2
@@ -265,38 +283,44 @@
         for i in range(3):
             at = i * width + (s % 2) * LANES
             lhs_ref[s // 2 * levels : (s // 2 + 1) * levels, at : at + LANES] = thirds[i]
+
+    def by_product(t):
+        index = jnp.concatenate(
+            [source_ref[i : i + 1, :] * LANES + slot_ref[i : i + 1, :] for i in (2 * t, 2 * t + 1)],
+            axis=1,
+        )
+        return pick_by_product(lhs_ref, levels, index)
+
+    def by_gather(t):
+        halves = []
+        for i in (2 * t, 2 * t + 1):
+            lane = wide(slot_ref[i : i + 1, :])
+            which = wide(source_ref[i : i + 1, :])
+            half = [jnp.zeros((SUBLANES, LANES), jnp.float32)] * groups
+            for s in range(sources):
+                here = which == s
+                for q in range(groups):
+                    part = curves_ref[s, q * SUBLANES : (q + 1) * SUBLANES, :]
+                    half[q] = jnp.where(here, lane_gather(part, lane), half[q])
+            halves.append(half)
+        return [jnp.concatenate([h[q] for h in halves], axis=1) for q in range(groups)]
+
     for t in range(assets // width):
-        pair = range(2 * t, 2 * t + 2)
-        if t % PRODUCTS == 0:
-            index = jnp.concatenate(
-                [source_ref[i : i + 1, :] * LANES + slot_ref[i : i + 1, :] for i in pair], axis=1
-            )
-            picked = pick_by_product(lhs_ref, levels, index)
-        else:
-            halves = []
-            for i in pair:
-                lane = jnp.broadcast_to(slot_ref[i : i + 1, :], (SUBLANES, LANES))
-                which = jnp.broadcast_to(source_ref[i : i + 1, :], (SUBLANES, LANES))
-                half = [jnp.zeros((SUBLANES, LANES), jnp.float32)] * groups
-                for s in range(sources):
-                    here = which == s
-                    for q in range(groups):
-                        part = curves_ref[s, q * SUBLANES : (q + 1) * SUBLANES, :]
-                        half[q] = jnp.where(here, lane_gather(part, lane), half[q])
-                halves.append(half)
-            picked = [jnp.concatenate([h[q] for h in halves], axis=1) for q in range(groups)]
-        curves = jnp.concatenate(picked, axis=0)
+        curves = jnp.concatenate(by_product(t) if t < PRODUCTS else by_gather(t), axis=0)
         following = jnp.concatenate([curves[1:], jnp.zeros((1, width), jnp.float32)], axis=0)
-        occurrence = curves - following
-        kinds = jnp.concatenate([class_ref[i : i + 1, :] for i in pair], axis=1)
+        change_ref[:, t * width : (t + 1) * width] = curves - following
+    for t in range(assets // width):
+        across = slice(t * width, (t + 1) * width)
+        kinds = jnp.concatenate([class_ref[i : i + 1, :] for i in (2 * t, 2 * t + 1)], axis=1)
         match = lax.broadcasted_iota(jnp.int32, (classes, width), 0) == kinds
         onehot = jnp.where(match, 1.0, 0.0).astype(jnp.bfloat16)
         both = jnp.concatenate([onehot, onehot], axis=0)
         chosen = jnp.dot(split_ref[...], both, preferred_element_type=jnp.float32)
         total = jnp.zeros((bins, width), jnp.float32)
         for l in range(levels):
-            total = total + occurrence[l : l + 1, :] * chosen[l * bins : (l + 1) * bins, :]
-        out_ref[:, t * width : (t + 1) * width] = total
+            part = chosen[l * bins : (l + 1) * bins, :]
+            total = total + change_ref[l : l + 1, across] * part
+        out_ref[:, across] = total
 
 
 def per_device(
@@ -329,14 +353,11 @@
     line = lambda a: a.reshape(1, -1)
     square = lambda a: a.reshape(-1, LANES)
     tiles = own_sites // LANES
-    packed, own = pl.pallas_call(
+    packed = pl.pallas_call(
         pack_kernel,
-        out_shape=(
-            jax.ShapeDtypeStruct((rows, SUBLANES, LANES), jnp.float32),
-            jax.ShapeDtypeStruct((3 * tiles + 2, LANES), jnp.float32),
-        ),
-        in_specs=[VMEM] * 11,
-        out_specs=(VMEM, VMEM),
+        out_shape=jax.ShapeDtypeStruct((rows, SUBLANES, LANES), jnp.float32),
+        in_specs=[VMEM] * 6,
+        out_specs=VMEM,
     )(
         line(rup_x),
         line(rup_y),
@@ -344,11 +365,26 @@
         line(rup_rate),
         line(rup_source),
         relay_sites[0, 0],
-        line(src_sigma),
-        line(src_shift),
+    )
+    units = rows * LANES // SUBLANES
+    sums_shape = (tiles * levels, SUBLANES, LANES)
+    own, sums = pl.pallas_call(
+        functools.partial(own_kernel, levels),
+        out_shape=(
+            jax.ShapeDtypeStruct((3 * tiles + 2, LANES), jnp.float32),
+            jax.ShapeDtypeStruct(sums_shape, jnp.float32),
+        ),
+        in_specs=[VMEM] * 6,
+        out_specs=(VMEM, VMEM),
+        scratch_shapes=[pltpu.VMEM((2 + tiles, units // rows, SUBLANES, LANES), jnp.float32)],
+        compiler_params=limit,
+    )(
+        packed,
         square(site_x),
         square(site_y),
         square(site_amp),
+        line(src_sigma),
+        line(src_shift),
     )
     groups = [[j * columns + partner(0, d, j) for j in range(rows)] for d in range(columns)]
     ruptures = lax.all_to_all(packed, ("rup", "site"), 0, 0, axis_index_groups=groups, tiled=True)
@@ -356,14 +392,14 @@
     copies = pl.pallas_call(
         functools.partial(hazard_kernel, levels),
         out_shape=jax.ShapeDtypeStruct((rows, height, LANES), jnp.float32),
-        in_specs=[VMEM] * 2,
+        in_specs=[VMEM] * 3,
         out_specs=VMEM,
         scratch_shapes=[
-            pltpu.VMEM((2 + tiles, rows * LANES // SUBLANES, SUBLANES, LANES), jnp.float32),
-            pltpu.VMEM((tiles * levels, SUBLANES, LANES), jnp.float32),
+            pltpu.VMEM((2 + tiles, units, SUBLANES, LANES), jnp.float32),
+            pltpu.VMEM(sums_shape, jnp.float32),
         ],
         compiler_params=limit,
-    )(own, ruptures)
+    )(own, sums, ruptures)
     blocks = lax.all_to_all(copies, "rup", 0, 0, tiled=True)
     hazard = blocks[:, : tiles * levels].reshape(rows, tiles, levels, LANES)
     hazard = jnp.transpose(hazard, (2, 0, 1, 3)).reshape(levels, sites)
@@ -392,7 +428,10 @@
         out_shape=jax.ShapeDtypeStruct((bins, assets), jnp.float32),
         in_specs=[VMEM] * 5,
         out_specs=VMEM,
-        scratch_shapes=[pltpu.VMEM((sources * levels // 2, 6 * LANES), jnp.bfloat16)],
+        scratch_shapes=[
+            pltpu.VMEM((sources * levels // 2, 6 * LANES), jnp.bfloat16),
+            pltpu.VMEM((levels, assets), jnp.float32),
+        ],
         compiler_params=limit,
     )(curves, square(asset_source), slot, square(asset_class), split)
     return hazard, losses

time: 77.8 us -> 76.9 us (0.988)
  blocking collectives: 44.1 us -> 19.4 us
  starting transfers between devices: 8.27 us -> 22.3 us
  waiting for transfers between devices: 4.16 us -> 13.2 us
    all_to_all x1 -> x0, blocking collectives: 24.7 us -> none  [per_device(): lax.all_to_all(packed, ('rup', 'site'), 0, 0, axis_index_groups=groups, t...]
    all_to_all x0 -> x1, starting transfers between devices: none -> 14 us  [per_device(): lax.all_to_all(packed, ('rup', 'site'), 0, 0, axis_index_groups=groups, t...]
    all_to_all x0 -> x1, waiting for transfers between devices: none -> 9.01 us  [per_device(): lax.all_to_all(packed, ('rup', 'site'), 0, 0, axis_index_groups=groups, t...]
    pallas_call x1 -> x2, Pallas kernels: 1.52 us -> 2.42 us  [the longest x1 1.43 us: per_device(): pl.pallas_call(pack_kernel, out_shape=jax.ShapeDtypeStruct((rows, SUBLANE...]
  transfers between devices with their start and end apart: 1 -> 2, of which waited for: 1 -> 2; matrix products, arithmetic and copies ran while one was open for 2% -> 2% of each run, Pallas kernels for 1% -> 2%
where the time goes in v3:
time: 76.9 us; the launch traced here: 76.5 us
  starting transfers between devices  22.3 us (29%)
  blocking collectives  19.4 us (25%)
  Pallas kernels  17.9 us (23%)
  waiting for transfers between devices  13.2 us (17%)
  local copies, waits for them, and re-layouts  2.94 us (4%)
  between operations  0.78 us (1%)
    all_to_all x1, blocking collectives, per_device(): blocks = lax.all_to_all(copies, 'rup', 0, 0, tiled=True)  19.4 us
    all_to_all x1, starting transfers between devices, per_device(): lax.all_to_all(packed, ('rup', 'site'), 0, 0, axis_index_groups=groups, t...  14 us
    pallas_call x1, Pallas kernels, per_device(): pl.pallas_call(functools.partial(hazard_kernel, levels), out_shape=jax.Sh...  10.6 us
    all_to_all x1, waiting for transfers between devices, per_device(): lax.all_to_all(packed, ('rup', 'site'), 0, 0, axis_index_groups=groups, t...  9.01 us
    all_to_all x1, starting transfers between devices, per_device(): curves = lax.all_to_all(send, 'site', 0, 0, tiled=True)  8.29 us
    all_to_all x1, waiting for transfers between devices, per_device(): curves = lax.all_to_all(send, 'site', 0, 0, tiled=True)  4.16 us
    pallas_call x1, Pallas kernels, per_device(): pl.pallas_call(loss_kernel, out_shape=jax.ShapeDtypeStruct((bins, assets)...  2.24 us
    pallas_call x1, Pallas kernels, per_device(): pl.pallas_call(functools.partial(relay_kernel, levels), out_shape=jax.Sha...  1.93 us
  transfers between devices with their start and end apart: 2, of which 2 were waited for; matrix products, arithmetic and copies ran while one was open for 2% of the time, Pallas kernels for 2%

profile of v3, /device:TPU:1, one launch (start us, length us, event | category | flops | bytes accessed | tf_op | source)
XLA Modules:
  0.0 76.5 jit_solution(11867516434767680158)
XLA Ops:
  0.6 1.4 %shard_map.167.rup_ref = f32[16,8,128]{2,1,0:T(8,128)} custom-call(f32[1,128]{1,0:T(1,128)} %bitcast.34, f32[1,128]{1,0:T(1,128)} %bitcast.35, f32[1,128]{1,0:T(1,128)} %bitcast.36, f32[1,128]{1,0:T(1,128)} %bitcast.37, s32[1,128]{1,0:T(1,128)} %bitcast.38, s32[16,128]{1,0:T(8,128)} %bitcast.33), custom_call_target="tpu_custom_call" | custom-call | tf_op jit(solution)/shard_map/pallas_call | solution.py:356
  2.1 0.0 copy-start
  2.1 0.0 copy-start.3
  2.1 0.0 copy-start.4
  2.1 0.0 copy-start.5
  2.1 14.0 %all-to-all-start = ((f32[16,8,128]{2,1,0:T(8,128)}), f32[16,8,128]{2,1,0:T(8,128)S(1)}, u32[]{:S(2)}, u32[]{:S(2)}) async-start(f32[16,8,128]{2,1,0:T(8,128)} %shard_map.167.rup_ref), calls=%async_computation | async-start | bytes 131072 | tf_op jit(solution)/shard_map/all_to_all | solution.py:390
  16.1 0.0 copy-start.8
  16.1 0.0 copy-start.9
  16.1 0.0 copy-done
  16.2 0.0 copy-done.3
  16.2 0.0 copy-done.4
  16.2 0.0 copy-done.5
  16.2 0.6 copy-done.8
  16.8 0.0 copy-done.9
  16.8 1.0 %shard_map.168 = (f32[8,128]{1,0:T(8,128)S(1)}, f32[64,8,128]{2,1,0:T(8,128)S(1)}) custom-call(f32[16,8,128]{2,1,0:T(8,128)S(1)} %copy-done, f32[32,128]{1,0:T(8,128)S(1)} %bitcast.24, f32[32,128]{1,0:T(8,128)S(1)} %bitcast.25, f32[32,128]{1,0:T(8,128)S(1)} %bitcast.26, f32[1,64]{1,0:T(1,128)S(1)} %bitcast.29, f32[1,64]{1,0:T(1,128)S(1)} %bitcast.30), custom_call_target="tpu_custom_call" | custom-call | tf_op jit(solution)/shard_map/pallas_call | solution.py:371
  17.8 9.0 %all-to-all-done.rup_ref = f32[16,8,128]{2,1,0:T(8,128)S(1)} async-done(((f32[16,8,128]{2,1,0:T(8,128)}), f32[16,8,128]{2,1,0:T(8,128)S(1)}, u32[]{:S(2)}, u32[]{:S(2)}) %all-to-all-start) | async-done | bytes 65568 | tf_op jit(solution)/shard_map/all_to_all | solution.py:390
  26.8 10.6 %shard_map.169 = f32[16,72,128]{2,1,0:T(8,128)S(1)} custom-call(f32[8,128]{1,0:T(8,128)S(1)} %get-tuple-element.6.own_ref, f32[64,8,128]{2,1,0:T(8,128)S(1)} %get-tuple-element.7.sums_ref, f32[16,8,128]{2,1,0:T(8,128)S(1)} %all-to-all-done.rup_ref), custom_call_target="tpu_custom_call" | custom-call | tf_op jit(solution)/shard_map/pallas_call | solution.py:392
  37.4 19.4 %all_to_all.15.blocks_ref = f32[16,72,128]{2,1,0:T(8,128)S(1)} all-to-all(f32[16,72,128]{2,1,0:T(8,128)S(1)} %shard_map.169), channel_id=1, replica_groups=mesh['rup'=16,'site'=16] {'rup'}, dimensions={0} | all-to-all | bytes 1179648 | tf_op jit(solution)/shard_map/all_to_all | solution.py:403
  56.8 0.0 copy-start.1
  56.8 1.9 %shard_map.170 = f32[16,32,128]{2,1,0:T(8,128)} custom-call(f32[16,72,128]{2,1,0:T(8,128)S(1)} %all_to_all.15.blocks_ref), custom_call_target="tpu_custom_call" | custom-call | tf_op jit(solution)/shard_map/pallas_call | solution.py:406
  58.8 0.0 copy-start.2
  58.8 0.0 copy-start.6
  58.8 8.3 %all-to-all-start.2 = ((f32[16,32,128]{2,1,0:T(8,128)}), f32[16,32,128]{2,1,0:T(8,128)S(1)}, u32[]{:S(2)}, u32[]{:S(2)}) async-start(f32[16,32,128]{2,1,0:T(8,128)} %shard_map.170), calls=%async_computation.2 | async-start | bytes 524288 | tf_op jit(solution)/shard_map/all_to_all | solution.py:414
  67.0 0.0 copy-start.10
  67.0 0.0 copy-done.1
  67.1 0.0 copy-done.2
  67.1 0.0 copy-done.6
  67.1 0.6 copy-done.10
  67.7 0.7 shard_map.171
  68.4 0.4 copy.18
  68.8 0.0 copy-start.7
  68.8 1.2 %reshape.67 = f32[32,4096]{1,0:T(8,128)} reshape(f32[32,16,2,128]{3,2,1,0:T(2,128)S(1)} %copy.18) | data formatting | bytes 1048576 | tf_op jit(solution)/shard_map/reshape | solution.py:405
  70.1 4.2 %all-to-all-done.2.curves_ref = f32[16,32,128]{2,1,0:T(8,128)S(1)} async-done(((f32[16,32,128]{2,1,0:T(8,128)}), f32[16,32,128]{2,1,0:T(8,128)S(1)}, u32[]{:S(2)}, u32[]{:S(2)}) %all-to-all-start.2) | async-done | bytes 262176 | tf_op jit(solution)/shard_map/all_to_all | solution.py:414
  74.2 0.0 copy-done.7
  74.2 2.2 %shard_map.172 = f32[32,2048]{1,0:T(8,128)} custom-call(f32[16,32,128]{2,1,0:T(8,128)S(1)} %all-to-all-done.2.curves_ref, s32[16,128]{1,0:T(8,128)S(1)} %bitcast.23, s32[16,128]{1,0:T(8,128)S(1)} %get-tuple-element.8.slot_ref, s32[16,128]{1,0:T(8,128)S(1)} %bitcast.28, bf16[1024,256]{1,0:T(8,128)(2,1)S(1)} %get-tuple-element.9.split_ref), custom_call_target="tpu_custom_call" | custom-call | tf_op jit(solution)/shard_map/pallas_call | solution.py:426
  (1 shorter events, 0.0 us)
Async XLA Ops:
  2.1 14.1 %copy-start = (f32[16,8,128]{2,1,0:T(8,128)S(1)}, f32[16,8,128]{2,1,0:T(8,128)}, u32[]{:S(2)}) copy-start(f32[16,8,128]{2,1,0:T(8,128)} %shard_map.167.rup_ref) | copy-start | bytes 196612
  2.1 14.1 %copy-start.3 = (f32[4096]{0:T(1024)S(1)}, f32[4096]{0:T(1024)}, u32[]{:S(2)}) copy-start(f32[4096]{0:T(1024)} %param.16) | copy-start | bytes 49156
  2.1 14.1 %copy-start.4 = (f32[4096]{0:T(1024)S(1)}, f32[4096]{0:T(1024)}, u32[]{:S(2)}) copy-start(f32[4096]{0:T(1024)} %param.17) | copy-start | bytes 49156
  2.1 14.1 %copy-start.5 = (f32[4096]{0:T(1024)S(1)}, f32[4096]{0:T(1024)}, u32[]{:S(2)}) copy-start(f32[4096]{0:T(1024)} %param.18) | copy-start | bytes 49156
  2.1 24.7 %all-to-all-start = ((f32[16,8,128]{2,1,0:T(8,128)}), f32[16,8,128]{2,1,0:T(8,128)S(1)}, u32[]{:S(2)}, u32[]{:S(2)}) async-start(f32[16,8,128]{2,1,0:T(8,128)} %shard_map.167.rup_ref), calls=%async_computation | async-start | bytes 131072 | tf_op jit(solution)/shard_map/all_to_all | solution.py:390
  16.1 0.7 copy-start.8
  16.1 0.7 copy-start.9
  56.8 10.2 %copy-start.1 = (f32[128,32,32]{0,2,1:T(8,128)S(1)}, f32[128,32,32]{0,2,1:T(8,128)}, u32[]{:S(2)}) copy-start(f32[128,32,32]{0,2,1:T(8,128)} %param.31) | copy-start | bytes 1572868
  58.8 8.3 %copy-start.2 = (s32[2048]{0:T(1024)S(1)}, s32[2048]{0:T(1024)}, u32[]{:S(2)}) copy-start(s32[2048]{0:T(1024)} %param.28) | copy-start | bytes 24580
  58.8 8.3 %copy-start.6 = (s32[2048]{0:T(1024)S(1)}, s32[2048]{0:T(1024)}, u32[]{:S(2)}) copy-start(s32[2048]{0:T(1024)} %param.29) | copy-start | bytes 24580
  58.8 15.5 %all-to-all-start.2 = ((f32[16,32,128]{2,1,0:T(8,128)}), f32[16,32,128]{2,1,0:T(8,128)S(1)}, u32[]{:S(2)}, u32[]{:S(2)}) async-start(f32[16,32,128]{2,1,0:T(8,128)} %shard_map.170), calls=%async_computation.2 | async-start | bytes 524288 | tf_op jit(solution)/shard_map/all_to_all | solution.py:414
  67.0 0.7 copy-start.10
  68.8 5.4 %copy-start.7 = (s32[2048]{0:T(1024)S(1)}, s32[2048]{0:T(1024)}, u32[]{:S(2)}) copy-start(s32[2048]{0:T(1024)} %param.30) | copy-start | bytes 24580

commit v4 on v3

--- a/solution.py
+++ b/solution.py
@@ -134,9 +134,11 @@
             acc_ref[t * levels + l] = sums[l]
 
 
-def hazard_kernel(levels, own_ref, sums_ref, rup_ref, out_ref, pre_ref, acc_ref):
+def hazard_kernel(levels, own_ref, sums_ref, rup_ref, *refs):
+    out_refs, pre_ref, acc_ref = refs[:-2], refs[-2], refs[-1]
     blocks = rup_ref.shape[0]
-    tiles = out_ref.shape[1] // levels
+    heights = len(out_refs)
+    tiles = out_refs[0].shape[0] // levels
     units = LANES // SUBLANES
     row = place()[0]
     spread_out = spreading()
@@ -174,12 +176,29 @@
                 axis=0,
             )
             hazard = 1.0 - jnp.exp(-rates)
-            for b in range(blocks):
-                out_ref[b, t * levels + q : t * levels + q + SUBLANES, :] = hazard
-    for b in range(blocks):
-        out_ref[b, tiles * levels : tiles * levels + SUBLANES, :] = wide(
-            rup_ref[b, LIST : LIST + 1, :]
-        )
+            for out_ref in out_refs:
+                out_ref[t * levels + q : t * levels + q + SUBLANES, :] = hazard
+    for k, out_ref in enumerate(out_refs):
+        height = (row + k) & (heights - 1)
+        lists = [rup_ref[x * heights + height, LIST : LIST + 1, :] for x in range(blocks // heights)]
+        lists.append(jnp.zeros((SUBLANES - len(lists), LANES), jnp.float32))
+        out_ref[tiles * levels :, :] = jnp.concatenate(lists, axis=0)
+
+
+def merge_kernel(*refs):
+    in_refs, out_ref = refs[:-1], refs[-1]
+    heights = len(in_refs)
+    length = in_refs[0].shape[0] - SUBLANES
+    row = place()[0]
+    for x in range(out_ref.shape[0]):
+        out_ref[x, heights * length :, :] = jnp.zeros((SUBLANES, LANES), jnp.float32)
+        for k, in_ref in enumerate(in_refs):
+            height = (row - k) & (heights - 1)
+            at = pl.multiple_of(height * length, length)
+            out_ref[x, pl.ds(at, length), :] = in_ref[0:length, :]
+            out_ref[x, pl.ds(heights * length + height, 1), :] = in_ref[
+                length + x : length + x + 1, :
+            ]
 
 
 def pick_by_product(lhs_ref, levels, index):
@@ -204,23 +223,32 @@
     return picked
 
 
-def relay_kernel(levels, blocks_ref, send_ref, lhs_ref):
-    blocks, rows, _ = blocks_ref.shape
+def relay_kernel(levels, span, blocks_ref, send_ref, lhs_ref):
+    parts, rows, _ = blocks_ref.shape
+    heights = (rows - SUBLANES) * LANES // (levels * span)
+    blocks = parts * heights
     groups = levels // SUBLANES
-    tiles = rows // levels
-    lists = tiles * levels
+    tiles = span // LANES
     row, site = place()
-    span = tiles * LANES
+
+    def piece(b, t, first, count):
+        at = ((b % heights) * tiles + t) * levels + first
+        return blocks_ref[b // heights, at : at + count, :]
+
+    def wanted(k):
+        at = heights * tiles * levels + k % heights
+        return blocks_ref[k // heights, at : at + 1, :].astype(jnp.int32)
+
     for b in range(blocks):
         for t in range(tiles):
-            thirds = split_in_three(blocks_ref[b, t * levels : (t + 1) * levels, :])
+            thirds = split_in_three(piece(b, t, 0, levels))
             for i in range(3):
                 at = i * span + t * LANES
                 lhs_ref[b * levels : (b + 1) * levels, at : at + LANES] = thirds[i]
 
     def by_product(k):
-        index = jnp.concatenate([blocks_ref[k + i, lists : lists + 1, :] for i in range(2)], axis=1)
-        picked = pick_by_product(lhs_ref, levels, index.astype(jnp.int32))
+        index = jnp.concatenate([wanted(k + i) for i in range(2)], axis=1)
+        picked = pick_by_product(lhs_ref, levels, index)
         for i in range(2):
             owner = partner(k + i, site, row)
             for q in range(groups):
@@ -229,7 +257,7 @@
                 ]
 
     def by_gather(k):
-        index = blocks_ref[k, lists : lists + SUBLANES, :].astype(jnp.int32)
+        index = wide(wanted(k))
         lane = index & (LANES - 1)
         tile = index >> 7
         picked = [jnp.zeros((SUBLANES, LANES), jnp.float32)] * groups
@@ -237,10 +265,8 @@
             b, t = c // tiles, c % tiles
             here = tile == c
             for q in range(groups):
-                at = t * levels + q * SUBLANES
-                picked[q] = jnp.where(
-                    here, lane_gather(blocks_ref[b, at : at + SUBLANES, :], lane), picked[q]
-                )
+                part = piece(b, t, q * SUBLANES, SUBLANES)
+                picked[q] = jnp.where(here, lane_gather(part, lane), picked[q])
         owner = partner(k, site, row)
         for q in range(groups):
             send_ref[owner, q * SUBLANES : (q + 1) * SUBLANES, :] = picked[q]
@@ -388,23 +414,41 @@
     )
     groups = [[j * columns + partner(0, d, j) for j in range(rows)] for d in range(columns)]
     ruptures = lax.all_to_all(packed, ("rup", "site"), 0, 0, axis_index_groups=groups, tiled=True)
-    height = tiles * levels + SUBLANES
+    heights = 4
+    length = tiles * levels
+    copy = jax.ShapeDtypeStruct((length + SUBLANES, LANES), jnp.float32)
     copies = pl.pallas_call(
         functools.partial(hazard_kernel, levels),
-        out_shape=jax.ShapeDtypeStruct((rows, height, LANES), jnp.float32),
+        out_shape=(copy,) * heights,
         in_specs=[VMEM] * 3,
-        out_specs=VMEM,
+        out_specs=(VMEM,) * heights,
         scratch_shapes=[
             pltpu.VMEM((2 + tiles, units, SUBLANES, LANES), jnp.float32),
             pltpu.VMEM(sums_shape, jnp.float32),
         ],
         compiler_params=limit,
     )(own, sums, ruptures)
-    blocks = lax.all_to_all(copies, "rup", 0, 0, tiled=True)
-    hazard = blocks[:, : tiles * levels].reshape(rows, tiles, levels, LANES)
-    hazard = jnp.transpose(hazard, (2, 0, 1, 3)).reshape(levels, sites)
+    along = lambda k: [(r, r // heights * heights + (r + k) % heights) for r in range(rows)]
+    far_first = sorted(range(1, heights), key=lambda k: -min(k, heights - k))
+    moved = {k: lax.ppermute(copies[k], "rup", along(k)) for k in far_first}
+    east = rows // heights
+    merged = pl.pallas_call(
+        merge_kernel,
+        out_shape=jax.ShapeDtypeStruct((east, heights * length + SUBLANES, LANES), jnp.float32),
+        in_specs=[VMEM] * heights,
+        out_specs=VMEM,
+        compiler_params=limit,
+    )(copies[0], *[moved[k] for k in range(1, heights)])
+    lines = [
+        [(x * heights + height) * columns + d for x in range(east)]
+        for height in range(heights)
+        for d in range(columns)
+    ]
+    blocks = lax.all_to_all(merged, ("rup", "site"), 0, 0, axis_index_groups=lines, tiled=True)
+    hazard = blocks[:, : heights * length].reshape(rows * tiles, levels, LANES)
+    hazard = jnp.transpose(hazard, (1, 0, 2)).reshape(levels, sites)
     send = pl.pallas_call(
-        functools.partial(relay_kernel, levels),
+        functools.partial(relay_kernel, levels, own_sites),
         out_shape=jax.ShapeDtypeStruct((columns, levels, capacity), jnp.float32),
         in_specs=[VMEM],
         out_specs=VMEM,

time: 76.9 us -> 74.3 us (0.966)
  blocking collectives: 19.4 us -> 10.8 us
  waiting for transfers between devices: 13.2 us -> 17.8 us
  starting transfers between devices: 22.3 us -> 24.4 us
  local copies, waits for them, and re-layouts: 2.94 us -> 2.14 us
    all_to_all x1, blocking collectives: 19.4 us -> 10.8 us  [per_device(): lax.all_to_all(merged, ('rup', 'site'), 0, 0, axis_index_groups=lines, ti...]
    ppermute x0 -> x3, waiting for transfers between devices: none -> 3.73 us  [per_device(): moved = {k: lax.ppermute(copies[k], 'rup', along(k)) for k in far_first}]
    ppermute x0 -> x3, starting transfers between devices: none -> 3.65 us  [per_device(): moved = {k: lax.ppermute(copies[k], 'rup', along(k)) for k in far_first}]
    all_to_all x1, starting transfers between devices: 8.29 us -> 6.74 us  [per_device(): curves = lax.all_to_all(send, 'site', 0, 0, tiled=True)]
    all_to_all x1, waiting for transfers between devices: 4.16 us -> 5.03 us  [per_device(): curves = lax.all_to_all(send, 'site', 0, 0, tiled=True)]
    pallas_call x2 -> x3, Pallas kernels: 12.6 us -> 12.6 us  [the longest x1 10.6 us: per_device(): pl.pallas_call(functools.partial(hazard_kernel, levels), out_shape=(copy,...]
  transfers between devices with their start and end apart: 2 -> 5, of which waited for: 2 -> 5; matrix products, arithmetic and copies ran while one was open for 2% -> 1% of each run, Pallas kernels for 2% -> 2%
where the time goes in v4:
time: 74.3 us; the launch traced here: 73.8 us
  starting transfers between devices  24.4 us (33%)
  Pallas kernels  17.9 us (24%)
  waiting for transfers between devices  17.8 us (24%)
  blocking collectives  10.8 us (15%)
  local copies, waits for them, and re-layouts  2.14 us (3%)
  between operations  0.79 us (1%)
    all_to_all x1, starting transfers between devices, per_device(): lax.all_to_all(packed, ('rup', 'site'), 0, 0, axis_index_groups=groups, t...  14 us
    all_to_all x1, blocking collectives, per_device(): lax.all_to_all(merged, ('rup', 'site'), 0, 0, axis_index_groups=lines, ti...  10.8 us
    pallas_call x1, Pallas kernels, per_device(): pl.pallas_call(functools.partial(hazard_kernel, levels), out_shape=(copy,...  10.6 us
    all_to_all x1, waiting for transfers between devices, per_device(): lax.all_to_all(packed, ('rup', 'site'), 0, 0, axis_index_groups=groups, t...  9.01 us
    all_to_all x1, starting transfers between devices, per_device(): curves = lax.all_to_all(send, 'site', 0, 0, tiled=True)  6.74 us
    all_to_all x1, waiting for transfers between devices, per_device(): curves = lax.all_to_all(send, 'site', 0, 0, tiled=True)  5.03 us
    ppermute x3, waiting for transfers between devices, per_device(): moved = {k: lax.ppermute(copies[k], 'rup', along(k)) for k in far_first}  3.73 us
    ppermute x3, starting transfers between devices, per_device(): moved = {k: lax.ppermute(copies[k], 'rup', along(k)) for k in far_first}  3.65 us
  transfers between devices with their start and end apart: 5, of which 5 were waited for; matrix products, arithmetic and copies ran while one was open for 1% of the time, Pallas kernels for 2%

profile of v4, /device:TPU:1, one launch (start us, length us, event | category | flops | bytes accessed | tf_op | source)
XLA Modules:
  0.0 73.8 jit_solution(9573824041194251739)
XLA Ops:
  0.6 1.4 %shard_map.167.rup_ref = f32[16,8,128]{2,1,0:T(8,128)} custom-call(f32[1,128]{1,0:T(1,128)} %bitcast.39, f32[1,128]{1,0:T(1,128)} %bitcast.40, f32[1,128]{1,0:T(1,128)} %bitcast.41, f32[1,128]{1,0:T(1,128)} %bitcast.42, s32[1,128]{1,0:T(1,128)} %bitcast.43, s32[16,128]{1,0:T(8,128)} %bitcast.38), custom_call_target="tpu_custom_call" | custom-call | tf_op jit(solution)/shard_map/pallas_call | solution.py:382
  2.1 0.0 copy-start
  2.1 0.0 copy-start.3
  2.1 0.0 copy-start.4
  2.1 0.0 copy-start.5
  2.1 14.0 %all-to-all-start = ((f32[16,8,128]{2,1,0:T(8,128)}), f32[16,8,128]{2,1,0:T(8,128)S(1)}, u32[]{:S(2)}, u32[]{:S(2)}) async-start(f32[16,8,128]{2,1,0:T(8,128)} %shard_map.167.rup_ref), calls=%async_computation | async-start | bytes 131072 | tf_op jit(solution)/shard_map/all_to_all | solution.py:416
  16.1 0.0 copy-start.8
  16.1 0.0 copy-start.9
  16.1 0.0 copy-done
  16.2 0.0 copy-done.3
  16.2 0.0 copy-done.4
  16.2 0.0 copy-done.5
  16.2 0.6 copy-done.8
  16.8 0.0 copy-done.9
  16.8 1.0 %shard_map.168 = (f32[8,128]{1,0:T(8,128)S(1)}, f32[64,8,128]{2,1,0:T(8,128)S(1)}) custom-call(f32[16,8,128]{2,1,0:T(8,128)S(1)} %copy-done, f32[32,128]{1,0:T(8,128)S(1)} %bitcast.28, f32[32,128]{1,0:T(8,128)S(1)} %bitcast.29, f32[32,128]{1,0:T(8,128)S(1)} %bitcast.30, f32[1,64]{1,0:T(1,128)S(1)} %bitcast.33, f32[1,64]{1,0:T(1,128)S(1)} %bitcast.34), custom_call_target="tpu_custom_call" | custom-call | tf_op jit(solution)/shard_map/pallas_call | solution.py:397
  17.8 9.0 %all-to-all-done.rup_ref = f32[16,8,128]{2,1,0:T(8,128)S(1)} async-done(((f32[16,8,128]{2,1,0:T(8,128)}), f32[16,8,128]{2,1,0:T(8,128)S(1)}, u32[]{:S(2)}, u32[]{:S(2)}) %all-to-all-start) | async-done | bytes 65568 | tf_op jit(solution)/shard_map/all_to_all | solution.py:416
  26.8 10.6 %shard_map.169 = (f32[72,128]{1,0:T(8,128)S(1)}, f32[72,128]{1,0:T(8,128)S(1)}, f32[72,128]{1,0:T(8,128)S(1)}, f32[72,128]{1,0:T(8,128)S(1)}) custom-call(f32[8,128]{1,0:T(8,128)S(1)} %get-tuple-element.10.own_ref, f32[64,8,128]{2,1,0:T(8,128)S(1)} %get-tuple-element.11.sums_ref, f32[16,8,128]{2,1,0:T(8,128)S(1)} %all-to-all-done.rup_ref), custom_call_target="tpu_custom_call" | custom-call | tf_op jit(solution)/shard_map/pallas_call | solution.py:420
  37.4 0.1 collective-permute-start
  37.5 2.7 %collective-permute-start.1 = (f32[72,128]{1,0:T(8,128)S(1)}, f32[72,128]{1,0:T(8,128)S(1)}, u32[]{:S(2)}, u32[]{:S(2)}) collective-permute-start(f32[72,128]{1,0:T(8,128)S(1)} %get-tuple-element.14), channel_id=1, source_target_pairs={{0,32},{16,48},{32,0},{48,16},{64,96},{80,112},{96,64},{112,80},{1... | collective-permute-start | bytes 110600 | tf_op jit(solution)/shard_map/ppermute | solution.py:433
  40.2 0.8 %collective-permute-start.2 = (f32[72,128]{1,0:T(8,128)S(1)}, f32[72,128]{1,0:T(8,128)S(1)}, u32[]{:S(2)}, u32[]{:S(2)}) collective-permute-start(f32[72,128]{1,0:T(8,128)S(1)} %get-tuple-element.15), channel_id=1, source_target_pairs={{0,48},{16,0},{32,16},{48,32},{64,112},{80,64},{96,80},{112,96},{1... | collective-permute-start | bytes 110600 | tf_op jit(solution)/shard_map/ppermute | solution.py:433
  41.1 1.7 %collective-permute-done.refs_1_ = f32[72,128]{1,0:T(8,128)S(1)} collective-permute-done((f32[72,128]{1,0:T(8,128)S(1)}, f32[72,128]{1,0:T(8,128)S(1)}, u32[]{:S(2)}, u32[]{:S(2)}) %collective-permute-start) | collective-permute-done | bytes 36896 | tf_op jit(solution)/shard_map/ppermute | solution.py:433
  42.8 1.9 %collective-permute-done.1.refs_2_ = f32[72,128]{1,0:T(8,128)S(1)} collective-permute-done((f32[72,128]{1,0:T(8,128)S(1)}, f32[72,128]{1,0:T(8,128)S(1)}, u32[]{:S(2)}, u32[]{:S(2)}) %collective-permute-start.1) | collective-permute-done | bytes 36896 | tf_op jit(solution)/shard_map/ppermute | solution.py:433
  44.7 0.1 collective-permute-done.2.refs_3_
  44.9 10.8 %all_to_all.15.blocks_ref = f32[4,264,128]{2,1,0:T(8,128)S(1)} all-to-all(f32[4,264,128]{2,1,0:T(8,128)S(1)} %shard_map.170), channel_id=1, replica_groups={{0,64,128,192},{1,65,129,193},{2,66,130,194},{3,67,131,195},{4,68,132,1..., dimensions={0} | all-to-all | bytes 1081344 | tf_op jit(solution)/shard_map/all_to_all | solution.py:447
  55.7 0.0 copy-start.1
  55.7 1.9 %shard_map.171 = f32[16,32,128]{2,1,0:T(8,128)} custom-call(f32[4,264,128]{2,1,0:T(8,128)S(1)} %all_to_all.15.blocks_ref), custom_call_target="tpu_custom_call" | custom-call | tf_op jit(solution)/shard_map/pallas_call | solution.py:450
  57.6 0.0 copy-start.2
  57.6 0.0 copy-start.6
  57.6 6.7 %all-to-all-start.2 = ((f32[16,32,128]{2,1,0:T(8,128)}), f32[16,32,128]{2,1,0:T(8,128)S(1)}, u32[]{:S(2)}, u32[]{:S(2)}) async-start(f32[16,32,128]{2,1,0:T(8,128)} %shard_map.171), calls=%async_computation.2 | async-start | bytes 524288 | tf_op jit(solution)/shard_map/all_to_all | solution.py:458
  64.4 0.0 copy-start.10
  64.4 0.0 copy-done.1
  64.4 0.0 copy-done.2
  64.4 0.0 copy-done.6
  64.4 0.6 copy-done.10
  65.0 0.7 shard_map.172
  65.7 0.0 copy-start.7
  65.7 0.8 %copy.21 = f32[32,4,8,128]{3,2,0,1:T(8,128)} copy(f32[32,4,8,128]{3,2,1,0:T(8,128)S(1)} %bitcast.36) | data formatting | bytes 1048576 | tf_op jit(solution)/shard_map/reshape | solution.py:449
  66.6 5.0 %all-to-all-done.2.curves_ref = f32[16,32,128]{2,1,0:T(8,128)S(1)} async-done(((f32[16,32,128]{2,1,0:T(8,128)}), f32[16,32,128]{2,1,0:T(8,128)S(1)}, u32[]{:S(2)}, u32[]{:S(2)}) %all-to-all-start.2) | async-done | bytes 262176 | tf_op jit(solution)/shard_map/all_to_all | solution.py:458
  71.6 0.0 copy-done.7
  71.6 2.2 %shard_map.173 = f32[32,2048]{1,0:T(8,128)} custom-call(f32[16,32,128]{2,1,0:T(8,128)S(1)} %all-to-all-done.2.curves_ref, s32[16,128]{1,0:T(8,128)S(1)} %bitcast.27, s32[16,128]{1,0:T(8,128)S(1)} %get-tuple-element.16.slot_ref, s32[16,128]{1,0:T(8,128)S(1)} %bitcast.32, bf16[1024,256]{1,0:T(8,128)(2,1)S(1)} %get-tuple-element.17.split_ref), custom_call_target="tpu_custom_call" | custom-call | tf_op jit(solution)/shard_map/pallas_call | solution.py:470
  (2 shorter events, 0.1 us)
Async XLA Ops:
  2.1 14.1 %copy-start = (f32[16,8,128]{2,1,0:T(8,128)S(1)}, f32[16,8,128]{2,1,0:T(8,128)}, u32[]{:S(2)}) copy-start(f32[16,8,128]{2,1,0:T(8,128)} %shard_map.167.rup_ref) | copy-start | bytes 196612
  2.1 14.1 %copy-start.3 = (f32[4096]{0:T(1024)S(1)}, f32[4096]{0:T(1024)}, u32[]{:S(2)}) copy-start(f32[4096]{0:T(1024)} %param.16) | copy-start | bytes 49156
  2.1 14.1 %copy-start.4 = (f32[4096]{0:T(1024)S(1)}, f32[4096]{0:T(1024)}, u32[]{:S(2)}) copy-start(f32[4096]{0:T(1024)} %param.17) | copy-start | bytes 49156
  2.1 14.1 %copy-start.5 = (f32[4096]{0:T(1024)S(1)}, f32[4096]{0:T(1024)}, u32[]{:S(2)}) copy-start(f32[4096]{0:T(1024)} %param.18) | copy-start | bytes 49156
  2.1 24.7 %all-to-all-start = ((f32[16,8,128]{2,1,0:T(8,128)}), f32[16,8,128]{2,1,0:T(8,128)S(1)}, u32[]{:S(2)}, u32[]{:S(2)}) async-start(f32[16,8,128]{2,1,0:T(8,128)} %shard_map.167.rup_ref), calls=%async_computation | async-start | bytes 131072 | tf_op jit(solution)/shard_map/all_to_all | solution.py:416
  16.1 0.7 copy-start.8
  16.1 0.7 copy-start.9
  37.4 5.4 %collective-permute-start = (f32[72,128]{1,0:T(8,128)S(1)}, f32[72,128]{1,0:T(8,128)S(1)}, u32[]{:S(2)}, u32[]{:S(2)}) collective-permute-start(f32[72,128]{1,0:T(8,128)S(1)} %get-tuple-element.13), channel_id=1, source_target_pairs={{0,16},{16,32},{32,48},{48,0},{64,80},{80,96},{96,112},{112,64},{1... | collective-permute-start | bytes 110600 | tf_op jit(solution)/shard_map/ppermute | solution.py:433
  37.5 7.2 %collective-permute-start.1 = (f32[72,128]{1,0:T(8,128)S(1)}, f32[72,128]{1,0:T(8,128)S(1)}, u32[]{:S(2)}, u32[]{:S(2)}) collective-permute-start(f32[72,128]{1,0:T(8,128)S(1)} %get-tuple-element.14), channel_id=1, source_target_pairs={{0,32},{16,48},{32,0},{48,16},{64,96},{80,112},{96,64},{112,80},{1... | collective-permute-start | bytes 110600 | tf_op jit(solution)/shard_map/ppermute | solution.py:433
  40.2 4.6 %collective-permute-start.2 = (f32[72,128]{1,0:T(8,128)S(1)}, f32[72,128]{1,0:T(8,128)S(1)}, u32[]{:S(2)}, u32[]{:S(2)}) collective-permute-start(f32[72,128]{1,0:T(8,128)S(1)} %get-tuple-element.15), channel_id=1, source_target_pairs={{0,48},{16,0},{32,16},{48,32},{64,112},{80,64},{96,80},{112,96},{1... | collective-permute-start | bytes 110600 | tf_op jit(solution)/shard_map/ppermute | solution.py:433
  55.7 8.7 %copy-start.1 = (f32[128,32,32]{0,2,1:T(8,128)S(1)}, f32[128,32,32]{0,2,1:T(8,128)}, u32[]{:S(2)}) copy-start(f32[128,32,32]{0,2,1:T(8,128)} %param.31) | copy-start | bytes 1572868
  57.6 6.8 %copy-start.2 = (s32[2048]{0:T(1024)S(1)}, s32[2048]{0:T(1024)}, u32[]{:S(2)}) copy-start(s32[2048]{0:T(1024)} %param.28) | copy-start | bytes 24580
  57.6 6.8 %copy-start.6 = (s32[2048]{0:T(1024)S(1)}, s32[2048]{0:T(1024)}, u32[]{:S(2)}) copy-start(s32[2048]{0:T(1024)} %param.29) | copy-start | bytes 24580
  57.6 14.0 %all-to-all-start.2 = ((f32[16,32,128]{2,1,0:T(8,128)}), f32[16,32,128]{2,1,0:T(8,128)S(1)}, u32[]{:S(2)}, u32[]{:S(2)}) async-start(f32[16,32,128]{2,1,0:T(8,128)} %shard_map.171), calls=%async_computation.2 | async-start | bytes 524288 | tf_op jit(solution)/shard_map/all_to_all | solution.py:458
  64.4 0.7 copy-start.10
  65.7 5.9 %copy-start.7 = (s32[2048]{0:T(1024)S(1)}, s32[2048]{0:T(1024)}, u32[]{:S(2)}) copy-start(s32[2048]{0:T(1024)} %param.30) | copy-start | bytes 24580

commit v5 on v4

--- a/solution.py
+++ b/solution.py
@@ -179,26 +179,35 @@
             for out_ref in out_refs:
                 out_ref[t * levels + q : t * levels + q + SUBLANES, :] = hazard
     for k, out_ref in enumerate(out_refs):
-        height = (row + k) & (heights - 1)
+        height = (row & (heights - 1)) ^ k
         lists = [rup_ref[x * heights + height, LIST : LIST + 1, :] for x in range(blocks // heights)]
         lists.append(jnp.zeros((SUBLANES - len(lists), LANES), jnp.float32))
         out_ref[tiles * levels :, :] = jnp.concatenate(lists, axis=0)
 
 
-def merge_kernel(*refs):
-    in_refs, out_ref = refs[:-1], refs[-1]
-    heights = len(in_refs)
+def merge_kernel(heights, *refs):
+    in_refs, out_refs = refs[:heights], refs[heights:]
     length = in_refs[0].shape[0] - SUBLANES
     row = place()[0]
-    for x in range(out_ref.shape[0]):
-        out_ref[x, heights * length :, :] = jnp.zeros((SUBLANES, LANES), jnp.float32)
-        for k, in_ref in enumerate(in_refs):
-            height = (row - k) & (heights - 1)
+    for k, out_ref in enumerate(out_refs):
+        x = ((row >> 2) + k) & (len(out_refs) - 1)
+        out_ref[heights * length :, :] = jnp.zeros((SUBLANES, LANES), jnp.float32)
+        for flip, in_ref in enumerate(in_refs):
+            height = (row & (heights - 1)) ^ flip
             at = pl.multiple_of(height * length, length)
-            out_ref[x, pl.ds(at, length), :] = in_ref[0:length, :]
-            out_ref[x, pl.ds(heights * length + height, 1), :] = in_ref[
-                length + x : length + x + 1, :
-            ]
+            out_ref[pl.ds(at, length), :] = in_ref[0:length, :]
+            out_ref[pl.ds(heights * length + height, 1), :] = in_ref[pl.ds(length + x, 1), :]
+
+
+def output_kernel(levels, *refs):
+    in_refs, out_ref = refs[:-1], refs[-1]
+    row = place()[0]
+    tiles = out_ref.shape[1] // (len(in_refs) * LANES)
+    for k, in_ref in enumerate(in_refs):
+        x = ((row >> 2) - k) & (len(in_refs) - 1)
+        for t in range(tiles):
+            at = pl.multiple_of((x * tiles + t) * LANES, LANES)
+            out_ref[:, pl.ds(at, LANES)] = in_ref[t * levels : (t + 1) * levels, :]
 
 
 def pick_by_product(lhs_ref, levels, index):
@@ -223,34 +232,39 @@
     return picked
 
 
-def relay_kernel(levels, span, blocks_ref, send_ref, lhs_ref):
-    parts, rows, _ = blocks_ref.shape
-    heights = (rows - SUBLANES) * LANES // (levels * span)
+def relay_kernel(levels, span, *refs):
+    part_refs, send_ref, lhs_ref = refs[:-2], refs[-2], refs[-1]
+    parts = len(part_refs)
+    heights = (part_refs[0].shape[0] - SUBLANES) * LANES // (levels * span)
     blocks = parts * heights
     groups = levels // SUBLANES
     tiles = span // LANES
     row, site = place()
 
+    def origin(b):
+        return (((row >> 2) - b // heights) & (parts - 1)) * heights + b % heights
+
     def piece(b, t, first, count):
-        at = ((b % heights) * tiles + t) * levels + first
-        return blocks_ref[b // heights, at : at + count, :]
+        at = (b % heights * tiles + t) * levels + first
+        return part_refs[b // heights][at : at + count, :]
 
     def wanted(k):
         at = heights * tiles * levels + k % heights
-        return blocks_ref[k // heights, at : at + 1, :].astype(jnp.int32)
+        return part_refs[k // heights][at : at + 1, :].astype(jnp.int32)
 
     for b in range(blocks):
         for t in range(tiles):
             thirds = split_in_three(piece(b, t, 0, levels))
             for i in range(3):
                 at = i * span + t * LANES
-                lhs_ref[b * levels : (b + 1) * levels, at : at + LANES] = thirds[i]
+                first = pl.multiple_of(origin(b) * levels, levels)
+                lhs_ref[pl.ds(first, levels), at : at + LANES] = thirds[i]
 
     def by_product(k):
         index = jnp.concatenate([wanted(k + i) for i in range(2)], axis=1)
         picked = pick_by_product(lhs_ref, levels, index)
         for i in range(2):
-            owner = partner(k + i, site, row)
+            owner = partner(origin(k + i), site, row)
             for q in range(groups):
                 send_ref[owner, q * SUBLANES : (q + 1) * SUBLANES, :] = picked[q][
                     :, i * LANES : (i + 1) * LANES
@@ -263,11 +277,11 @@
         picked = [jnp.zeros((SUBLANES, LANES), jnp.float32)] * groups
         for c in range(blocks * tiles):
             b, t = c // tiles, c % tiles
-            here = tile == c
+            here = tile == origin(b) * tiles + t
             for q in range(groups):
                 part = piece(b, t, q * SUBLANES, SUBLANES)
                 picked[q] = jnp.where(here, lane_gather(part, lane), picked[q])
-        owner = partner(k, site, row)
+        owner = partner(origin(k), site, row)
         for q in range(groups):
             send_ref[owner, q * SUBLANES : (q + 1) * SUBLANES, :] = picked[q]
 
@@ -428,33 +442,34 @@
         ],
         compiler_params=limit,
     )(own, sums, ruptures)
-    along = lambda k: [(r, r // heights * heights + (r + k) % heights) for r in range(rows)]
-    far_first = sorted(range(1, heights), key=lambda k: -min(k, heights - k))
-    moved = {k: lax.ppermute(copies[k], "rup", along(k)) for k in far_first}
+    swap = lambda k: lax.ppermute(copies[k], "rup", [(r, r ^ k) for r in range(rows)])
     east = rows // heights
     merged = pl.pallas_call(
-        merge_kernel,
-        out_shape=jax.ShapeDtypeStruct((east, heights * length + SUBLANES, LANES), jnp.float32),
+        functools.partial(merge_kernel, heights),
+        out_shape=(jax.ShapeDtypeStruct((heights * length + SUBLANES, LANES), jnp.float32),) * east,
         in_specs=[VMEM] * heights,
+        out_specs=(VMEM,) * east,
+        compiler_params=limit,
+    )(copies[0], *[swap(k) for k in range(1, heights)])
+    shift = lambda k: lax.ppermute(
+        merged[k], "rup", [(r, (r + k * heights) % rows) for r in range(rows)]
+    )
+    parts = [merged[0]] + [shift(k) for k in range(1, east)]
+    hazard = pl.pallas_call(
+        functools.partial(output_kernel, levels),
+        out_shape=jax.ShapeDtypeStruct((levels, sites), jnp.float32),
+        in_specs=[VMEM] * east,
         out_specs=VMEM,
         compiler_params=limit,
-    )(copies[0], *[moved[k] for k in range(1, heights)])
-    lines = [
-        [(x * heights + height) * columns + d for x in range(east)]
-        for height in range(heights)
-        for d in range(columns)
-    ]
-    blocks = lax.all_to_all(merged, ("rup", "site"), 0, 0, axis_index_groups=lines, tiled=True)
-    hazard = blocks[:, : heights * length].reshape(rows * tiles, levels, LANES)
-    hazard = jnp.transpose(hazard, (1, 0, 2)).reshape(levels, sites)
+    )(*parts)
     send = pl.pallas_call(
         functools.partial(relay_kernel, levels, own_sites),
         out_shape=jax.ShapeDtypeStruct((columns, levels, capacity), jnp.float32),
-        in_specs=[VMEM],
+        in_specs=[VMEM] * east,
         out_specs=VMEM,
         scratch_shapes=[pltpu.VMEM((rows * levels, 3 * own_sites), jnp.bfloat16)],
         compiler_params=limit,
-    )(blocks)
+    )(*parts)
     curves = lax.all_to_all(send, "site", 0, 0, tiled=True)
     table = jnp.transpose(vulnerability, (1, 2, 0)).reshape(levels * bins, classes)
     slot, split = pl.pallas_call(

time: 74.3 us -> 72.8 us (0.980)
  blocking collectives: 10.8 us -> 0 us
  waiting for transfers between devices: 17.8 us -> 22.4 us
  starting transfers between devices: 24.4 us -> 28.9 us
  Pallas kernels: 17.9 us -> 19 us
  local copies, waits for them, and re-layouts: 2.14 us -> 1.27 us
    all_to_all x1 -> x0, blocking collectives: 10.8 us -> none  [per_device(): lax.all_to_all(merged, ('rup', 'site'), 0, 0, axis_index_groups=lines, ti...]
    ppermute x3 -> x6, starting transfers between devices: 3.65 us -> 8.7 us  [the longest x3 5.74 us: per_device(): lax.ppermute(copies[k], 'rup', [(r, r ^ k) for r in range(rows)])]
    ppermute x3 -> x6, waiting for transfers between devices: 3.73 us -> 8.43 us  [the longest x3 5.59 us: per_device(): lax.ppermute(merged[k], 'rup', [(r, (r + k * heights) % rows) for r in ra...]
    pallas_call x1 -> x2, Pallas kernels: 0.05 us -> 0.89 us  [the longest x1 0.84 us: per_device(): pl.pallas_call(functools.partial(output_kernel, levels), out_shape=jax.Sh...]
    reshape x1 -> x0, local copies, waits for them, and re-layouts: 0.83 us -> none  [per_device(): hazard = jnp.transpose(hazard, (1, 0, 2)).reshape(levels, sites)]
  transfers between devices with their start and end apart: 5 -> 8, of which waited for: 5 -> 6; matrix products, arithmetic and copies ran while one was open for 1% -> 0% of each run, Pallas kernels for 2% -> 3%
where the time goes in v5:
time: 72.8 us; the launch traced here: 72.4 us
  starting transfers between devices  28.9 us (40%)
  waiting for transfers between devices  22.4 us (31%)
  Pallas kernels  19 us (26%)
  local copies, waits for them, and re-layouts  1.27 us (2%)
  between operations  0.79 us (1%)
    all_to_all x1, starting transfers between devices, per_device(): lax.all_to_all(packed, ('rup', 'site'), 0, 0, axis_index_groups=groups, t...  14 us
    pallas_call x1, Pallas kernels, per_device(): pl.pallas_call(functools.partial(hazard_kernel, levels), out_shape=(copy,...  10.6 us
    all_to_all x1, waiting for transfers between devices, per_device(): lax.all_to_all(packed, ('rup', 'site'), 0, 0, axis_index_groups=groups, t...  9.01 us
    all_to_all x1, starting transfers between devices, per_device(): curves = lax.all_to_all(send, 'site', 0, 0, tiled=True)  6.19 us
    ppermute x3, starting transfers between devices, per_device(): lax.ppermute(copies[k], 'rup', [(r, r ^ k) for r in range(rows)])  5.74 us
    ppermute x3, waiting for transfers between devices, per_device(): lax.ppermute(merged[k], 'rup', [(r, (r + k * heights) % rows) for r in ra...  5.59 us
    all_to_all x1, waiting for transfers between devices, per_device(): curves = lax.all_to_all(send, 'site', 0, 0, tiled=True)  4.99 us
    ppermute x3, starting transfers between devices, per_device(): lax.ppermute(merged[k], 'rup', [(r, (r + k * heights) % rows) for r in ra...  2.96 us
  transfers between devices with their start and end apart: 8, of which 6 were waited for; matrix products, arithmetic and copies ran while one was open for 0% of the time, Pallas kernels for 3%

profile of v5, /device:TPU:1, one launch (start us, length us, event | category | flops | bytes accessed | tf_op | source)
XLA Modules:
  0.0 72.4 jit_solution(11397373168463230501)
XLA Ops:
  0.6 1.4 %shard_map.167.rup_ref = f32[16,8,128]{2,1,0:T(8,128)} custom-call(f32[1,128]{1,0:T(1,128)} %bitcast.30, f32[1,128]{1,0:T(1,128)} %bitcast.31, f32[1,128]{1,0:T(1,128)} %bitcast.32, f32[1,128]{1,0:T(1,128)} %bitcast.33, s32[1,128]{1,0:T(1,128)} %bitcast.34, s32[16,128]{1,0:T(8,128)} %bitcast.29), custom_call_target="tpu_custom_call" | custom-call | tf_op jit(solution)/shard_map/pallas_call | solution.py:396
  2.1 0.0 copy-start
  2.1 0.0 copy-start.3
  2.1 0.0 copy-start.4
  2.1 0.0 copy-start.5
  2.1 14.0 %all-to-all-start = ((f32[16,8,128]{2,1,0:T(8,128)}), f32[16,8,128]{2,1,0:T(8,128)S(1)}, u32[]{:S(2)}, u32[]{:S(2)}) async-start(f32[16,8,128]{2,1,0:T(8,128)} %shard_map.167.rup_ref), calls=%async_computation | async-start | bytes 131072 | tf_op jit(solution)/shard_map/all_to_all | solution.py:430
  16.1 0.0 copy-start.8
  16.1 0.0 copy-start.9
  16.1 0.0 copy-done
  16.2 0.0 copy-done.3
  16.2 0.0 copy-done.4
  16.2 0.0 copy-done.5
  16.2 0.6 copy-done.8
  16.8 0.0 copy-done.9
  16.8 1.0 %shard_map.168 = (f32[8,128]{1,0:T(8,128)S(1)}, f32[64,8,128]{2,1,0:T(8,128)S(1)}) custom-call(f32[16,8,128]{2,1,0:T(8,128)S(1)} %copy-done, f32[32,128]{1,0:T(8,128)S(1)} %bitcast.21, f32[32,128]{1,0:T(8,128)S(1)} %bitcast.22, f32[32,128]{1,0:T(8,128)S(1)} %bitcast.23, f32[1,64]{1,0:T(1,128)S(1)} %bitcast.26, f32[1,64]{1,0:T(1,128)S(1)} %bitcast.27), custom_call_target="tpu_custom_call" | custom-call | tf_op jit(solution)/shard_map/pallas_call | solution.py:411
  17.8 9.0 %all-to-all-done.rup_ref = f32[16,8,128]{2,1,0:T(8,128)S(1)} async-done(((f32[16,8,128]{2,1,0:T(8,128)}), f32[16,8,128]{2,1,0:T(8,128)S(1)}, u32[]{:S(2)}, u32[]{:S(2)}) %all-to-all-start) | async-done | bytes 65568 | tf_op jit(solution)/shard_map/all_to_all | solution.py:430
  26.8 10.6 %shard_map.169 = (f32[72,128]{1,0:T(8,128)S(1)}, f32[72,128]{1,0:T(8,128)S(1)}, f32[72,128]{1,0:T(8,128)S(1)}, f32[72,128]{1,0:T(8,128)S(1)}) custom-call(f32[8,128]{1,0:T(8,128)S(1)} %get-tuple-element.14.own_ref, f32[64,8,128]{2,1,0:T(8,128)S(1)} %get-tuple-element.15.sums_ref, f32[16,8,128]{2,1,0:T(8,128)S(1)} %all-to-all-done.rup_ref), custom_call_target="tpu_custom_call" | custom-call | tf_op jit(solution)/shard_map/pallas_call | solution.py:434
  37.4 0.1 collective-permute-start
  37.5 2.7 %collective-permute-start.1 = (f32[72,128]{1,0:T(8,128)S(1)}, f32[72,128]{1,0:T(8,128)S(1)}, u32[]{:S(2)}, u32[]{:S(2)}) collective-permute-start(f32[72,128]{1,0:T(8,128)S(1)} %get-tuple-element.18), channel_id=1, source_target_pairs={{0,32},{16,48},{32,0},{48,16},{64,96},{80,112},{96,64},{112,80},{1... | collective-permute-start | bytes 110600 | tf_op jit(solution)/shard_map/ppermute | solution.py:445
  40.3 2.9 %collective-permute-start.2 = (f32[72,128]{1,0:T(8,128)S(1)}, f32[72,128]{1,0:T(8,128)S(1)}, u32[]{:S(2)}, u32[]{:S(2)}) collective-permute-start(f32[72,128]{1,0:T(8,128)S(1)} %get-tuple-element.19), channel_id=1, source_target_pairs={{0,48},{16,32},{32,16},{48,0},{64,112},{80,96},{96,80},{112,64},{1... | collective-permute-start | bytes 110600 | tf_op jit(solution)/shard_map/ppermute | solution.py:445
  43.2 0.0 collective-permute-done.refs_1_
  43.2 1.8 %collective-permute-done.1.refs_2_ = f32[72,128]{1,0:T(8,128)S(1)} collective-permute-done((f32[72,128]{1,0:T(8,128)S(1)}, f32[72,128]{1,0:T(8,128)S(1)}, u32[]{:S(2)}, u32[]{:S(2)}) %collective-permute-start.1) | collective-permute-done | bytes 36896 | tf_op jit(solution)/shard_map/ppermute | solution.py:445
  45.0 1.1 %collective-permute-done.2.refs_3_ = f32[72,128]{1,0:T(8,128)S(1)} collective-permute-done((f32[72,128]{1,0:T(8,128)S(1)}, f32[72,128]{1,0:T(8,128)S(1)}, u32[]{:S(2)}, u32[]{:S(2)}) %collective-permute-start.2) | collective-permute-done | bytes 36896 | tf_op jit(solution)/shard_map/ppermute | solution.py:445
  46.1 0.1 collective-permute-start.3
  46.2 1.7 %collective-permute-start.4 = (f32[264,128]{1,0:T(8,128)S(1)}, f32[264,128]{1,0:T(8,128)S(1)}, u32[]{:S(2)}, u32[]{:S(2)}) collective-permute-start(f32[264,128]{1,0:T(8,128)S(1)} %get-tuple-element.22), channel_id=1, source_target_pairs={{0,128},{16,144},{32,160},{48,176},{64,192},{80,208},{96,224},{112... | collective-permute-start | bytes 405512 | tf_op jit(solution)/shard_map/ppermute | solution.py:454
  47.9 1.2 %collective-permute-start.5 = (f32[264,128]{1,0:T(8,128)S(1)}, f32[264,128]{1,0:T(8,128)S(1)}, u32[]{:S(2)}, u32[]{:S(2)}) collective-permute-start(f32[264,128]{1,0:T(8,128)S(1)} %get-tuple-element.23), channel_id=1, source_target_pairs={{0,192},{16,208},{32,224},{48,240},{64,0},{80,16},{96,32},{112,48}... | collective-permute-start | bytes 405512 | tf_op jit(solution)/shard_map/ppermute | solution.py:454
  49.0 4.3 %collective-permute-done.3.refs_1_ = f32[264,128]{1,0:T(8,128)S(1)} collective-permute-done((f32[264,128]{1,0:T(8,128)S(1)}, f32[264,128]{1,0:T(8,128)S(1)}, u32[]{:S(2)}, u32[]{:S(2)}) %collective-permute-start.3) | collective-permute-done | bytes 135200 | tf_op jit(solution)/shard_map/ppermute | solution.py:454
  53.3 0.0 collective-permute-done.4.refs_2_
  53.4 1.3 %collective-permute-done.5.refs_3_ = f32[264,128]{1,0:T(8,128)S(1)} collective-permute-done((f32[264,128]{1,0:T(8,128)S(1)}, f32[264,128]{1,0:T(8,128)S(1)}, u32[]{:S(2)}, u32[]{:S(2)}) %collective-permute-start.5) | collective-permute-done | bytes 135200 | tf_op jit(solution)/shard_map/ppermute | solution.py:454
  54.6 0.0 copy-start.1
  54.6 2.1 %shard_map.172 = f32[16,32,128]{2,1,0:T(8,128)} custom-call(f32[264,128]{1,0:T(8,128)S(1)} %get-tuple-element.20.refs_0_, f32[264,128]{1,0:T(8,128)S(1)} %collective-permute-done.3.refs_1_, f32[264,128]{1,0:T(8,128)S(1)} %collective-permute-done.4.refs_2_, f32[264,128]{1,0:T(8,128)S(1)} %collective-permute-done.5.refs_3_), custom_call_target="tpu_custom_call" | custom-call | tf_op jit(solution)/shard_map/pallas_call | solution.py:465
  56.8 0.0 copy-start.2
  56.8 0.0 copy-start.6
  56.8 6.2 %all-to-all-start.1 = ((f32[16,32,128]{2,1,0:T(8,128)}), f32[16,32,128]{2,1,0:T(8,128)S(1)}, u32[]{:S(2)}, u32[]{:S(2)}) async-start(f32[16,32,128]{2,1,0:T(8,128)} %shard_map.172), calls=%async_computation.1 | async-start | bytes 524288 | tf_op jit(solution)/shard_map/all_to_all | solution.py:473
  63.0 0.0 copy-start.10
  63.0 0.0 copy-done.1
  63.0 0.0 copy-done.2
  63.0 0.0 copy-done.6
  63.0 0.6 copy-done.10
  63.6 0.7 shard_map.173
  64.3 0.0 copy-start.7
  64.3 0.8 %shard_map.171 = f32[32,4096]{1,0:T(8,128)} custom-call(f32[264,128]{1,0:T(8,128)S(1)} %get-tuple-element.20.refs_0_, f32[264,128]{1,0:T(8,128)S(1)} %collective-permute-done.3.refs_1_, f32[264,128]{1,0:T(8,128)S(1)} %collective-permute-done.4.refs_2_, f32[264,128]{1,0:T(8,128)S(1)} %collective-permute-done.5.refs_3_), custom_call_target="tpu_custom_call" | custom-call | tf_op jit(solution)/shard_map/pallas_call | solution.py:458
  65.1 5.0 %all-to-all-done.1.curves_ref = f32[16,32,128]{2,1,0:T(8,128)S(1)} async-done(((f32[16,32,128]{2,1,0:T(8,128)}), f32[16,32,128]{2,1,0:T(8,128)S(1)}, u32[]{:S(2)}, u32[]{:S(2)}) %all-to-all-start.1) | async-done | bytes 262176 | tf_op jit(solution)/shard_map/all_to_all | solution.py:473
  70.1 0.0 copy-done.7
  70.1 2.2 %shard_map.174 = f32[32,2048]{1,0:T(8,128)} custom-call(f32[16,32,128]{2,1,0:T(8,128)S(1)} %all-to-all-done.1.curves_ref, s32[16,128]{1,0:T(8,128)S(1)} %bitcast.20, s32[16,128]{1,0:T(8,128)S(1)} %get-tuple-element.24.slot_ref, s32[16,128]{1,0:T(8,128)S(1)} %bitcast.25, bf16[1024,256]{1,0:T(8,128)(2,1)S(1)} %get-tuple-element.25.split_ref), custom_call_target="tpu_custom_call" | custom-call | tf_op jit(solution)/shard_map/pallas_call | solution.py:485
  (1 shorter events, 0.0 us)
Async XLA Ops:
  2.1 14.1 %copy-start = (f32[16,8,128]{2,1,0:T(8,128)S(1)}, f32[16,8,128]{2,1,0:T(8,128)}, u32[]{:S(2)}) copy-start(f32[16,8,128]{2,1,0:T(8,128)} %shard_map.167.rup_ref) | copy-start | bytes 196612
  2.1 14.1 %copy-start.3 = (f32[4096]{0:T(1024)S(1)}, f32[4096]{0:T(1024)}, u32[]{:S(2)}) copy-start(f32[4096]{0:T(1024)} %param.16) | copy-start | bytes 49156
  2.1 14.1 %copy-start.4 = (f32[4096]{0:T(1024)S(1)}, f32[4096]{0:T(1024)}, u32[]{:S(2)}) copy-start(f32[4096]{0:T(1024)} %param.17) | copy-start | bytes 49156
  2.1 14.1 %copy-start.5 = (f32[4096]{0:T(1024)S(1)}, f32[4096]{0:T(1024)}, u32[]{:S(2)}) copy-start(f32[4096]{0:T(1024)} %param.18) | copy-start | bytes 49156
  2.1 24.7 %all-to-all-start = ((f32[16,8,128]{2,1,0:T(8,128)}), f32[16,8,128]{2,1,0:T(8,128)S(1)}, u32[]{:S(2)}, u32[]{:S(2)}) async-start(f32[16,8,128]{2,1,0:T(8,128)} %shard_map.167.rup_ref), calls=%async_computation | async-start | bytes 131072 | tf_op jit(solution)/shard_map/all_to_all | solution.py:430
  16.1 0.7 copy-start.8
  16.1 0.7 copy-start.9
  37.4 5.7 %collective-permute-start = (f32[72,128]{1,0:T(8,128)S(1)}, f32[72,128]{1,0:T(8,128)S(1)}, u32[]{:S(2)}, u32[]{:S(2)}) collective-permute-start(f32[72,128]{1,0:T(8,128)S(1)} %get-tuple-element.17), channel_id=1, source_target_pairs={{0,16},{16,0},{32,48},{48,32},{64,80},{80,64},{96,112},{112,96},{1... | collective-permute-start | bytes 110600 | tf_op jit(solution)/shard_map/ppermute | solution.py:445
  37.5 7.4 %collective-permute-start.1 = (f32[72,128]{1,0:T(8,128)S(1)}, f32[72,128]{1,0:T(8,128)S(1)}, u32[]{:S(2)}, u32[]{:S(2)}) collective-permute-start(f32[72,128]{1,0:T(8,128)S(1)} %get-tuple-element.18), channel_id=1, source_target_pairs={{0,32},{16,48},{32,0},{48,16},{64,96},{80,112},{96,64},{112,80},{1... | collective-permute-start | bytes 110600 | tf_op jit(solution)/shard_map/ppermute | solution.py:445
  40.3 5.8 %collective-permute-start.2 = (f32[72,128]{1,0:T(8,128)S(1)}, f32[72,128]{1,0:T(8,128)S(1)}, u32[]{:S(2)}, u32[]{:S(2)}) collective-permute-start(f32[72,128]{1,0:T(8,128)S(1)} %get-tuple-element.19), channel_id=1, source_target_pairs={{0,48},{16,32},{32,16},{48,0},{64,112},{80,96},{96,80},{112,64},{1... | collective-permute-start | bytes 110600 | tf_op jit(solution)/shard_map/ppermute | solution.py:445
  46.1 7.3 %collective-permute-start.3 = (f32[264,128]{1,0:T(8,128)S(1)}, f32[264,128]{1,0:T(8,128)S(1)}, u32[]{:S(2)}, u32[]{:S(2)}) collective-permute-start(f32[264,128]{1,0:T(8,128)S(1)} %get-tuple-element.21), channel_id=1, source_target_pairs={{0,64},{16,80},{32,96},{48,112},{64,128},{80,144},{96,160},{112,17... | collective-permute-start | bytes 405512 | tf_op jit(solution)/shard_map/ppermute | solution.py:454
  46.2 7.2 %collective-permute-start.4 = (f32[264,128]{1,0:T(8,128)S(1)}, f32[264,128]{1,0:T(8,128)S(1)}, u32[]{:S(2)}, u32[]{:S(2)}) collective-permute-start(f32[264,128]{1,0:T(8,128)S(1)} %get-tuple-element.22), channel_id=1, source_target_pairs={{0,128},{16,144},{32,160},{48,176},{64,192},{80,208},{96,224},{112... | collective-permute-start | bytes 405512 | tf_op jit(solution)/shard_map/ppermute | solution.py:454
  47.9 6.7 %collective-permute-start.5 = (f32[264,128]{1,0:T(8,128)S(1)}, f32[264,128]{1,0:T(8,128)S(1)}, u32[]{:S(2)}, u32[]{:S(2)}) collective-permute-start(f32[264,128]{1,0:T(8,128)S(1)} %get-tuple-element.23), channel_id=1, source_target_pairs={{0,192},{16,208},{32,224},{48,240},{64,0},{80,16},{96,32},{112,48}... | collective-permute-start | bytes 405512 | tf_op jit(solution)/shard_map/ppermute | solution.py:454
  54.6 8.3 %copy-start.1 = (f32[128,32,32]{0,2,1:T(8,128)S(1)}, f32[128,32,32]{0,2,1:T(8,128)}, u32[]{:S(2)}) copy-start(f32[128,32,32]{0,2,1:T(8,128)} %param.31) | copy-start | bytes 1572868
  56.8 6.2 %copy-start.2 = (s32[2048]{0:T(1024)S(1)}, s32[2048]{0:T(1024)}, u32[]{:S(2)}) copy-start(s32[2048]{0:T(1024)} %param.28) | copy-start | bytes 24580
  56.8 6.2 %copy-start.6 = (s32[2048]{0:T(1024)S(1)}, s32[2048]{0:T(1024)}, u32[]{:S(2)}) copy-start(s32[2048]{0:T(1024)} %param.29) | copy-start | bytes 24580
  56.8 13.4 %all-to-all-start.1 = ((f32[16,32,128]{2,1,0:T(8,128)}), f32[16,32,128]{2,1,0:T(8,128)S(1)}, u32[]{:S(2)}, u32[]{:S(2)}) async-start(f32[16,32,128]{2,1,0:T(8,128)} %shard_map.172), calls=%async_computation.1 | async-start | bytes 524288 | tf_op jit(solution)/shard_map/all_to_all | solution.py:473
  63.0 0.7 copy-start.10
  64.3 5.8 %copy-start.7 = (s32[2048]{0:T(1024)S(1)}, s32[2048]{0:T(1024)}, u32[]{:S(2)}) copy-start(s32[2048]{0:T(1024)} %param.30) | copy-start | bytes 24580

commit v6 on v5

--- a/solution.py
+++ b/solution.py
@@ -105,13 +105,12 @@
     for u in range(count):
         rate = pre_ref[0, first + u]
         gap = pre_ref[1, first + u]
-        z = pre_ref[2 + t, first + u]
+        start = pre_ref[2 + t, first + u]
         whole = rate if u == 0 else whole + rate
         for l in range(levels):
+            z = z + gap if l % 16 else start + gap * float(l)
             term = rate * lax.erf(z)
             total[l] = term if u == 0 else total[l] + term
-            if l < levels - 1:
-                z = z + gap
     return [whole - part for part in total]
 
 
@@ -190,7 +189,7 @@
     length = in_refs[0].shape[0] - SUBLANES
     row = place()[0]
     for k, out_ref in enumerate(out_refs):
-        x = ((row >> 2) + k) & (len(out_refs) - 1)
+        x = (row >> 2) ^ k
         out_ref[heights * length :, :] = jnp.zeros((SUBLANES, LANES), jnp.float32)
         for flip, in_ref in enumerate(in_refs):
             height = (row & (heights - 1)) ^ flip
@@ -204,7 +203,7 @@
     row = place()[0]
     tiles = out_ref.shape[1] // (len(in_refs) * LANES)
     for k, in_ref in enumerate(in_refs):
-        x = ((row >> 2) - k) & (len(in_refs) - 1)
+        x = (row >> 2) ^ k
         for t in range(tiles):
             at = pl.multiple_of((x * tiles + t) * LANES, LANES)
             out_ref[:, pl.ds(at, LANES)] = in_ref[t * levels : (t + 1) * levels, :]
@@ -242,7 +241,7 @@
     row, site = place()
 
     def origin(b):
-        return (((row >> 2) - b // heights) & (parts - 1)) * heights + b % heights
+        return ((row >> 2) ^ (b // heights)) * heights + b % heights
 
     def piece(b, t, first, count):
         at = (b % heights * tiles + t) * levels + first
@@ -452,7 +451,7 @@
         compiler_params=limit,
     )(copies[0], *[swap(k) for k in range(1, heights)])
     shift = lambda k: lax.ppermute(
-        merged[k], "rup", [(r, (r + k * heights) % rows) for r in range(rows)]
+        merged[k], "rup", [(r, r ^ (k * heights)) for r in range(rows)]
     )
     parts = [merged[0]] + [shift(k) for k in range(1, east)]
     hazard = pl.pallas_call(

time: 72.8 us -> 73 us (level)
    all_to_all x1, starting transfers between devices: 6.19 us -> 5.21 us  [per_device(): curves = lax.all_to_all(send, 'site', 0, 0, tiled=True)]
    ppermute x3, starting transfers between devices: 2.96 us -> 3.94 us  [per_device(): lax.ppermute(merged[k], 'rup', [(r, r ^ k * heights) for r in range(rows)])]
where the time goes in v6:
time: 73 us; the launch traced here: 72.6 us
  starting transfers between devices  28.9 us (40%)
  waiting for transfers between devices  22.6 us (31%)
  Pallas kernels  19 us (26%)
  local copies, waits for them, and re-layouts  1.27 us (2%)
  between operations  0.79 us (1%)
    all_to_all x1, starting transfers between devices, per_device(): lax.all_to_all(packed, ('rup', 'site'), 0, 0, axis_index_groups=groups, t...  14 us
    pallas_call x1, Pallas kernels, per_device(): pl.pallas_call(functools.partial(hazard_kernel, levels), out_shape=(copy,...  10.7 us
    all_to_all x1, waiting for transfers between devices, per_device(): lax.all_to_all(packed, ('rup', 'site'), 0, 0, axis_index_groups=groups, t...  9 us
    ppermute x3, waiting for transfers between devices, per_device(): lax.ppermute(merged[k], 'rup', [(r, r ^ k * heights) for r in range(rows)])  5.76 us
    ppermute x3, starting transfers between devices, per_device(): lax.ppermute(copies[k], 'rup', [(r, r ^ k) for r in range(rows)])  5.74 us
    all_to_all x1, starting transfers between devices, per_device(): curves = lax.all_to_all(send, 'site', 0, 0, tiled=True)  5.21 us
    all_to_all x1, waiting for transfers between devices, per_device(): curves = lax.all_to_all(send, 'site', 0, 0, tiled=True)  4.98 us
    ppermute x3, starting transfers between devices, per_device(): lax.ppermute(merged[k], 'rup', [(r, r ^ k * heights) for r in range(rows)])  3.94 us
  transfers between devices with their start and end apart: 8, of which 6 were waited for; matrix products, arithmetic and copies ran while one was open for 0% of the time, Pallas kernels for 3%

profile of v6, /device:TPU:1, one launch (start us, length us, event | category | flops | bytes accessed | tf_op | source)
XLA Modules:
  0.0 72.6 jit_solution(5868005602883070469)
XLA Ops:
  0.6 1.4 %shard_map.167.rup_ref = f32[16,8,128]{2,1,0:T(8,128)} custom-call(f32[1,128]{1,0:T(1,128)} %bitcast.30, f32[1,128]{1,0:T(1,128)} %bitcast.31, f32[1,128]{1,0:T(1,128)} %bitcast.32, f32[1,128]{1,0:T(1,128)} %bitcast.33, s32[1,128]{1,0:T(1,128)} %bitcast.34, s32[16,128]{1,0:T(8,128)} %bitcast.29), custom_call_target="tpu_custom_call" | custom-call | tf_op jit(solution)/shard_map/pallas_call | solution.py:395
  2.1 0.0 copy-start
  2.1 0.0 copy-start.3
  2.1 0.0 copy-start.4
  2.1 0.0 copy-start.5
  2.1 14.0 %all-to-all-start = ((f32[16,8,128]{2,1,0:T(8,128)}), f32[16,8,128]{2,1,0:T(8,128)S(1)}, u32[]{:S(2)}, u32[]{:S(2)}) async-start(f32[16,8,128]{2,1,0:T(8,128)} %shard_map.167.rup_ref), calls=%async_computation | async-start | bytes 131072 | tf_op jit(solution)/shard_map/all_to_all | solution.py:429
  16.1 0.0 copy-start.8
  16.1 0.0 copy-start.9
  16.1 0.0 copy-done
  16.2 0.0 copy-done.3
  16.2 0.0 copy-done.4
  16.2 0.0 copy-done.5
  16.2 0.6 copy-done.8
  16.8 0.0 copy-done.9
  16.8 1.0 %shard_map.168 = (f32[8,128]{1,0:T(8,128)S(1)}, f32[64,8,128]{2,1,0:T(8,128)S(1)}) custom-call(f32[16,8,128]{2,1,0:T(8,128)S(1)} %copy-done, f32[32,128]{1,0:T(8,128)S(1)} %bitcast.21, f32[32,128]{1,0:T(8,128)S(1)} %bitcast.22, f32[32,128]{1,0:T(8,128)S(1)} %bitcast.23, f32[1,64]{1,0:T(1,128)S(1)} %bitcast.26, f32[1,64]{1,0:T(1,128)S(1)} %bitcast.27), custom_call_target="tpu_custom_call" | custom-call | tf_op jit(solution)/shard_map/pallas_call | solution.py:410
  17.8 9.0 %all-to-all-done.rup_ref = f32[16,8,128]{2,1,0:T(8,128)S(1)} async-done(((f32[16,8,128]{2,1,0:T(8,128)}), f32[16,8,128]{2,1,0:T(8,128)S(1)}, u32[]{:S(2)}, u32[]{:S(2)}) %all-to-all-start) | async-done | bytes 65568 | tf_op jit(solution)/shard_map/all_to_all | solution.py:429
  26.8 10.7 %shard_map.169 = (f32[72,128]{1,0:T(8,128)S(1)}, f32[72,128]{1,0:T(8,128)S(1)}, f32[72,128]{1,0:T(8,128)S(1)}, f32[72,128]{1,0:T(8,128)S(1)}) custom-call(f32[8,128]{1,0:T(8,128)S(1)} %get-tuple-element.14.own_ref, f32[64,8,128]{2,1,0:T(8,128)S(1)} %get-tuple-element.15.sums_ref, f32[16,8,128]{2,1,0:T(8,128)S(1)} %all-to-all-done.rup_ref), custom_call_target="tpu_custom_call" | custom-call | tf_op jit(solution)/shard_map/pallas_call | solution.py:433
  37.5 0.1 collective-permute-start
  37.6 2.7 %collective-permute-start.1 = (f32[72,128]{1,0:T(8,128)S(1)}, f32[72,128]{1,0:T(8,128)S(1)}, u32[]{:S(2)}, u32[]{:S(2)}) collective-permute-start(f32[72,128]{1,0:T(8,128)S(1)} %get-tuple-element.18), channel_id=1, source_target_pairs={{0,32},{16,48},{32,0},{48,16},{64,96},{80,112},{96,64},{112,80},{1... | collective-permute-start | bytes 110600 | tf_op jit(solution)/shard_map/ppermute | solution.py:444
  40.3 2.9 %collective-permute-start.2 = (f32[72,128]{1,0:T(8,128)S(1)}, f32[72,128]{1,0:T(8,128)S(1)}, u32[]{:S(2)}, u32[]{:S(2)}) collective-permute-start(f32[72,128]{1,0:T(8,128)S(1)} %get-tuple-element.19), channel_id=1, source_target_pairs={{0,48},{16,32},{32,16},{48,0},{64,112},{80,96},{96,80},{112,64},{1... | collective-permute-start | bytes 110600 | tf_op jit(solution)/shard_map/ppermute | solution.py:444
  43.2 0.0 collective-permute-done.refs_1_
  43.2 1.8 %collective-permute-done.1.refs_2_ = f32[72,128]{1,0:T(8,128)S(1)} collective-permute-done((f32[72,128]{1,0:T(8,128)S(1)}, f32[72,128]{1,0:T(8,128)S(1)}, u32[]{:S(2)}, u32[]{:S(2)}) %collective-permute-start.1) | collective-permute-done | bytes 36896 | tf_op jit(solution)/shard_map/ppermute | solution.py:444
  45.0 1.1 %collective-permute-done.2.refs_3_ = f32[72,128]{1,0:T(8,128)S(1)} collective-permute-done((f32[72,128]{1,0:T(8,128)S(1)}, f32[72,128]{1,0:T(8,128)S(1)}, u32[]{:S(2)}, u32[]{:S(2)}) %collective-permute-start.2) | collective-permute-done | bytes 36896 | tf_op jit(solution)/shard_map/ppermute | solution.py:444
  46.1 0.1 collective-permute-start.3
  46.2 1.7 %collective-permute-start.4 = (f32[264,128]{1,0:T(8,128)S(1)}, f32[264,128]{1,0:T(8,128)S(1)}, u32[]{:S(2)}, u32[]{:S(2)}) collective-permute-start(f32[264,128]{1,0:T(8,128)S(1)} %get-tuple-element.22), channel_id=1, source_target_pairs={{0,128},{16,144},{32,160},{48,176},{64,192},{80,208},{96,224},{112... | collective-permute-start | bytes 405512 | tf_op jit(solution)/shard_map/ppermute | solution.py:453
  47.9 2.1 %collective-permute-start.5 = (f32[264,128]{1,0:T(8,128)S(1)}, f32[264,128]{1,0:T(8,128)S(1)}, u32[]{:S(2)}, u32[]{:S(2)}) collective-permute-start(f32[264,128]{1,0:T(8,128)S(1)} %get-tuple-element.23), channel_id=1, source_target_pairs={{0,192},{16,208},{32,224},{48,240},{64,128},{80,144},{96,160},{112... | collective-permute-start | bytes 405512 | tf_op jit(solution)/shard_map/ppermute | solution.py:453
  50.1 0.0 collective-permute-done.3.refs_1_
  50.1 2.9 %collective-permute-done.4.refs_2_ = f32[264,128]{1,0:T(8,128)S(1)} collective-permute-done((f32[264,128]{1,0:T(8,128)S(1)}, f32[264,128]{1,0:T(8,128)S(1)}, u32[]{:S(2)}, u32[]{:S(2)}) %collective-permute-start.4) | collective-permute-done | bytes 135200 | tf_op jit(solution)/shard_map/ppermute | solution.py:453
  53.0 2.8 %collective-permute-done.5.refs_3_ = f32[264,128]{1,0:T(8,128)S(1)} collective-permute-done((f32[264,128]{1,0:T(8,128)S(1)}, f32[264,128]{1,0:T(8,128)S(1)}, u32[]{:S(2)}, u32[]{:S(2)}) %collective-permute-start.5) | collective-permute-done | bytes 135200 | tf_op jit(solution)/shard_map/ppermute | solution.py:453
  55.8 0.0 copy-start.1
  55.8 2.1 %shard_map.172 = f32[16,32,128]{2,1,0:T(8,128)} custom-call(f32[264,128]{1,0:T(8,128)S(1)} %get-tuple-element.20.refs_0_, f32[264,128]{1,0:T(8,128)S(1)} %collective-permute-done.3.refs_1_, f32[264,128]{1,0:T(8,128)S(1)} %collective-permute-done.4.refs_2_, f32[264,128]{1,0:T(8,128)S(1)} %collective-permute-done.5.refs_3_), custom_call_target="tpu_custom_call" | custom-call | tf_op jit(solution)/shard_map/pallas_call | solution.py:464
  58.0 0.0 copy-start.2
  58.0 0.0 copy-start.6
  58.0 5.2 %all-to-all-start.1 = ((f32[16,32,128]{2,1,0:T(8,128)}), f32[16,32,128]{2,1,0:T(8,128)S(1)}, u32[]{:S(2)}, u32[]{:S(2)}) async-start(f32[16,32,128]{2,1,0:T(8,128)} %shard_map.172), calls=%async_computation.1 | async-start | bytes 524288 | tf_op jit(solution)/shard_map/all_to_all | solution.py:472
  63.2 0.0 copy-start.10
  63.2 0.0 copy-done.1
  63.2 0.0 copy-done.2
  63.2 0.0 copy-done.6
  63.2 0.6 copy-done.10
  63.8 0.7 shard_map.173
  64.5 0.0 copy-start.7
  64.5 0.9 %shard_map.171 = f32[32,4096]{1,0:T(8,128)} custom-call(f32[264,128]{1,0:T(8,128)S(1)} %get-tuple-element.20.refs_0_, f32[264,128]{1,0:T(8,128)S(1)} %collective-permute-done.3.refs_1_, f32[264,128]{1,0:T(8,128)S(1)} %collective-permute-done.4.refs_2_, f32[264,128]{1,0:T(8,128)S(1)} %collective-permute-done.5.refs_3_), custom_call_target="tpu_custom_call" | custom-call | tf_op jit(solution)/shard_map/pallas_call | solution.py:457
  65.4 5.0 %all-to-all-done.1.curves_ref = f32[16,32,128]{2,1,0:T(8,128)S(1)} async-done(((f32[16,32,128]{2,1,0:T(8,128)}), f32[16,32,128]{2,1,0:T(8,128)S(1)}, u32[]{:S(2)}, u32[]{:S(2)}) %all-to-all-start.1) | async-done | bytes 262176 | tf_op jit(solution)/shard_map/all_to_all | solution.py:472
  70.3 0.0 copy-done.7
  70.3 2.2 %shard_map.174 = f32[32,2048]{1,0:T(8,128)} custom-call(f32[16,32,128]{2,1,0:T(8,128)S(1)} %all-to-all-done.1.curves_ref, s32[16,128]{1,0:T(8,128)S(1)} %bitcast.20, s32[16,128]{1,0:T(8,128)S(1)} %get-tuple-element.24.slot_ref, s32[16,128]{1,0:T(8,128)S(1)} %bitcast.25, bf16[1024,256]{1,0:T(8,128)(2,1)S(1)} %get-tuple-element.25.split_ref), custom_call_target="tpu_custom_call" | custom-call | tf_op jit(solution)/shard_map/pallas_call | solution.py:484
  (1 shorter events, 0.0 us)
Async XLA Ops:
  2.1 14.1 %copy-start = (f32[16,8,128]{2,1,0:T(8,128)S(1)}, f32[16,8,128]{2,1,0:T(8,128)}, u32[]{:S(2)}) copy-start(f32[16,8,128]{2,1,0:T(8,128)} %shard_map.167.rup_ref) | copy-start | bytes 196612
  2.1 14.1 %copy-start.3 = (f32[4096]{0:T(1024)S(1)}, f32[4096]{0:T(1024)}, u32[]{:S(2)}) copy-start(f32[4096]{0:T(1024)} %param.16) | copy-start | bytes 49156
  2.1 14.1 %copy-start.4 = (f32[4096]{0:T(1024)S(1)}, f32[4096]{0:T(1024)}, u32[]{:S(2)}) copy-start(f32[4096]{0:T(1024)} %param.17) | copy-start | bytes 49156
  2.1 14.1 %copy-start.5 = (f32[4096]{0:T(1024)S(1)}, f32[4096]{0:T(1024)}, u32[]{:S(2)}) copy-start(f32[4096]{0:T(1024)} %param.18) | copy-start | bytes 49156
  2.1 24.7 %all-to-all-start = ((f32[16,8,128]{2,1,0:T(8,128)}), f32[16,8,128]{2,1,0:T(8,128)S(1)}, u32[]{:S(2)}, u32[]{:S(2)}) async-start(f32[16,8,128]{2,1,0:T(8,128)} %shard_map.167.rup_ref), calls=%async_computation | async-start | bytes 131072 | tf_op jit(solution)/shard_map/all_to_all | solution.py:429
  16.1 0.7 copy-start.8
  16.1 0.7 copy-start.9
  37.5 5.7 %collective-permute-start = (f32[72,128]{1,0:T(8,128)S(1)}, f32[72,128]{1,0:T(8,128)S(1)}, u32[]{:S(2)}, u32[]{:S(2)}) collective-permute-start(f32[72,128]{1,0:T(8,128)S(1)} %get-tuple-element.17), channel_id=1, source_target_pairs={{0,16},{16,0},{32,48},{48,32},{64,80},{80,64},{96,112},{112,96},{1... | collective-permute-start | bytes 110600 | tf_op jit(solution)/shard_map/ppermute | solution.py:444
  37.6 7.4 %collective-permute-start.1 = (f32[72,128]{1,0:T(8,128)S(1)}, f32[72,128]{1,0:T(8,128)S(1)}, u32[]{:S(2)}, u32[]{:S(2)}) collective-permute-start(f32[72,128]{1,0:T(8,128)S(1)} %get-tuple-element.18), channel_id=1, source_target_pairs={{0,32},{16,48},{32,0},{48,16},{64,96},{80,112},{96,64},{112,80},{1... | collective-permute-start | bytes 110600 | tf_op jit(solution)/shard_map/ppermute | solution.py:444
  40.3 5.8 %collective-permute-start.2 = (f32[72,128]{1,0:T(8,128)S(1)}, f32[72,128]{1,0:T(8,128)S(1)}, u32[]{:S(2)}, u32[]{:S(2)}) collective-permute-start(f32[72,128]{1,0:T(8,128)S(1)} %get-tuple-element.19), channel_id=1, source_target_pairs={{0,48},{16,32},{32,16},{48,0},{64,112},{80,96},{96,80},{112,64},{1... | collective-permute-start | bytes 110600 | tf_op jit(solution)/shard_map/ppermute | solution.py:444
  46.1 3.9 %collective-permute-start.3 = (f32[264,128]{1,0:T(8,128)S(1)}, f32[264,128]{1,0:T(8,128)S(1)}, u32[]{:S(2)}, u32[]{:S(2)}) collective-permute-start(f32[264,128]{1,0:T(8,128)S(1)} %get-tuple-element.21), channel_id=1, source_target_pairs={{0,64},{16,80},{32,96},{48,112},{64,0},{80,16},{96,32},{112,48},{1... | collective-permute-start | bytes 405512 | tf_op jit(solution)/shard_map/ppermute | solution.py:453
  46.2 6.8 %collective-permute-start.4 = (f32[264,128]{1,0:T(8,128)S(1)}, f32[264,128]{1,0:T(8,128)S(1)}, u32[]{:S(2)}, u32[]{:S(2)}) collective-permute-start(f32[264,128]{1,0:T(8,128)S(1)} %get-tuple-element.22), channel_id=1, source_target_pairs={{0,128},{16,144},{32,160},{48,176},{64,192},{80,208},{96,224},{112... | collective-permute-start | bytes 405512 | tf_op jit(solution)/shard_map/ppermute | solution.py:453
  47.9 7.9 %collective-permute-start.5 = (f32[264,128]{1,0:T(8,128)S(1)}, f32[264,128]{1,0:T(8,128)S(1)}, u32[]{:S(2)}, u32[]{:S(2)}) collective-permute-start(f32[264,128]{1,0:T(8,128)S(1)} %get-tuple-element.23), channel_id=1, source_target_pairs={{0,192},{16,208},{32,224},{48,240},{64,128},{80,144},{96,160},{112... | collective-permute-start | bytes 405512 | tf_op jit(solution)/shard_map/ppermute | solution.py:453
  55.8 7.3 %copy-start.1 = (f32[128,32,32]{0,2,1:T(8,128)S(1)}, f32[128,32,32]{0,2,1:T(8,128)}, u32[]{:S(2)}) copy-start(f32[128,32,32]{0,2,1:T(8,128)} %param.31) | copy-start | bytes 1572868
  58.0 5.2 %copy-start.2 = (s32[2048]{0:T(1024)S(1)}, s32[2048]{0:T(1024)}, u32[]{:S(2)}) copy-start(s32[2048]{0:T(1024)} %param.28) | copy-start | bytes 24580
  58.0 5.2 %copy-start.6 = (s32[2048]{0:T(1024)S(1)}, s32[2048]{0:T(1024)}, u32[]{:S(2)}) copy-start(s32[2048]{0:T(1024)} %param.29) | copy-start | bytes 24580
  58.0 12.4 %all-to-all-start.1 = ((f32[16,32,128]{2,1,0:T(8,128)}), f32[16,32,128]{2,1,0:T(8,128)S(1)}, u32[]{:S(2)}, u32[]{:S(2)}) async-start(f32[16,32,128]{2,1,0:T(8,128)} %shard_map.172), calls=%async_computation.1 | async-start | bytes 524288 | tf_op jit(solution)/shard_map/all_to_all | solution.py:472
  63.2 0.7 copy-start.10
  64.5 5.8 %copy-start.7 = (s32[2048]{0:T(1024)S(1)}, s32[2048]{0:T(1024)}, u32[]{:S(2)}) copy-start(s32[2048]{0:T(1024)} %param.30) | copy-start | bytes 24580

commit v7 on v6

--- a/solution.py
+++ b/solution.py
@@ -11,6 +11,7 @@
 LANES = 128
 SUBLANES = 8
 LIST = 5
+FAR_FIRST = (0, 2, 1, 3)
 UNROLL = 24
 PRODUCTS = 2
 VMEM = pl.BlockSpec(memory_space=pltpu.VMEM)
@@ -191,7 +192,7 @@
     for k, out_ref in enumerate(out_refs):
         x = (row >> 2) ^ k
         out_ref[heights * length :, :] = jnp.zeros((SUBLANES, LANES), jnp.float32)
-        for flip, in_ref in enumerate(in_refs):
+        for flip, in_ref in zip(FAR_FIRST, in_refs):
             height = (row & (heights - 1)) ^ flip
             at = pl.multiple_of(height * length, length)
             out_ref[pl.ds(at, length), :] = in_ref[0:length, :]
@@ -202,7 +203,7 @@
     in_refs, out_ref = refs[:-1], refs[-1]
     row = place()[0]
     tiles = out_ref.shape[1] // (len(in_refs) * LANES)
-    for k, in_ref in enumerate(in_refs):
+    for k, in_ref in zip(FAR_FIRST, in_refs):
         x = (row >> 2) ^ k
         for t in range(tiles):
             at = pl.multiple_of((x * tiles + t) * LANES, LANES)
@@ -232,7 +233,7 @@
 
 
 def relay_kernel(levels, span, *refs):
-    part_refs, send_ref, lhs_ref = refs[:-2], refs[-2], refs[-1]
+    part_refs, send_ref, lhs_ref = [refs[k] for k in FAR_FIRST], refs[-2], refs[-1]
     parts = len(part_refs)
     heights = (part_refs[0].shape[0] - SUBLANES) * LANES // (levels * span)
     blocks = parts * heights
@@ -449,11 +450,11 @@
         in_specs=[VMEM] * heights,
         out_specs=(VMEM,) * east,
         compiler_params=limit,
-    )(copies[0], *[swap(k) for k in range(1, heights)])
+    )(*[swap(k) if k else copies[0] for k in FAR_FIRST])
     shift = lambda k: lax.ppermute(
         merged[k], "rup", [(r, r ^ (k * heights)) for r in range(rows)]
     )
-    parts = [merged[0]] + [shift(k) for k in range(1, east)]
+    parts = [shift(k) if k else merged[0] for k in FAR_FIRST]
     hazard = pl.pallas_call(
         functools.partial(output_kernel, levels),
         out_shape=jax.ShapeDtypeStruct((levels, sites), jnp.float32),

time: 73 us -> 71.9 us (0.985)
  waiting for transfers between devices: 22.6 us -> 20.8 us
    ppermute x3, waiting for transfers between devices: 5.76 us -> 4.37 us  [per_device(): lax.ppermute(merged[k], 'rup', [(r, r ^ k * heights) for r in range(rows)])]
    all_to_all x1, starting transfers between devices: 5.21 us -> 6.49 us  [per_device(): curves = lax.all_to_all(send, 'site', 0, 0, tiled=True)]
  transfers between devices with their start and end apart: 8 -> 8, of which waited for: 6 -> 6; matrix products, arithmetic and copies ran while one was open for 0% -> 0% of each run, Pallas kernels for 3% -> 4%
where the time goes in v7:
time: 71.9 us; the launch traced here: 71.5 us
  starting transfers between devices  29.6 us (41%)
  waiting for transfers between devices  20.8 us (29%)
  Pallas kernels  19 us (26%)
  local copies, waits for them, and re-layouts  1.27 us (2%)
  between operations  0.79 us (1%)
    all_to_all x1, starting transfers between devices, per_device(): lax.all_to_all(packed, ('rup', 'site'), 0, 0, axis_index_groups=groups, t...  14 us
    pallas_call x1, Pallas kernels, per_device(): pl.pallas_call(functools.partial(hazard_kernel, levels), out_shape=(copy,...  10.7 us
    all_to_all x1, waiting for transfers between devices, per_device(): lax.all_to_all(packed, ('rup', 'site'), 0, 0, axis_index_groups=groups, t...  9 us
    all_to_all x1, starting transfers between devices, per_device(): curves = lax.all_to_all(send, 'site', 0, 0, tiled=True)  6.49 us
    ppermute x3, starting transfers between devices, per_device(): lax.ppermute(copies[k], 'rup', [(r, r ^ k) for r in range(rows)])  5.74 us
    all_to_all x1, waiting for transfers between devices, per_device(): curves = lax.all_to_all(send, 'site', 0, 0, tiled=True)  4.98 us
    ppermute x3, waiting for transfers between devices, per_device(): lax.ppermute(merged[k], 'rup', [(r, r ^ k * heights) for r in range(rows)])  4.37 us
    ppermute x3, starting transfers between devices, per_device(): lax.ppermute(merged[k], 'rup', [(r, r ^ k * heights) for r in range(rows)])  3.33 us
  transfers between devices with their start and end apart: 8, of which 6 were waited for; matrix products, arithmetic and copies ran while one was open for 0% of the time, Pallas kernels for 4%

profile of v7, /device:TPU:1, one launch (start us, length us, event | category | flops | bytes accessed | tf_op | source)
XLA Modules:
  0.0 71.5 jit_solution(13736662219738449511)
XLA Ops:
  0.6 1.4 %shard_map.167.rup_ref = f32[16,8,128]{2,1,0:T(8,128)} custom-call(f32[1,128]{1,0:T(1,128)} %bitcast.30, f32[1,128]{1,0:T(1,128)} %bitcast.31, f32[1,128]{1,0:T(1,128)} %bitcast.32, f32[1,128]{1,0:T(1,128)} %bitcast.33, s32[1,128]{1,0:T(1,128)} %bitcast.34, s32[16,128]{1,0:T(8,128)} %bitcast.29), custom_call_target="tpu_custom_call" | custom-call | tf_op jit(solution)/shard_map/pallas_call | solution.py:396
  2.1 0.0 copy-start
  2.1 0.0 copy-start.3
  2.1 0.0 copy-start.4
  2.1 0.0 copy-start.5
  2.1 14.0 %all-to-all-start = ((f32[16,8,128]{2,1,0:T(8,128)}), f32[16,8,128]{2,1,0:T(8,128)S(1)}, u32[]{:S(2)}, u32[]{:S(2)}) async-start(f32[16,8,128]{2,1,0:T(8,128)} %shard_map.167.rup_ref), calls=%async_computation | async-start | bytes 131072 | tf_op jit(solution)/shard_map/all_to_all | solution.py:430
  16.1 0.0 copy-start.8
  16.1 0.0 copy-start.9
  16.1 0.0 copy-done
  16.2 0.0 copy-done.3
  16.2 0.0 copy-done.4
  16.2 0.0 copy-done.5
  16.2 0.6 copy-done.8
  16.8 0.0 copy-done.9
  16.8 1.0 %shard_map.168 = (f32[8,128]{1,0:T(8,128)S(1)}, f32[64,8,128]{2,1,0:T(8,128)S(1)}) custom-call(f32[16,8,128]{2,1,0:T(8,128)S(1)} %copy-done, f32[32,128]{1,0:T(8,128)S(1)} %bitcast.21, f32[32,128]{1,0:T(8,128)S(1)} %bitcast.22, f32[32,128]{1,0:T(8,128)S(1)} %bitcast.23, f32[1,64]{1,0:T(1,128)S(1)} %bitcast.26, f32[1,64]{1,0:T(1,128)S(1)} %bitcast.27), custom_call_target="tpu_custom_call" | custom-call | tf_op jit(solution)/shard_map/pallas_call | solution.py:411
  17.8 9.0 %all-to-all-done.rup_ref = f32[16,8,128]{2,1,0:T(8,128)S(1)} async-done(((f32[16,8,128]{2,1,0:T(8,128)}), f32[16,8,128]{2,1,0:T(8,128)S(1)}, u32[]{:S(2)}, u32[]{:S(2)}) %all-to-all-start) | async-done | bytes 65568 | tf_op jit(solution)/shard_map/all_to_all | solution.py:430
  26.8 10.7 %shard_map.169 = (f32[72,128]{1,0:T(8,128)S(1)}, f32[72,128]{1,0:T(8,128)S(1)}, f32[72,128]{1,0:T(8,128)S(1)}, f32[72,128]{1,0:T(8,128)S(1)}) custom-call(f32[8,128]{1,0:T(8,128)S(1)} %get-tuple-element.14.own_ref, f32[64,8,128]{2,1,0:T(8,128)S(1)} %get-tuple-element.15.sums_ref, f32[16,8,128]{2,1,0:T(8,128)S(1)} %all-to-all-done.rup_ref), custom_call_target="tpu_custom_call" | custom-call | tf_op jit(solution)/shard_map/pallas_call | solution.py:434
  37.5 0.1 collective-permute-start
  37.6 2.7 %collective-permute-start.1 = (f32[72,128]{1,0:T(8,128)S(1)}, f32[72,128]{1,0:T(8,128)S(1)}, u32[]{:S(2)}, u32[]{:S(2)}) collective-permute-start(f32[72,128]{1,0:T(8,128)S(1)} %get-tuple-element.18), channel_id=1, source_target_pairs={{0,16},{16,0},{32,48},{48,32},{64,80},{80,64},{96,112},{112,96},{1... | collective-permute-start | bytes 110600 | tf_op jit(solution)/shard_map/ppermute | solution.py:445
  40.3 2.9 %collective-permute-start.2 = (f32[72,128]{1,0:T(8,128)S(1)}, f32[72,128]{1,0:T(8,128)S(1)}, u32[]{:S(2)}, u32[]{:S(2)}) collective-permute-start(f32[72,128]{1,0:T(8,128)S(1)} %get-tuple-element.19), channel_id=1, source_target_pairs={{0,48},{16,32},{32,16},{48,0},{64,112},{80,96},{96,80},{112,64},{1... | collective-permute-start | bytes 110600 | tf_op jit(solution)/shard_map/ppermute | solution.py:445
  43.2 1.8 %collective-permute-done.refs_1_ = f32[72,128]{1,0:T(8,128)S(1)} collective-permute-done((f32[72,128]{1,0:T(8,128)S(1)}, f32[72,128]{1,0:T(8,128)S(1)}, u32[]{:S(2)}, u32[]{:S(2)}) %collective-permute-start) | collective-permute-done | bytes 36896 | tf_op jit(solution)/shard_map/ppermute | solution.py:445
  45.1 0.0 collective-permute-done.1.refs_2_
  45.1 0.6 collective-permute-done.2.refs_3_
  45.8 0.1 collective-permute-start.3
  45.9 0.6 collective-permute-start.4
  46.5 2.6 %collective-permute-start.5 = (f32[264,128]{1,0:T(8,128)S(1)}, f32[264,128]{1,0:T(8,128)S(1)}, u32[]{:S(2)}, u32[]{:S(2)}) collective-permute-start(f32[264,128]{1,0:T(8,128)S(1)} %get-tuple-element.23), channel_id=1, source_target_pairs={{0,192},{16,208},{32,224},{48,240},{64,128},{80,144},{96,160},{112... | collective-permute-start | bytes 405512 | tf_op jit(solution)/shard_map/ppermute | solution.py:454
  49.1 2.2 %collective-permute-done.3.refs_1_ = f32[264,128]{1,0:T(8,128)S(1)} collective-permute-done((f32[264,128]{1,0:T(8,128)S(1)}, f32[264,128]{1,0:T(8,128)S(1)}, u32[]{:S(2)}, u32[]{:S(2)}) %collective-permute-start.3) | collective-permute-done | bytes 135200 | tf_op jit(solution)/shard_map/ppermute | solution.py:454
  51.3 0.0 collective-permute-done.4.refs_2_
  51.3 2.2 %collective-permute-done.5.refs_3_ = f32[264,128]{1,0:T(8,128)S(1)} collective-permute-done((f32[264,128]{1,0:T(8,128)S(1)}, f32[264,128]{1,0:T(8,128)S(1)}, u32[]{:S(2)}, u32[]{:S(2)}) %collective-permute-start.5) | collective-permute-done | bytes 135200 | tf_op jit(solution)/shard_map/ppermute | solution.py:454
  53.5 0.0 copy-start.1
  53.5 2.1 %shard_map.172 = f32[16,32,128]{2,1,0:T(8,128)} custom-call(f32[264,128]{1,0:T(8,128)S(1)} %get-tuple-element.20.refs_0_, f32[264,128]{1,0:T(8,128)S(1)} %collective-permute-done.3.refs_1_, f32[264,128]{1,0:T(8,128)S(1)} %collective-permute-done.4.refs_2_, f32[264,128]{1,0:T(8,128)S(1)} %collective-permute-done.5.refs_3_), custom_call_target="tpu_custom_call" | custom-call | tf_op jit(solution)/shard_map/pallas_call | solution.py:465
  55.6 0.0 copy-start.2
  55.6 0.0 copy-start.6
  55.6 6.5 %all-to-all-start.1 = ((f32[16,32,128]{2,1,0:T(8,128)}), f32[16,32,128]{2,1,0:T(8,128)S(1)}, u32[]{:S(2)}, u32[]{:S(2)}) async-start(f32[16,32,128]{2,1,0:T(8,128)} %shard_map.172), calls=%async_computation.1 | async-start | bytes 524288 | tf_op jit(solution)/shard_map/all_to_all | solution.py:473
  62.1 0.0 copy-start.10
  62.1 0.0 copy-done.1
  62.1 0.0 copy-done.2
  62.1 0.0 copy-done.6
  62.1 0.6 copy-done.10
  62.7 0.7 shard_map.173
  63.4 0.0 copy-start.7
  63.4 0.9 %shard_map.171 = f32[32,4096]{1,0:T(8,128)} custom-call(f32[264,128]{1,0:T(8,128)S(1)} %get-tuple-element.20.refs_0_, f32[264,128]{1,0:T(8,128)S(1)} %collective-permute-done.3.refs_1_, f32[264,128]{1,0:T(8,128)S(1)} %collective-permute-done.4.refs_2_, f32[264,128]{1,0:T(8,128)S(1)} %collective-permute-done.5.refs_3_), custom_call_target="tpu_custom_call" | custom-call | tf_op jit(solution)/shard_map/pallas_call | solution.py:458
  64.3 5.0 %all-to-all-done.1.curves_ref = f32[16,32,128]{2,1,0:T(8,128)S(1)} async-done(((f32[16,32,128]{2,1,0:T(8,128)}), f32[16,32,128]{2,1,0:T(8,128)S(1)}, u32[]{:S(2)}, u32[]{:S(2)}) %all-to-all-start.1) | async-done | bytes 262176 | tf_op jit(solution)/shard_map/all_to_all | solution.py:473
  69.3 0.0 copy-done.7
  69.3 2.2 %shard_map.174 = f32[32,2048]{1,0:T(8,128)} custom-call(f32[16,32,128]{2,1,0:T(8,128)S(1)} %all-to-all-done.1.curves_ref, s32[16,128]{1,0:T(8,128)S(1)} %bitcast.20, s32[16,128]{1,0:T(8,128)S(1)} %get-tuple-element.24.slot_ref, s32[16,128]{1,0:T(8,128)S(1)} %bitcast.25, bf16[1024,256]{1,0:T(8,128)(2,1)S(1)} %get-tuple-element.25.split_ref), custom_call_target="tpu_custom_call" | custom-call | tf_op jit(solution)/shard_map/pallas_call | solution.py:485
  (1 shorter events, 0.0 us)
Async XLA Ops:
  2.1 14.1 %copy-start = (f32[16,8,128]{2,1,0:T(8,128)S(1)}, f32[16,8,128]{2,1,0:T(8,128)}, u32[]{:S(2)}) copy-start(f32[16,8,128]{2,1,0:T(8,128)} %shard_map.167.rup_ref) | copy-start | bytes 196612
  2.1 14.1 %copy-start.3 = (f32[4096]{0:T(1024)S(1)}, f32[4096]{0:T(1024)}, u32[]{:S(2)}) copy-start(f32[4096]{0:T(1024)} %param.16) | copy-start | bytes 49156
  2.1 14.1 %copy-start.4 = (f32[4096]{0:T(1024)S(1)}, f32[4096]{0:T(1024)}, u32[]{:S(2)}) copy-start(f32[4096]{0:T(1024)} %param.17) | copy-start | bytes 49156
  2.1 14.1 %copy-start.5 = (f32[4096]{0:T(1024)S(1)}, f32[4096]{0:T(1024)}, u32[]{:S(2)}) copy-start(f32[4096]{0:T(1024)} %param.18) | copy-start | bytes 49156
  2.1 24.7 %all-to-all-start = ((f32[16,8,128]{2,1,0:T(8,128)}), f32[16,8,128]{2,1,0:T(8,128)S(1)}, u32[]{:S(2)}, u32[]{:S(2)}) async-start(f32[16,8,128]{2,1,0:T(8,128)} %shard_map.167.rup_ref), calls=%async_computation | async-start | bytes 131072 | tf_op jit(solution)/shard_map/all_to_all | solution.py:430
  16.1 0.7 copy-start.8
  16.1 0.7 copy-start.9
  37.5 7.6 %collective-permute-start = (f32[72,128]{1,0:T(8,128)S(1)}, f32[72,128]{1,0:T(8,128)S(1)}, u32[]{:S(2)}, u32[]{:S(2)}) collective-permute-start(f32[72,128]{1,0:T(8,128)S(1)} %get-tuple-element.17), channel_id=1, source_target_pairs={{0,32},{16,48},{32,0},{48,16},{64,96},{80,112},{96,64},{112,80},{1... | collective-permute-start | bytes 110600 | tf_op jit(solution)/shard_map/ppermute | solution.py:445
  37.6 7.5 %collective-permute-start.1 = (f32[72,128]{1,0:T(8,128)S(1)}, f32[72,128]{1,0:T(8,128)S(1)}, u32[]{:S(2)}, u32[]{:S(2)}) collective-permute-start(f32[72,128]{1,0:T(8,128)S(1)} %get-tuple-element.18), channel_id=1, source_target_pairs={{0,16},{16,0},{32,48},{48,32},{64,80},{80,64},{96,112},{112,96},{1... | collective-permute-start | bytes 110600 | tf_op jit(solution)/shard_map/ppermute | solution.py:445
  40.3 5.4 %collective-permute-start.2 = (f32[72,128]{1,0:T(8,128)S(1)}, f32[72,128]{1,0:T(8,128)S(1)}, u32[]{:S(2)}, u32[]{:S(2)}) collective-permute-start(f32[72,128]{1,0:T(8,128)S(1)} %get-tuple-element.19), channel_id=1, source_target_pairs={{0,48},{16,32},{32,16},{48,0},{64,112},{80,96},{96,80},{112,64},{1... | collective-permute-start | bytes 110600 | tf_op jit(solution)/shard_map/ppermute | solution.py:445
  45.8 5.6 %collective-permute-start.3 = (f32[264,128]{1,0:T(8,128)S(1)}, f32[264,128]{1,0:T(8,128)S(1)}, u32[]{:S(2)}, u32[]{:S(2)}) collective-permute-start(f32[264,128]{1,0:T(8,128)S(1)} %get-tuple-element.21), channel_id=1, source_target_pairs={{0,128},{16,144},{32,160},{48,176},{64,192},{80,208},{96,224},{112... | collective-permute-start | bytes 405512 | tf_op jit(solution)/shard_map/ppermute | solution.py:454
  45.9 5.5 %collective-permute-start.4 = (f32[264,128]{1,0:T(8,128)S(1)}, f32[264,128]{1,0:T(8,128)S(1)}, u32[]{:S(2)}, u32[]{:S(2)}) collective-permute-start(f32[264,128]{1,0:T(8,128)S(1)} %get-tuple-element.22), channel_id=1, source_target_pairs={{0,64},{16,80},{32,96},{48,112},{64,0},{80,16},{96,32},{112,48},{1... | collective-permute-start | bytes 405512 | tf_op jit(solution)/shard_map/ppermute | solution.py:454
  46.5 7.0 %collective-permute-start.5 = (f32[264,128]{1,0:T(8,128)S(1)}, f32[264,128]{1,0:T(8,128)S(1)}, u32[]{:S(2)}, u32[]{:S(2)}) collective-permute-start(f32[264,128]{1,0:T(8,128)S(1)} %get-tuple-element.23), channel_id=1, source_target_pairs={{0,192},{16,208},{32,224},{48,240},{64,128},{80,144},{96,160},{112... | collective-permute-start | bytes 405512 | tf_op jit(solution)/shard_map/ppermute | solution.py:454
  53.5 8.6 %copy-start.1 = (f32[128,32,32]{0,2,1:T(8,128)S(1)}, f32[128,32,32]{0,2,1:T(8,128)}, u32[]{:S(2)}) copy-start(f32[128,32,32]{0,2,1:T(8,128)} %param.31) | copy-start | bytes 1572868
  55.6 6.5 %copy-start.2 = (s32[2048]{0:T(1024)S(1)}, s32[2048]{0:T(1024)}, u32[]{:S(2)}) copy-start(s32[2048]{0:T(1024)} %param.28) | copy-start | bytes 24580
  55.6 6.5 %copy-start.6 = (s32[2048]{0:T(1024)S(1)}, s32[2048]{0:T(1024)}, u32[]{:S(2)}) copy-start(s32[2048]{0:T(1024)} %param.29) | copy-start | bytes 24580
  55.6 13.7 %all-to-all-start.1 = ((f32[16,32,128]{2,1,0:T(8,128)}), f32[16,32,128]{2,1,0:T(8,128)S(1)}, u32[]{:S(2)}, u32[]{:S(2)}) async-start(f32[16,32,128]{2,1,0:T(8,128)} %shard_map.172), calls=%async_computation.1 | async-start | bytes 524288 | tf_op jit(solution)/shard_map/all_to_all | solution.py:473
  62.1 0.7 copy-start.10
  63.4 5.8 %copy-start.7 = (s32[2048]{0:T(1024)S(1)}, s32[2048]{0:T(1024)}, u32[]{:S(2)}) copy-start(s32[2048]{0:T(1024)} %param.30) | copy-start | bytes 24580

commit v8 on v7

--- a/solution.py
+++ b/solution.py
@@ -44,7 +44,17 @@
     return high, middle, (rest - middle.astype(jnp.float32)).astype(jnp.bfloat16)
 
 
-def pack_kernel(x_ref, y_ref, mag_ref, rate_ref, source_ref, relay_ref, out_ref):
+def pack_kernel(*refs):
+    count = 6
+    out_ref, semaphores = refs[count], refs[-1]
+    x_ref, y_ref, mag_ref, rate_ref, source_ref, relay_ref = refs[count + 1 : -1]
+    copies = [
+        pltpu.make_async_copy(refs[i], refs[count + 1 + i], semaphores.at[i]) for i in range(count)
+    ]
+    for copy in copies:
+        copy.start()
+    for copy in copies:
+        copy.wait()
     row, site = place()
     source = source_ref[...].astype(jnp.float32)
     zero = jnp.zeros((1, LANES), jnp.float32)
@@ -396,8 +406,14 @@
     packed = pl.pallas_call(
         pack_kernel,
         out_shape=jax.ShapeDtypeStruct((rows, SUBLANES, LANES), jnp.float32),
-        in_specs=[VMEM] * 6,
+        in_specs=[pl.BlockSpec(memory_space=pltpu.HBM)] * 6,
         out_specs=VMEM,
+        scratch_shapes=[pltpu.VMEM((1, LANES), jnp.float32)] * 4
+        + [
+            pltpu.VMEM((1, LANES), jnp.int32),
+            pltpu.VMEM((columns, capacity), jnp.int32),
+            pltpu.SemaphoreType.DMA((6,)),
+        ],
     )(
         line(rup_x),
         line(rup_y),

time: 71.9 us -> 72 us (level)
  no operation moved by 1% of the time
where the time goes in v8:
time: 72 us; the launch traced here: 71.6 us
  starting transfers between devices  29.6 us (41%)
  waiting for transfers between devices  20.8 us (29%)
  Pallas kernels  19.1 us (27%)
  local copies, waits for them, and re-layouts  1.28 us (2%)
  between operations  0.82 us (1%)
    all_to_all x1, starting transfers between devices, per_device(): lax.all_to_all(packed, ('rup', 'site'), 0, 0, axis_index_groups=groups, t...  14 us
    pallas_call x1, Pallas kernels, per_device(): pl.pallas_call(functools.partial(hazard_kernel, levels), out_shape=(copy,...  10.7 us
    all_to_all x1, waiting for transfers between devices, per_device(): lax.all_to_all(packed, ('rup', 'site'), 0, 0, axis_index_groups=groups, t...  9.01 us
    all_to_all x1, starting transfers between devices, per_device(): curves = lax.all_to_all(send, 'site', 0, 0, tiled=True)  6.51 us
    ppermute x3, starting transfers between devices, per_device(): lax.ppermute(copies[k], 'rup', [(r, r ^ k) for r in range(rows)])  5.74 us
    all_to_all x1, waiting for transfers between devices, per_device(): curves = lax.all_to_all(send, 'site', 0, 0, tiled=True)  4.98 us
    ppermute x3, waiting for transfers between devices, per_device(): lax.ppermute(merged[k], 'rup', [(r, r ^ k * heights) for r in range(rows)])  4.36 us
    ppermute x3, starting transfers between devices, per_device(): lax.ppermute(merged[k], 'rup', [(r, r ^ k * heights) for r in range(rows)])  3.33 us
  transfers between devices with their start and end apart: 8, of which 6 were waited for; matrix products, arithmetic and copies ran while one was open for 0% of the time, Pallas kernels for 4%

profile of v8, /device:TPU:1, one launch (start us, length us, event | category | flops | bytes accessed | tf_op | source)
XLA Modules:
  0.0 71.6 jit_solution(13827454397141105274)
XLA Ops:
  0.6 1.5 %shard_map.167.rup_ref = f32[16,8,128]{2,1,0:T(8,128)} custom-call(f32[1,128]{1,0:T(1,128)} %bitcast.30, f32[1,128]{1,0:T(1,128)} %bitcast.31, f32[1,128]{1,0:T(1,128)} %bitcast.32, f32[1,128]{1,0:T(1,128)} %bitcast.33, s32[1,128]{1,0:T(1,128)} %bitcast.34, s32[16,128]{1,0:T(8,128)} %bitcast.29), custom_call_target="tpu_custom_call" | custom-call | tf_op jit(solution)/shard_map/pallas_call | solution.py:406
  2.1 0.0 copy-start
  2.1 0.0 copy-start.3
  2.1 0.0 copy-start.4
  2.2 0.0 copy-start.5
  2.2 14.0 %all-to-all-start = ((f32[16,8,128]{2,1,0:T(8,128)}), f32[16,8,128]{2,1,0:T(8,128)S(1)}, u32[]{:S(2)}, u32[]{:S(2)}) async-start(f32[16,8,128]{2,1,0:T(8,128)} %shard_map.167.rup_ref), calls=%async_computation | async-start | bytes 131072 | tf_op jit(solution)/shard_map/all_to_all | solution.py:446
  16.2 0.0 copy-start.8
  16.2 0.0 copy-start.9
  16.2 0.0 copy-done
  16.2 0.0 copy-done.3
  16.2 0.0 copy-done.4
  16.3 0.0 copy-done.5
  16.3 0.6 copy-done.8
  16.9 0.0 copy-done.9
  16.9 1.0 %shard_map.168 = (f32[8,128]{1,0:T(8,128)S(1)}, f32[64,8,128]{2,1,0:T(8,128)S(1)}) custom-call(f32[16,8,128]{2,1,0:T(8,128)S(1)} %copy-done, f32[32,128]{1,0:T(8,128)S(1)} %bitcast.21, f32[32,128]{1,0:T(8,128)S(1)} %bitcast.22, f32[32,128]{1,0:T(8,128)S(1)} %bitcast.23, f32[1,64]{1,0:T(1,128)S(1)} %bitcast.26, f32[1,64]{1,0:T(1,128)S(1)} %bitcast.27), custom_call_target="tpu_custom_call" | custom-call | tf_op jit(solution)/shard_map/pallas_call | solution.py:427
  17.9 9.0 %all-to-all-done.rup_ref = f32[16,8,128]{2,1,0:T(8,128)S(1)} async-done(((f32[16,8,128]{2,1,0:T(8,128)}), f32[16,8,128]{2,1,0:T(8,128)S(1)}, u32[]{:S(2)}, u32[]{:S(2)}) %all-to-all-start) | async-done | bytes 65568 | tf_op jit(solution)/shard_map/all_to_all | solution.py:446
  26.9 10.7 %shard_map.169 = (f32[72,128]{1,0:T(8,128)S(1)}, f32[72,128]{1,0:T(8,128)S(1)}, f32[72,128]{1,0:T(8,128)S(1)}, f32[72,128]{1,0:T(8,128)S(1)}) custom-call(f32[8,128]{1,0:T(8,128)S(1)} %get-tuple-element.14.own_ref, f32[64,8,128]{2,1,0:T(8,128)S(1)} %get-tuple-element.15.sums_ref, f32[16,8,128]{2,1,0:T(8,128)S(1)} %all-to-all-done.rup_ref), custom_call_target="tpu_custom_call" | custom-call | tf_op jit(solution)/shard_map/pallas_call | solution.py:450
  37.6 0.1 collective-permute-start
  37.7 2.7 %collective-permute-start.1 = (f32[72,128]{1,0:T(8,128)S(1)}, f32[72,128]{1,0:T(8,128)S(1)}, u32[]{:S(2)}, u32[]{:S(2)}) collective-permute-start(f32[72,128]{1,0:T(8,128)S(1)} %get-tuple-element.18), channel_id=1, source_target_pairs={{0,16},{16,0},{32,48},{48,32},{64,80},{80,64},{96,112},{112,96},{1... | collective-permute-start | bytes 110600 | tf_op jit(solution)/shard_map/ppermute | solution.py:461
  40.4 2.9 %collective-permute-start.2 = (f32[72,128]{1,0:T(8,128)S(1)}, f32[72,128]{1,0:T(8,128)S(1)}, u32[]{:S(2)}, u32[]{:S(2)}) collective-permute-start(f32[72,128]{1,0:T(8,128)S(1)} %get-tuple-element.19), channel_id=1, source_target_pairs={{0,48},{16,32},{32,16},{48,0},{64,112},{80,96},{96,80},{112,64},{1... | collective-permute-start | bytes 110600 | tf_op jit(solution)/shard_map/ppermute | solution.py:461
  43.3 1.8 %collective-permute-done.refs_1_ = f32[72,128]{1,0:T(8,128)S(1)} collective-permute-done((f32[72,128]{1,0:T(8,128)S(1)}, f32[72,128]{1,0:T(8,128)S(1)}, u32[]{:S(2)}, u32[]{:S(2)}) %collective-permute-start) | collective-permute-done | bytes 36896 | tf_op jit(solution)/shard_map/ppermute | solution.py:461
  45.2 0.0 collective-permute-done.1.refs_2_
  45.2 0.6 collective-permute-done.2.refs_3_
  45.8 0.1 collective-permute-start.3
  45.9 0.6 collective-permute-start.4
  46.6 2.6 %collective-permute-start.5 = (f32[264,128]{1,0:T(8,128)S(1)}, f32[264,128]{1,0:T(8,128)S(1)}, u32[]{:S(2)}, u32[]{:S(2)}) collective-permute-start(f32[264,128]{1,0:T(8,128)S(1)} %get-tuple-element.23), channel_id=1, source_target_pairs={{0,192},{16,208},{32,224},{48,240},{64,128},{80,144},{96,160},{112... | collective-permute-start | bytes 405512 | tf_op jit(solution)/shard_map/ppermute | solution.py:470
  49.2 2.2 %collective-permute-done.3.refs_1_ = f32[264,128]{1,0:T(8,128)S(1)} collective-permute-done((f32[264,128]{1,0:T(8,128)S(1)}, f32[264,128]{1,0:T(8,128)S(1)}, u32[]{:S(2)}, u32[]{:S(2)}) %collective-permute-start.3) | collective-permute-done | bytes 135200 | tf_op jit(solution)/shard_map/ppermute | solution.py:470
  51.4 0.0 collective-permute-done.4.refs_2_
  51.4 2.1 %collective-permute-done.5.refs_3_ = f32[264,128]{1,0:T(8,128)S(1)} collective-permute-done((f32[264,128]{1,0:T(8,128)S(1)}, f32[264,128]{1,0:T(8,128)S(1)}, u32[]{:S(2)}, u32[]{:S(2)}) %collective-permute-start.5) | collective-permute-done | bytes 135200 | tf_op jit(solution)/shard_map/ppermute | solution.py:470
  53.5 0.0 copy-start.1
  53.5 2.1 %shard_map.172 = f32[16,32,128]{2,1,0:T(8,128)} custom-call(f32[264,128]{1,0:T(8,128)S(1)} %get-tuple-element.20.refs_0_, f32[264,128]{1,0:T(8,128)S(1)} %collective-permute-done.3.refs_1_, f32[264,128]{1,0:T(8,128)S(1)} %collective-permute-done.4.refs_2_, f32[264,128]{1,0:T(8,128)S(1)} %collective-permute-done.5.refs_3_), custom_call_target="tpu_custom_call" | custom-call | tf_op jit(solution)/shard_map/pallas_call | solution.py:481
  55.7 0.0 copy-start.2
  55.7 0.0 copy-start.6
  55.7 6.5 %all-to-all-start.1 = ((f32[16,32,128]{2,1,0:T(8,128)}), f32[16,32,128]{2,1,0:T(8,128)S(1)}, u32[]{:S(2)}, u32[]{:S(2)}) async-start(f32[16,32,128]{2,1,0:T(8,128)} %shard_map.172), calls=%async_computation.1 | async-start | bytes 524288 | tf_op jit(solution)/shard_map/all_to_all | solution.py:489
  62.2 0.0 copy-start.10
  62.2 0.0 copy-done.1
  62.2 0.0 copy-done.2
  62.2 0.0 copy-done.6
  62.2 0.6 copy-done.10
  62.8 0.7 shard_map.173
  63.5 0.0 copy-start.7
  63.5 0.9 %shard_map.171 = f32[32,4096]{1,0:T(8,128)} custom-call(f32[264,128]{1,0:T(8,128)S(1)} %get-tuple-element.20.refs_0_, f32[264,128]{1,0:T(8,128)S(1)} %collective-permute-done.3.refs_1_, f32[264,128]{1,0:T(8,128)S(1)} %collective-permute-done.4.refs_2_, f32[264,128]{1,0:T(8,128)S(1)} %collective-permute-done.5.refs_3_), custom_call_target="tpu_custom_call" | custom-call | tf_op jit(solution)/shard_map/pallas_call | solution.py:474
  64.4 5.0 %all-to-all-done.1.curves_ref = f32[16,32,128]{2,1,0:T(8,128)S(1)} async-done(((f32[16,32,128]{2,1,0:T(8,128)}), f32[16,32,128]{2,1,0:T(8,128)S(1)}, u32[]{:S(2)}, u32[]{:S(2)}) %all-to-all-start.1) | async-done | bytes 262176 | tf_op jit(solution)/shard_map/all_to_all | solution.py:489
  69.4 0.0 copy-done.7
  69.4 2.2 %shard_map.174 = f32[32,2048]{1,0:T(8,128)} custom-call(f32[16,32,128]{2,1,0:T(8,128)S(1)} %all-to-all-done.1.curves_ref, s32[16,128]{1,0:T(8,128)S(1)} %bitcast.20, s32[16,128]{1,0:T(8,128)S(1)} %get-tuple-element.24.slot_ref, s32[16,128]{1,0:T(8,128)S(1)} %bitcast.25, bf16[1024,256]{1,0:T(8,128)(2,1)S(1)} %get-tuple-element.25.split_ref), custom_call_target="tpu_custom_call" | custom-call | tf_op jit(solution)/shard_map/pallas_call | solution.py:501
  (1 shorter events, 0.0 us)
Async XLA Ops:
  2.1 14.1 %copy-start = (f32[16,8,128]{2,1,0:T(8,128)S(1)}, f32[16,8,128]{2,1,0:T(8,128)}, u32[]{:S(2)}) copy-start(f32[16,8,128]{2,1,0:T(8,128)} %shard_map.167.rup_ref) | copy-start | bytes 196612
  2.1 14.1 %copy-start.3 = (f32[4096]{0:T(1024)S(1)}, f32[4096]{0:T(1024)}, u32[]{:S(2)}) copy-start(f32[4096]{0:T(1024)} %param.16) | copy-start | bytes 49156
  2.1 14.1 %copy-start.4 = (f32[4096]{0:T(1024)S(1)}, f32[4096]{0:T(1024)}, u32[]{:S(2)}) copy-start(f32[4096]{0:T(1024)} %param.17) | copy-start | bytes 49156
  2.2 14.1 %copy-start.5 = (f32[4096]{0:T(1024)S(1)}, f32[4096]{0:T(1024)}, u32[]{:S(2)}) copy-start(f32[4096]{0:T(1024)} %param.18) | copy-start | bytes 49156
  2.2 24.7 %all-to-all-start = ((f32[16,8,128]{2,1,0:T(8,128)}), f32[16,8,128]{2,1,0:T(8,128)S(1)}, u32[]{:S(2)}, u32[]{:S(2)}) async-start(f32[16,8,128]{2,1,0:T(8,128)} %shard_map.167.rup_ref), calls=%async_computation | async-start | bytes 131072 | tf_op jit(solution)/shard_map/all_to_all | solution.py:446
  16.2 0.7 copy-start.8
  16.2 0.7 copy-start.9
  37.6 7.6 %collective-permute-start = (f32[72,128]{1,0:T(8,128)S(1)}, f32[72,128]{1,0:T(8,128)S(1)}, u32[]{:S(2)}, u32[]{:S(2)}) collective-permute-start(f32[72,128]{1,0:T(8,128)S(1)} %get-tuple-element.17), channel_id=1, source_target_pairs={{0,32},{16,48},{32,0},{48,16},{64,96},{80,112},{96,64},{112,80},{1... | collective-permute-start | bytes 110600 | tf_op jit(solution)/shard_map/ppermute | solution.py:461
  37.7 7.5 %collective-permute-start.1 = (f32[72,128]{1,0:T(8,128)S(1)}, f32[72,128]{1,0:T(8,128)S(1)}, u32[]{:S(2)}, u32[]{:S(2)}) collective-permute-start(f32[72,128]{1,0:T(8,128)S(1)} %get-tuple-element.18), channel_id=1, source_target_pairs={{0,16},{16,0},{32,48},{48,32},{64,80},{80,64},{96,112},{112,96},{1... | collective-permute-start | bytes 110600 | tf_op jit(solution)/shard_map/ppermute | solution.py:461
  40.4 5.4 %collective-permute-start.2 = (f32[72,128]{1,0:T(8,128)S(1)}, f32[72,128]{1,0:T(8,128)S(1)}, u32[]{:S(2)}, u32[]{:S(2)}) collective-permute-start(f32[72,128]{1,0:T(8,128)S(1)} %get-tuple-element.19), channel_id=1, source_target_pairs={{0,48},{16,32},{32,16},{48,0},{64,112},{80,96},{96,80},{112,64},{1... | collective-permute-start | bytes 110600 | tf_op jit(solution)/shard_map/ppermute | solution.py:461
  45.8 5.6 %collective-permute-start.3 = (f32[264,128]{1,0:T(8,128)S(1)}, f32[264,128]{1,0:T(8,128)S(1)}, u32[]{:S(2)}, u32[]{:S(2)}) collective-permute-start(f32[264,128]{1,0:T(8,128)S(1)} %get-tuple-element.21), channel_id=1, source_target_pairs={{0,128},{16,144},{32,160},{48,176},{64,192},{80,208},{96,224},{112... | collective-permute-start | bytes 405512 | tf_op jit(solution)/shard_map/ppermute | solution.py:470
  45.9 5.5 %collective-permute-start.4 = (f32[264,128]{1,0:T(8,128)S(1)}, f32[264,128]{1,0:T(8,128)S(1)}, u32[]{:S(2)}, u32[]{:S(2)}) collective-permute-start(f32[264,128]{1,0:T(8,128)S(1)} %get-tuple-element.22), channel_id=1, source_target_pairs={{0,64},{16,80},{32,96},{48,112},{64,0},{80,16},{96,32},{112,48},{1... | collective-permute-start | bytes 405512 | tf_op jit(solution)/shard_map/ppermute | solution.py:470
  46.6 7.0 %collective-permute-start.5 = (f32[264,128]{1,0:T(8,128)S(1)}, f32[264,128]{1,0:T(8,128)S(1)}, u32[]{:S(2)}, u32[]{:S(2)}) collective-permute-start(f32[264,128]{1,0:T(8,128)S(1)} %get-tuple-element.23), channel_id=1, source_target_pairs={{0,192},{16,208},{32,224},{48,240},{64,128},{80,144},{96,160},{112... | collective-permute-start | bytes 405512 | tf_op jit(solution)/shard_map/ppermute | solution.py:470
  53.5 8.7 %copy-start.1 = (f32[128,32,32]{0,2,1:T(8,128)S(1)}, f32[128,32,32]{0,2,1:T(8,128)}, u32[]{:S(2)}) copy-start(f32[128,32,32]{0,2,1:T(8,128)} %param.31) | copy-start | bytes 1572868
  55.7 6.5 %copy-start.2 = (s32[2048]{0:T(1024)S(1)}, s32[2048]{0:T(1024)}, u32[]{:S(2)}) copy-start(s32[2048]{0:T(1024)} %param.28) | copy-start | bytes 24580
  55.7 6.5 %copy-start.6 = (s32[2048]{0:T(1024)S(1)}, s32[2048]{0:T(1024)}, u32[]{:S(2)}) copy-start(s32[2048]{0:T(1024)} %param.29) | copy-start | bytes 24580
  55.7 13.7 %all-to-all-start.1 = ((f32[16,32,128]{2,1,0:T(8,128)}), f32[16,32,128]{2,1,0:T(8,128)S(1)}, u32[]{:S(2)}, u32[]{:S(2)}) async-start(f32[16,32,128]{2,1,0:T(8,128)} %shard_map.172), calls=%async_computation.1 | async-start | bytes 524288 | tf_op jit(solution)/shard_map/all_to_all | solution.py:489
  62.2 0.7 copy-start.10
  63.5 5.8 %copy-start.7 = (s32[2048]{0:T(1024)S(1)}, s32[2048]{0:T(1024)}, u32[]{:S(2)}) copy-start(s32[2048]{0:T(1024)} %param.30) | copy-start | bytes 24580

commit v9 on v7

--- a/solution.py
+++ b/solution.py
@@ -12,7 +12,7 @@
 SUBLANES = 8
 LIST = 5
 FAR_FIRST = (0, 2, 1, 3)
-UNROLL = 24
+UNROLL = 48
 PRODUCTS = 2
 VMEM = pl.BlockSpec(memory_space=pltpu.VMEM)
 SMEM = pl.BlockSpec(memory_space=pltpu.SMEM)

time: 71.9 us -> 72.3 us (level)
  transfers between devices with their start and end apart: 8 -> 8, of which waited for: 6 -> 6; matrix products, arithmetic and copies ran while one was open for 0% -> 0% of each run, Pallas kernels for 4% -> 3%
where the time goes in v9:
time: 72.3 us; the launch traced here: 71.9 us
  starting transfers between devices  29.6 us (41%)
  waiting for transfers between devices  20.8 us (29%)
  Pallas kernels  19.4 us (27%)
  local copies, waits for them, and re-layouts  1.27 us (2%)
  between operations  0.79 us (1%)
    all_to_all x1, starting transfers between devices, per_device(): lax.all_to_all(packed, ('rup', 'site'), 0, 0, axis_index_groups=groups, t...  14 us
    pallas_call x1, Pallas kernels, per_device(): pl.pallas_call(functools.partial(hazard_kernel, levels), out_shape=(copy,...  11.1 us
    all_to_all x1, waiting for transfers between devices, per_device(): lax.all_to_all(packed, ('rup', 'site'), 0, 0, axis_index_groups=groups, t...  9 us
    all_to_all x1, starting transfers between devices, per_device(): curves = lax.all_to_all(send, 'site', 0, 0, tiled=True)  6.49 us
    ppermute x3, starting transfers between devices, per_device(): lax.ppermute(copies[k], 'rup', [(r, r ^ k) for r in range(rows)])  5.74 us
    all_to_all x1, waiting for transfers between devices, per_device(): curves = lax.all_to_all(send, 'site', 0, 0, tiled=True)  4.98 us
    ppermute x3, waiting for transfers between devices, per_device(): lax.ppermute(merged[k], 'rup', [(r, r ^ k * heights) for r in range(rows)])  4.37 us
    ppermute x3, starting transfers between devices, per_device(): lax.ppermute(merged[k], 'rup', [(r, r ^ k * heights) for r in range(rows)])  3.33 us
  transfers between devices with their start and end apart: 8, of which 6 were waited for; matrix products, arithmetic and copies ran while one was open for 0% of the time, Pallas kernels for 3%

profile of v9, /device:TPU:1, one launch (start us, length us, event | category | flops | bytes accessed | tf_op | source)
XLA Modules:
  0.0 71.9 jit_solution(5205664514853155455)
XLA Ops:
  0.6 1.4 %shard_map.167.rup_ref = f32[16,8,128]{2,1,0:T(8,128)} custom-call(f32[1,128]{1,0:T(1,128)} %bitcast.30, f32[1,128]{1,0:T(1,128)} %bitcast.31, f32[1,128]{1,0:T(1,128)} %bitcast.32, f32[1,128]{1,0:T(1,128)} %bitcast.33, s32[1,128]{1,0:T(1,128)} %bitcast.34, s32[16,128]{1,0:T(8,128)} %bitcast.29), custom_call_target="tpu_custom_call" | custom-call | tf_op jit(solution)/shard_map/pallas_call | solution.py:396
  2.1 0.0 copy-start
  2.1 0.0 copy-start.3
  2.1 0.0 copy-start.4
  2.1 0.0 copy-start.5
  2.1 14.0 %all-to-all-start = ((f32[16,8,128]{2,1,0:T(8,128)}), f32[16,8,128]{2,1,0:T(8,128)S(1)}, u32[]{:S(2)}, u32[]{:S(2)}) async-start(f32[16,8,128]{2,1,0:T(8,128)} %shard_map.167.rup_ref), calls=%async_computation | async-start | bytes 131072 | tf_op jit(solution)/shard_map/all_to_all | solution.py:430
  16.1 0.0 copy-start.8
  16.1 0.0 copy-start.9
  16.1 0.0 copy-done
  16.2 0.0 copy-done.3
  16.2 0.0 copy-done.4
  16.2 0.0 copy-done.5
  16.2 0.6 copy-done.8
  16.8 0.0 copy-done.9
  16.8 1.0 %shard_map.168 = (f32[8,128]{1,0:T(8,128)S(1)}, f32[64,8,128]{2,1,0:T(8,128)S(1)}) custom-call(f32[16,8,128]{2,1,0:T(8,128)S(1)} %copy-done, f32[32,128]{1,0:T(8,128)S(1)} %bitcast.21, f32[32,128]{1,0:T(8,128)S(1)} %bitcast.22, f32[32,128]{1,0:T(8,128)S(1)} %bitcast.23, f32[1,64]{1,0:T(1,128)S(1)} %bitcast.26, f32[1,64]{1,0:T(1,128)S(1)} %bitcast.27), custom_call_target="tpu_custom_call" | custom-call | tf_op jit(solution)/shard_map/pallas_call | solution.py:411
  17.8 9.0 %all-to-all-done.rup_ref = f32[16,8,128]{2,1,0:T(8,128)S(1)} async-done(((f32[16,8,128]{2,1,0:T(8,128)}), f32[16,8,128]{2,1,0:T(8,128)S(1)}, u32[]{:S(2)}, u32[]{:S(2)}) %all-to-all-start) | async-done | bytes 65568 | tf_op jit(solution)/shard_map/all_to_all | solution.py:430
  26.8 11.1 %shard_map.169 = (f32[72,128]{1,0:T(8,128)S(1)}, f32[72,128]{1,0:T(8,128)S(1)}, f32[72,128]{1,0:T(8,128)S(1)}, f32[72,128]{1,0:T(8,128)S(1)}) custom-call(f32[8,128]{1,0:T(8,128)S(1)} %get-tuple-element.14.own_ref, f32[64,8,128]{2,1,0:T(8,128)S(1)} %get-tuple-element.15.sums_ref, f32[16,8,128]{2,1,0:T(8,128)S(1)} %all-to-all-done.rup_ref), custom_call_target="tpu_custom_call" | custom-call | tf_op jit(solution)/shard_map/pallas_call | solution.py:434
  37.9 0.1 collective-permute-start
  38.0 2.7 %collective-permute-start.1 = (f32[72,128]{1,0:T(8,128)S(1)}, f32[72,128]{1,0:T(8,128)S(1)}, u32[]{:S(2)}, u32[]{:S(2)}) collective-permute-start(f32[72,128]{1,0:T(8,128)S(1)} %get-tuple-element.18), channel_id=1, source_target_pairs={{0,16},{16,0},{32,48},{48,32},{64,80},{80,64},{96,112},{112,96},{1... | collective-permute-start | bytes 110600 | tf_op jit(solution)/shard_map/ppermute | solution.py:445
  40.7 2.9 %collective-permute-start.2 = (f32[72,128]{1,0:T(8,128)S(1)}, f32[72,128]{1,0:T(8,128)S(1)}, u32[]{:S(2)}, u32[]{:S(2)}) collective-permute-start(f32[72,128]{1,0:T(8,128)S(1)} %get-tuple-element.19), channel_id=1, source_target_pairs={{0,48},{16,32},{32,16},{48,0},{64,112},{80,96},{96,80},{112,64},{1... | collective-permute-start | bytes 110600 | tf_op jit(solution)/shard_map/ppermute | solution.py:445
  43.6 1.8 %collective-permute-done.refs_1_ = f32[72,128]{1,0:T(8,128)S(1)} collective-permute-done((f32[72,128]{1,0:T(8,128)S(1)}, f32[72,128]{1,0:T(8,128)S(1)}, u32[]{:S(2)}, u32[]{:S(2)}) %collective-permute-start) | collective-permute-done | bytes 36896 | tf_op jit(solution)/shard_map/ppermute | solution.py:445
  45.5 0.0 collective-permute-done.1.refs_2_
  45.5 0.6 collective-permute-done.2.refs_3_
  46.1 0.1 collective-permute-start.3
  46.2 0.6 collective-permute-start.4
  46.9 2.6 %collective-permute-start.5 = (f32[264,128]{1,0:T(8,128)S(1)}, f32[264,128]{1,0:T(8,128)S(1)}, u32[]{:S(2)}, u32[]{:S(2)}) collective-permute-start(f32[264,128]{1,0:T(8,128)S(1)} %get-tuple-element.23), channel_id=1, source_target_pairs={{0,192},{16,208},{32,224},{48,240},{64,128},{80,144},{96,160},{112... | collective-permute-start | bytes 405512 | tf_op jit(solution)/shard_map/ppermute | solution.py:454
  49.5 2.2 %collective-permute-done.3.refs_1_ = f32[264,128]{1,0:T(8,128)S(1)} collective-permute-done((f32[264,128]{1,0:T(8,128)S(1)}, f32[264,128]{1,0:T(8,128)S(1)}, u32[]{:S(2)}, u32[]{:S(2)}) %collective-permute-start.3) | collective-permute-done | bytes 135200 | tf_op jit(solution)/shard_map/ppermute | solution.py:454
  51.7 0.0 collective-permute-done.4.refs_2_
  51.7 2.2 %collective-permute-done.5.refs_3_ = f32[264,128]{1,0:T(8,128)S(1)} collective-permute-done((f32[264,128]{1,0:T(8,128)S(1)}, f32[264,128]{1,0:T(8,128)S(1)}, u32[]{:S(2)}, u32[]{:S(2)}) %collective-permute-start.5) | collective-permute-done | bytes 135200 | tf_op jit(solution)/shard_map/ppermute | solution.py:454
  53.9 0.0 copy-start.1
  53.9 2.1 %shard_map.172 = f32[16,32,128]{2,1,0:T(8,128)} custom-call(f32[264,128]{1,0:T(8,128)S(1)} %get-tuple-element.20.refs_0_, f32[264,128]{1,0:T(8,128)S(1)} %collective-permute-done.3.refs_1_, f32[264,128]{1,0:T(8,128)S(1)} %collective-permute-done.4.refs_2_, f32[264,128]{1,0:T(8,128)S(1)} %collective-permute-done.5.refs_3_), custom_call_target="tpu_custom_call" | custom-call | tf_op jit(solution)/shard_map/pallas_call | solution.py:465
  56.0 0.0 copy-start.2
  56.0 0.0 copy-start.6
  56.0 6.5 %all-to-all-start.1 = ((f32[16,32,128]{2,1,0:T(8,128)}), f32[16,32,128]{2,1,0:T(8,128)S(1)}, u32[]{:S(2)}, u32[]{:S(2)}) async-start(f32[16,32,128]{2,1,0:T(8,128)} %shard_map.172), calls=%async_computation.1 | async-start | bytes 524288 | tf_op jit(solution)/shard_map/all_to_all | solution.py:473
  62.5 0.0 copy-start.10
  62.5 0.0 copy-done.1
  62.5 0.0 copy-done.2
  62.5 0.0 copy-done.6
  62.5 0.6 copy-done.10
  63.1 0.7 shard_map.173
  63.8 0.0 copy-start.7
  63.8 0.9 %shard_map.171 = f32[32,4096]{1,0:T(8,128)} custom-call(f32[264,128]{1,0:T(8,128)S(1)} %get-tuple-element.20.refs_0_, f32[264,128]{1,0:T(8,128)S(1)} %collective-permute-done.3.refs_1_, f32[264,128]{1,0:T(8,128)S(1)} %collective-permute-done.4.refs_2_, f32[264,128]{1,0:T(8,128)S(1)} %collective-permute-done.5.refs_3_), custom_call_target="tpu_custom_call" | custom-call | tf_op jit(solution)/shard_map/pallas_call | solution.py:458
  64.7 5.0 %all-to-all-done.1.curves_ref = f32[16,32,128]{2,1,0:T(8,128)S(1)} async-done(((f32[16,32,128]{2,1,0:T(8,128)}), f32[16,32,128]{2,1,0:T(8,128)S(1)}, u32[]{:S(2)}, u32[]{:S(2)}) %all-to-all-start.1) | async-done | bytes 262176 | tf_op jit(solution)/shard_map/all_to_all | solution.py:473
  69.7 0.0 copy-done.7
  69.7 2.2 %shard_map.174 = f32[32,2048]{1,0:T(8,128)} custom-call(f32[16,32,128]{2,1,0:T(8,128)S(1)} %all-to-all-done.1.curves_ref, s32[16,128]{1,0:T(8,128)S(1)} %bitcast.20, s32[16,128]{1,0:T(8,128)S(1)} %get-tuple-element.24.slot_ref, s32[16,128]{1,0:T(8,128)S(1)} %bitcast.25, bf16[1024,256]{1,0:T(8,128)(2,1)S(1)} %get-tuple-element.25.split_ref), custom_call_target="tpu_custom_call" | custom-call | tf_op jit(solution)/shard_map/pallas_call | solution.py:485
  (1 shorter events, 0.0 us)
Async XLA Ops:
  2.1 14.1 %copy-start = (f32[16,8,128]{2,1,0:T(8,128)S(1)}, f32[16,8,128]{2,1,0:T(8,128)}, u32[]{:S(2)}) copy-start(f32[16,8,128]{2,1,0:T(8,128)} %shard_map.167.rup_ref) | copy-start | bytes 196612
  2.1 14.1 %copy-start.3 = (f32[4096]{0:T(1024)S(1)}, f32[4096]{0:T(1024)}, u32[]{:S(2)}) copy-start(f32[4096]{0:T(1024)} %param.16) | copy-start | bytes 49156
  2.1 14.1 %copy-start.4 = (f32[4096]{0:T(1024)S(1)}, f32[4096]{0:T(1024)}, u32[]{:S(2)}) copy-start(f32[4096]{0:T(1024)} %param.17) | copy-start | bytes 49156
  2.1 14.1 %copy-start.5 = (f32[4096]{0:T(1024)S(1)}, f32[4096]{0:T(1024)}, u32[]{:S(2)}) copy-start(f32[4096]{0:T(1024)} %param.18) | copy-start | bytes 49156
  2.1 24.7 %all-to-all-start = ((f32[16,8,128]{2,1,0:T(8,128)}), f32[16,8,128]{2,1,0:T(8,128)S(1)}, u32[]{:S(2)}, u32[]{:S(2)}) async-start(f32[16,8,128]{2,1,0:T(8,128)} %shard_map.167.rup_ref), calls=%async_computation | async-start | bytes 131072 | tf_op jit(solution)/shard_map/all_to_all | solution.py:430
  16.1 0.7 copy-start.8
  16.1 0.7 copy-start.9
  37.9 7.6 %collective-permute-start = (f32[72,128]{1,0:T(8,128)S(1)}, f32[72,128]{1,0:T(8,128)S(1)}, u32[]{:S(2)}, u32[]{:S(2)}) collective-permute-start(f32[72,128]{1,0:T(8,128)S(1)} %get-tuple-element.17), channel_id=1, source_target_pairs={{0,32},{16,48},{32,0},{48,16},{64,96},{80,112},{96,64},{112,80},{1... | collective-permute-start | bytes 110600 | tf_op jit(solution)/shard_map/ppermute | solution.py:445
  38.0 7.5 %collective-permute-start.1 = (f32[72,128]{1,0:T(8,128)S(1)}, f32[72,128]{1,0:T(8,128)S(1)}, u32[]{:S(2)}, u32[]{:S(2)}) collective-permute-start(f32[72,128]{1,0:T(8,128)S(1)} %get-tuple-element.18), channel_id=1, source_target_pairs={{0,16},{16,0},{32,48},{48,32},{64,80},{80,64},{96,112},{112,96},{1... | collective-permute-start | bytes 110600 | tf_op jit(solution)/shard_map/ppermute | solution.py:445
  40.7 5.4 %collective-permute-start.2 = (f32[72,128]{1,0:T(8,128)S(1)}, f32[72,128]{1,0:T(8,128)S(1)}, u32[]{:S(2)}, u32[]{:S(2)}) collective-permute-start(f32[72,128]{1,0:T(8,128)S(1)} %get-tuple-element.19), channel_id=1, source_target_pairs={{0,48},{16,32},{32,16},{48,0},{64,112},{80,96},{96,80},{112,64},{1... | collective-permute-start | bytes 110600 | tf_op jit(solution)/shard_map/ppermute | solution.py:445
  46.1 5.6 %collective-permute-start.3 = (f32[264,128]{1,0:T(8,128)S(1)}, f32[264,128]{1,0:T(8,128)S(1)}, u32[]{:S(2)}, u32[]{:S(2)}) collective-permute-start(f32[264,128]{1,0:T(8,128)S(1)} %get-tuple-element.21), channel_id=1, source_target_pairs={{0,128},{16,144},{32,160},{48,176},{64,192},{80,208},{96,224},{112... | collective-permute-start | bytes 405512 | tf_op jit(solution)/shard_map/ppermute | solution.py:454
  46.2 5.5 %collective-permute-start.4 = (f32[264,128]{1,0:T(8,128)S(1)}, f32[264,128]{1,0:T(8,128)S(1)}, u32[]{:S(2)}, u32[]{:S(2)}) collective-permute-start(f32[264,128]{1,0:T(8,128)S(1)} %get-tuple-element.22), channel_id=1, source_target_pairs={{0,64},{16,80},{32,96},{48,112},{64,0},{80,16},{96,32},{112,48},{1... | collective-permute-start | bytes 405512 | tf_op jit(solution)/shard_map/ppermute | solution.py:454
  46.9 7.0 %collective-permute-start.5 = (f32[264,128]{1,0:T(8,128)S(1)}, f32[264,128]{1,0:T(8,128)S(1)}, u32[]{:S(2)}, u32[]{:S(2)}) collective-permute-start(f32[264,128]{1,0:T(8,128)S(1)} %get-tuple-element.23), channel_id=1, source_target_pairs={{0,192},{16,208},{32,224},{48,240},{64,128},{80,144},{96,160},{112... | collective-permute-start | bytes 405512 | tf_op jit(solution)/shard_map/ppermute | solution.py:454
  53.9 8.6 %copy-start.1 = (f32[128,32,32]{0,2,1:T(8,128)S(1)}, f32[128,32,32]{0,2,1:T(8,128)}, u32[]{:S(2)}) copy-start(f32[128,32,32]{0,2,1:T(8,128)} %param.31) | copy-start | bytes 1572868
  56.0 6.5 %copy-start.2 = (s32[2048]{0:T(1024)S(1)}, s32[2048]{0:T(1024)}, u32[]{:S(2)}) copy-start(s32[2048]{0:T(1024)} %param.28) | copy-start | bytes 24580
  56.0 6.5 %copy-start.6 = (s32[2048]{0:T(1024)S(1)}, s32[2048]{0:T(1024)}, u32[]{:S(2)}) copy-start(s32[2048]{0:T(1024)} %param.29) | copy-start | bytes 24580
  56.0 13.7 %all-to-all-start.1 = ((f32[16,32,128]{2,1,0:T(8,128)}), f32[16,32,128]{2,1,0:T(8,128)S(1)}, u32[]{:S(2)}, u32[]{:S(2)}) async-start(f32[16,32,128]{2,1,0:T(8,128)} %shard_map.172), calls=%async_computation.1 | async-start | bytes 524288 | tf_op jit(solution)/shard_map/all_to_all | solution.py:473
  62.5 0.7 copy-start.10
  63.8 5.8 %copy-start.7 = (s32[2048]{0:T(1024)S(1)}, s32[2048]{0:T(1024)}, u32[]{:S(2)}) copy-start(s32[2048]{0:T(1024)} %param.30) | copy-start | bytes 24580
